TPU v7x, 32 devices: a whole 2x2x4 slice. The times are simulated.
32 devices in a mesh: space: 8 (over z, y), tm: 4 (over x, core).
Axes of the slice: x: 2, y: 2, z: 4, core: 2. Of those that a mesh axis runs over, the one named last changes fastest.
Arguments:
- velocity: float32 [4, 3, 3, 128, 128, 128], P('tm', None, None, 'space'), may hold values from -6 to 6
Outputs:
- new_velocity: float32 [4, 3, 3, 128, 128, 128], P('tm', None, None, 'space')
- new_rhs: bfloat16 [4, 3, 3, 128, 128, 128], P('tm', None, None, 'space')
All inputs are finite; a program needn't handle non-finite values.
Results may differ from a plain program's by a relative error of at most 0.001.
Values sent between devices are 32-bit elements; how exact they have to be, the bound alone decides.
No kernel may reach another device: no remote copies, remote signals or barrier semaphores. Data moves between devices by JAX's collectives and lax.ppermute only.
A program may use at most 192 MiB of HBM per device.

v0:
```python
import math

import jax
import jax.numpy as jnp
from jax import lax
from jax.sharding import PartitionSpec as P

viscosity = 1.0
coarse_viscosity = 10.0
time_step = 0.3
weights_first = (5.0 / 24.0, 1.0 / 3.0, -1.0 / 24.0)
weights_second = (-1.0 / 24.0, 1.0 / 3.0, 5.0 / 24.0)
highest = lax.Precision.HIGHEST


def extended_2(x, sides, width):
    for axis, dim in sides:
        peers, length = (lax.axis_size(axis), x.shape[dim])
        up = [(i, (i + 1) % peers) for i in range(peers)]
        down = [(j, i) for i, j in up]
        last = lax.slice_in_dim(x, length - width, length, axis=dim)
        initial = lax.slice_in_dim(x, 0, width, axis=dim)
        before = lax.ppermute(last, axis, up)
        after = lax.ppermute(initial, axis, down)
        x = jnp.concatenate([before, x, after], axis=dim)
    return x


def shifted(value, axis, steps):
    count = lax.axis_size(axis)
    pairs = [(source, (source + steps) % count) for source in range(count)]
    return lax.ppermute(value, axis, pairs)


def shifted_2(value, axis, steps):
    count = lax.axis_size(axis)
    initial, last = (max(0, -steps), min(count, count - steps))
    return lax.ppermute(value, axis, [(source, source + steps) for source in range(initial, last)])


def integrate(stacked, weights):
    return time_step * (weights[0] * stacked[0] + weights[1] * stacked[1] + weights[2] * stacked[2])


def advection_laplace(stacked, neighbours, spacing):
    advect = jnp.zeros_like(stacked)
    laplace = -6.0 * stacked
    for direction in range(3):
        forward_cell, backward_cell = neighbours[direction]
        advect = advect - stacked[:, direction : direction + 1] * (
            (forward_cell - backward_cell) / (2.0 * spacing)
        )
        laplace = laplace + forward_cell + backward_cell
    return (advect, laplace / (spacing * spacing))


def local_neighbours(stacked, padded):
    return (
        (padded[:, :, 2:], padded[:, :, :-2]),
        (jnp.roll(stacked, -1, 3), jnp.roll(stacked, 1, 3)),
        (jnp.roll(stacked, -1, 4), jnp.roll(stacked, 1, 4)),
    )


def fine_rhs(stacked):
    padded = extended_2(stacked, (("space", 2),), 1)
    advect, laplace = advection_laplace(stacked, local_neighbours(stacked, padded), 1.0)
    return advect + viscosity * laplace


def coarse_laplace(stacked):
    padded = extended_2(stacked, (("space", 2),), 1)
    return advection_laplace(stacked, local_neighbours(stacked, padded), 2.0)[1]


def along(values, table, form):
    return jnp.einsum(form, values, table, precision=highest)


def pair_table(fine_len):
    rows = lax.iota(jnp.int32, 2 * fine_len) % fine_len // 2
    targets = lax.iota(jnp.int32, fine_len // 2)
    return 0.125 * (rows[:, None] == targets[None, :]).astype(jnp.float32)


def restrict(stacked):
    lead = stacked.shape[:-3]
    x_len, y_len, z_len = stacked.shape[-3:]
    grouped = stacked.reshape(lead + (x_len // 2, 2, y_len // 2, 2 * z_len))
    summed = grouped[..., 0, :, :] + grouped[..., 1, :, :]
    return along(summed, pair_table(z_len), "...w,wk->...k")


def refine_table(length):
    sources = lax.iota(jnp.int32, length)
    outputs = lax.iota(jnp.int32, 2 * length)
    half = outputs // 2
    odd = (outputs % 2).astype(jnp.float32)
    own = (sources[:, None] == half[None, :]).astype(jnp.float32)
    nextone = (sources[:, None] == ((half + 1) % length)[None, :]).astype(jnp.float32)
    return own * (1.0 - odd[None, :]) + 0.5 * (own + nextone) * odd[None, :]


def refine_axis(coarse, axis_pos, following):
    middle = 0.5 * (coarse + following)
    paired = jnp.stack([coarse, middle], axis=axis_pos + 1)
    dims = list(coarse.shape)
    dims[axis_pos] = 2 * dims[axis_pos]
    return paired.reshape(tuple(dims))


def refine(coarse):
    following = shifted(coarse[:, :, :1], "space", -1)
    extended = jnp.concatenate([coarse, following], axis=2)
    result = refine_axis(coarse, 2, extended[:, :, 1:])
    result = along(result, refine_table(result.shape[3]), "abxyz,yv->abxvz")
    return along(result, refine_table(result.shape[4]), "abxyz,zw->abxyw")


def cos_sin(length):
    positions = lax.iota(jnp.int32, length)
    angles = (positions[:, None] * positions[None, :] % length).astype(jnp.float32) * (
        2.0 * math.pi / length
    )
    return (jnp.cos(angles), jnp.sin(angles))


def pair_swap(values):
    width = values.shape[-1]
    group = math.gcd(width, 128)
    outputs = lax.iota(jnp.int32, group)
    inputs = lax.iota(jnp.int32, group)
    upper = ((inputs[:, None] % 2 == 1) & (outputs[None, :] == inputs[:, None] - 1)).astype(
        jnp.float32
    )
    lower = ((inputs[:, None] % 2 == 0) & (outputs[None, :] == inputs[:, None] + 1)).astype(
        jnp.float32
    )
    table = upper - lower
    grouped = values.reshape(values.shape[:-1] + (width // group, group))
    return along(grouped, table, "...g,gh->...h").reshape(values.shape)


def z_forward_table(length):
    cos_z, sin_z = cos_sin(length)
    return jnp.stack([cos_z, -sin_z], axis=2).reshape(length, 2 * length)


def z_inverse_table(length):
    cos_z, sin_z = cos_sin(length)
    return jnp.stack([cos_z, -sin_z], axis=1).reshape(2 * length, length)


def complex_along(values, length, form, sign):
    cos_t, sin_t = cos_sin(length)
    return along(values, cos_t, form) + sign * along(pair_swap(values), sin_t, form)


def forward_local(stacked):
    spectra_z = along(stacked, z_forward_table(stacked.shape[4]), "abcyz,zw->abcyw")
    return complex_along(spectra_z, stacked.shape[3], "abcyw,yv->abcvw", 1.0)


def forward_x(block):
    return complex_along(block, block.shape[1], "bxc,xk->bkc", 1.0)


def inverse_x(block):
    return complex_along(block, block.shape[1], "bxc,xk->bkc", -1.0)


def inverse_local(block):
    spectra_y = complex_along(block, block.shape[3], "abcyw,yv->abcvw", -1.0)
    return along(spectra_y, z_inverse_table(block.shape[4] // 2), "abcyw,wz->abcyz")


def per_device(velocity):
    nodes = velocity[0]
    tm_first = lax.axis_index("tm") == 0
    half_step = 0.5 * time_step
    old_rhs = fine_rhs(nodes)
    sweep_first = nodes[0] + integrate(old_rhs, weights_first)
    rhs_first = fine_rhs(sweep_first[None])[0]
    sweep_last = (
        sweep_first + half_step * (rhs_first - old_rhs[1]) + integrate(old_rhs, weights_second)
    )
    rhs_last = fine_rhs(sweep_last[None])[0]
    swept = jnp.stack([nodes[0], sweep_first, sweep_last])
    fresh_rhs = jnp.stack([old_rhs[0], rhs_first, rhs_last])
    coarse = restrict(swept)
    sources = restrict(
        jnp.stack([integrate(fresh_rhs, weights_first), integrate(fresh_rhs, weights_second)])
    ) - half_step * coarse_viscosity * coarse_laplace(coarse[1:])
    size_c, size_y, size_z = (coarse.shape[2], coarse.shape[3], coarse.shape[4])
    local_spectra = forward_local(jnp.concatenate([coarse[:1], sources]))
    flattened = local_spectra.reshape(9, size_c, size_y * 2 * size_z)
    spectra = forward_x(lax.all_to_all(flattened, "space", split_axis=2, concat_axis=1, tiled=True))
    size_x = spectra.shape[1]
    column_count = spectra.shape[2]
    spectra = spectra.reshape(3, 3, size_x, column_count)
    own_start = spectra[0]
    first_source = spectra[1]
    second_source = spectra[2]
    columns = lax.axis_index("space") * column_count + lax.iota(jnp.int32, column_count)
    wave_x = jnp.sin(lax.iota(jnp.int32, size_x).astype(jnp.float32) * (math.pi / size_x)) ** 2
    wave_y = jnp.sin((columns // (2 * size_z)).astype(jnp.float32) * (math.pi / size_y)) ** 2
    wave_z = jnp.sin((columns % (2 * size_z) // 2).astype(jnp.float32) * (math.pi / size_z)) ** 2
    total = wave_x[:, None] + wave_y[None, :] + wave_z[None, :]
    denominator = 1.0 + half_step * coarse_viscosity * (4.0 / (2.0 * 2.0)) * total

    def advance(start_value):
        middle_value = (start_value + first_source) / denominator
        return (middle_value, (middle_value + second_source) / denominator)

    start = own_start
    for round_index in range(lax.axis_size("tm") - 1):
        end_value = advance(start)[1]
        arriving = shifted_2(end_value, "tm", 1)
        start = jnp.where(tm_first, own_start, arriving)
    middle_hat, last_hat = advance(start)
    wanted = jnp.stack([middle_hat, last_hat])
    count = wanted.shape[0]
    inverted = inverse_x(wanted.reshape(count * 3, size_x, column_count))
    returned = lax.all_to_all(inverted, "space", split_axis=1, concat_axis=2, tiled=True)
    physical = inverse_local(returned.reshape(count, 3, size_c, size_y, 2 * size_z)) * (
        1.0 / (size_x * size_y * size_z)
    )
    refined = refine(physical - coarse[1:])
    corrected = swept[1:] + refined
    first_node = jnp.where(tm_first, nodes[0], shifted_2(corrected[1], "tm", 1))
    new_nodes = jnp.stack([first_node, corrected[0], corrected[1]])
    new_rhs = fine_rhs(new_nodes).astype(jnp.bfloat16)
    return (new_nodes[None], new_rhs[None])


def solution(mesh):
    placed = (P("tm", None, None, "space", None, None),)
    return jax.shard_map(
        per_device,
        mesh=mesh,
        in_specs=placed,
        out_specs=(
            P("tm", None, None, "space", None, None),
            P("tm", None, None, "space", None, None),
        ),
        check_vma=False,
    )
```

profile of v0, /device:TPU:1, one launch (start us, length us, event | category | flops | bytes accessed | tf_op | source)
XLA Modules:
  0.0 712.5 jit_solution(17565221434446075363)
XLA Ops:
  3.1 5.1 collective-permute-start
  8.3 13.1 %fusion.236 = (f32[3,3,16,127,128]{4,3,2,1,0:T(8,128)}, f32[3,3,16,127,128]{4,3,2,1,0:T(8,128)}) fusion(f32[3,3,16,128,128]{4,3,2,1,0:T(8,128)} %bitcast.219), kind=kLoop, calls=%fused_computation.360 | loop fusion | bytes 37453824 | tf_op jit(solution)/shard_map/jit(_roll_static)/slice | solution.py:60
  21.4 8.3 %fusion.238 = (f32[3,3,16,128,127]{4,3,2,1,0:T(8,128)}, f32[3,3,16,128,127]{4,3,2,1,0:T(8,128)}) fusion(f32[3,3,16,128,128]{4,3,2,1,0:T(8,128)S(1)} %bitcast.224), kind=kLoop, calls=%fused_computation.362 | loop fusion | bytes 37453824 | tf_op jit(solution)/shard_map/jit(_roll_static)/slice | solution.py:61
  29.7 8.1 %fusion.239 = (f32[3,3,16,128,1]{4,3,2,1,0:T(8,128)}, f32[3,3,16,128,1]{4,3,2,1,0:T(8,128)}) fusion(f32[3,3,16,128,128]{4,3,2,1,0:T(8,128)S(1)} %bitcast.225), kind=kLoop, calls=%fused_computation.363 | loop fusion | bytes 294912 | tf_op jit(solution)/shard_map/jit(_roll_static)/slice | solution.py:61
  46.5 8.4 %fusion.27 = (f32[3,16,128,128]{3,2,1,0:T(8,128)S(1)}, f32[3,16,128,128]{3,2,1,0:T(8,128)}, f32[3,16,128,128]{3,2,1,0:T(8,128)}) fusion(f32[3,3,16,128,128]{4,3,2,1,0:T(8,128)} %bitcast.220), kind=kLoop, calls=%fused_computation.81 | loop fusion | flops 2359296 | bytes 18874368 | tf_op jit(solution)/shard_map/mul | solution.py:50
  55.0 35.6 %add_add_fusion = f32[3,3,16,128,128]{4,3,2,1,0:T(8,128)} fusion(f32[3,3,16,128,128]{4,3,2,1,0:T(8,128)} %bitcast.221, f32[3,3,16,128,127]{4,3,2,1,0:T(8,128)} %get-tuple-element.31, f32[3,3,16,128,1]{4,3,2,1,0:T(8,128)} %get-tuple-element.33, f32[3,3,16,128,1]{4,3,2,1,0:T(8,128)} %get-tuple-element.32, f32[3,3,16,128,127]{4,3,2,1,0:T(8,128)} %get-tuple-element.30, ...), kind=kLoop, calls=%fused_computation.48 | loop fusion | flops 54263808 | bytes 67239936 | tf_op jit(solution)/shard_map/add | solution.py:68
  90.6 6.4 bitcast_add_fusion
  121.6 14.5 %multiply_add_fusion = (f32[1,3,16,128,128]{4,3,2,1,0:T(8,128)S(1)}, f32[1,3,16,128,128]{4,3,2,1,0:T(8,128)}) fusion(f32[1,3,16,128,128]{4,3,2,1,0:T(8,128)S(1)} %copy-done.2, f32[3,3,16,128,128]{4,3,2,1,0:T(8,128)} %add_add_fusion, f32[16,128,128]{2,1,0:T(8,128)} %get-tuple-element.50, f32[1,3,16,128,127]{4,3,2,1,0:T(8,128)} %get-tuple-element.57, ...), kind=kLoop, calls=%fused_computation.99 | loop fusion | flops 25952256 | bytes 34996224 | tf_op jit(solution)/shard_map/add | solution.py:185
  156.8 6.8 fusion.9
  183.6 24.1 %add_multiply_fusion = (f32[1,3,16,128,128]{4,3,2,1,0:T(8,128)}, f32[1,3,16,128,128]{4,3,2,1,0:T(8,128)}) fusion(f32[1,3,16,128,128]{4,3,2,1,0:T(8,128)S(1)} %copy-done.8, f32[3,3,16,128,128]{4,3,2,1,0:T(8,128)} %add_add_fusion, f32[1,3,16,128,128]{4,3,2,1,0:T(8,128)S(1)} %get-tuple-element.6, f32[16,128,128]{2,1,0:T(8,128)} %get-tuple-element.38, ...), kind=kLoop, calls=%fused_computation.96 | loop fusion | flops 22806528 | bytes 31850496 | tf_op jit(solution)/shard_map/mul | solution.py:42
  207.7 5.7 add_multiply_fusion.1
  231.7 7.7 %fusion.54 = f32[2,3,8,64,64]{4,3,2,1,0:T(8,128)S(1)} fusion(f32[2,3,8,64,64]{4,3,2,1,0:T(8,128)S(1)} %slice-done.3, f32[2,3,1,64,64]{4,3,2,1,0:T(8,128)} %collective-permute-done.7, f32[2,3,1,64,64]{4,3,2,1,0:T(8,128)S(1)} %collective-permute-done.6, f32[2,3,8,1,64]{4,3,2,1,0:T(1,128)S(1)} %copy-done.20, f32[2,3,8,63,64]{4,3,2,1,0:T(8,128)} %get-tuple-element.67, ...), kind=kOutput, calls=%fused_computation.127 | convolution fusion | flops 607748096 | bytes 11207680 | tf_op jit(solution)/shard_map/...w,wk->...k/dot_general | solution.py:77
  253.7 16.9 %copy.46 = f32[9,8,8192]{0,1,2:T(8,128)} copy(f32[9,8,8192]{2,1,0:T(8,128)} %reshape.672) | data formatting | bytes 4718592 | tf_op jit(solution)/shard_map/reshape | solution.py:196
  270.7 31.2 %reshape.690 = f32[8,1,73728]{2,1,0:T(1,128)} reshape(f32[8192,8,9]{2,1,0:T(8,128)} %bitcast.227) | data formatting | bytes 4718592
  301.9 5.0 all-to-all-start
  307.1 50.0 %all-to-all-done = f32[8,1,73728]{2,1,0:T(1,128)} async-done(((f32[8,1,73728]{2,1,0:T(1,128)}), f32[8,1,73728]{2,1,0:T(1,128)}, u32[]{:S(2)}, u32[]{:S(2)}) %all-to-all-start) | async-done | bytes 2359328 | tf_op jit(solution)/shard_map/all_to_all | solution.py:197
  357.6 9.3 %reduce = f32[8,73728]{1,0:T(8,128)} reduce(f32[8,1,73728]{2,1,0:T(1,128)} %all-to-all-done, f32[]{:T(128)} %broadcast.903), dimensions={1}, to_apply=%all_to_all.24.reduce_sub_computation | reduce | bytes 4718596 | tf_op jit(solution)/shard_map/all_to_all | solution.py:197
  366.9 50.2 %reshape.691 = f32[8192,8,9]{2,1,0:T(8,128)} reshape(f32[8,73728]{1,0:T(8,128)} %reduce) | data formatting | bytes 4718592
  417.2 20.6 %copy.47 = f32[9,8,8,1024]{3,1,2,0:T(8,128)} copy(f32[9,8,8,1024]{0,1,3,2:T(8,128)} %bitcast.228) | data formatting | bytes 4718592 | tf_op jit(solution)/shard_map/all_to_all | solution.py:197
  455.8 7.9 %collective-permute-start.8 = (f32[3,64,1024]{2,1,0:T(8,128)}, f32[3,64,1024]{2,1,0:T(8,128)}, u32[]{:S(2)}, u32[]{:S(2)}) collective-permute-start(f32[3,64,1024]{2,1,0:T(8,128)} %add_divide_fusion.3), channel_id=1, source_target_pairs={{0,1},{1,2},{2,3},{4,5},{5,6},{6,7},{8,9},{9,10},{10,11},{12,13},{... | collective-permute-start | bytes 2359304 | tf_op jit(solution)/shard_map/ppermute | solution.py:38
  463.7 9.2 %collective-permute-done.8 = f32[3,64,1024]{2,1,0:T(8,128)} collective-permute-done((f32[3,64,1024]{2,1,0:T(8,128)}, f32[3,64,1024]{2,1,0:T(8,128)}, u32[]{:S(2)}, u32[]{:S(2)}) %collective-permute-start.8) | collective-permute-done | bytes 786464 | tf_op jit(solution)/shard_map/ppermute | solution.py:38
  479.5 8.9 %collective-permute-done.9 = f32[3,64,1024]{2,1,0:T(8,128)S(1)} collective-permute-done((f32[3,64,1024]{2,1,0:T(8,128)S(1)}, f32[3,64,1024]{2,1,0:T(8,128)S(1)}, u32[]{:S(2)}, u32[]{:S(2)}) %collective-permute-start.9) | collective-permute-done | bytes 786464 | tf_op jit(solution)/shard_map/ppermute | solution.py:38
  493.3 8.7 %collective-permute-done.10 = f32[3,64,1024]{2,1,0:T(8,128)S(1)} collective-permute-done((f32[3,64,1024]{2,1,0:T(8,128)S(1)}, f32[3,64,1024]{2,1,0:T(8,128)S(1)}, u32[]{:S(2)}, u32[]{:S(2)}) %collective-permute-start.10) | collective-permute-done | bytes 786464 | tf_op jit(solution)/shard_map/ppermute | solution.py:38
  521.0 40.2 %all-to-all-done.1 = f32[6,64,1024]{2,0,1:T(8,128)} async-done(((f32[6,64,1024]{2,0,1:T(8,128)}), f32[6,64,1024]{2,0,1:T(8,128)}, u32[]{:S(2)}, u32[]{:S(2)}) %all-to-all-start.1) | async-done | bytes 1572896 | tf_op jit(solution)/shard_map/all_to_all | solution.py:224
  581.2 5.1 fusion.144
  586.3 10.5 %maximum_add_fusion = f32[2,3,16,128,128]{4,3,2,1,0:T(8,128)S(1)} fusion(f32[1,3,16,128,128]{4,3,2,1,0:T(8,128)S(1)} %get-tuple-element.6, f32[1,3,16,128,128]{4,3,2,1,0:T(8,128)S(1)} %copy-done.3, f32[128,2,3,16,64]{0,4,3,2,1:T(8,128)S(1)} %fusion.144, f32[128]{0:T(128)S(1)} %get-tuple-element.82, s32[128]{0:T(128)S(1)} %get-tuple-element.80, ...), kind=kOutput, calls=%fused_computation.50 | convolution fusion | flops 1211170816 | bytes 15730688 | tf_op jit(solution)/shard_map/abxyz,zw->abxyw/dot_general | solution.py:77
  602.1 34.2 %collective-permute-done.12 = f32[3,16,128,128]{3,2,1,0:T(8,128)S(1)} collective-permute-done((f32[3,16,128,128]{3,2,1,0:T(8,128)S(1)}, f32[3,16,128,128]{3,2,1,0:T(8,128)S(1)}, u32[]{:S(2)}, u32[]{:S(2)}) %collective-permute-start.12) | collective-permute-done | bytes 3145760 | tf_op jit(solution)/shard_map/ppermute | solution.py:38
  639.1 7.2 %fusion = (f32[3,3,16,127,128]{4,3,2,1,0:T(8,128)}, f32[3,3,16,127,128]{4,3,2,1,0:T(8,128)}) fusion(f32[2,3,16,128,128]{4,3,2,1,0:T(8,128)S(1)} %maximum_add_fusion, f32[1,3,16,128,128]{4,3,2,1,0:T(8,128)S(1)} %fusion.30), kind=kLoop, calls=%fused_computation.27 | loop fusion | flops 4681728 | bytes 28164096 | tf_op jit(solution)/shard_map/stack | solution.py:231
  646.3 8.0 %fusion.3 = (f32[3,3,16,128,1]{4,3,2,1,0:T(8,128)}, f32[3,3,16,128,1]{4,3,2,1,0:T(8,128)}) fusion(f32[2,3,16,128,128]{4,3,2,1,0:T(8,128)S(1)} %maximum_add_fusion, f32[1,3,16,128,128]{4,3,2,1,0:T(8,128)S(1)} %fusion.30), kind=kLoop, calls=%fused_computation.30 | loop fusion | flops 36864 | bytes 9584640 | tf_op jit(solution)/shard_map/stack | solution.py:231
  658.5 5.1 fusion.6
  668.3 8.0 %fusion.2 = (f32[3,3,16,128,127]{4,3,2,1,0:T(8,128)}, f32[3,3,16,128,127]{4,3,2,1,0:T(8,128)}) fusion(f32[2,3,16,128,128]{4,3,2,1,0:T(8,128)S(1)} %maximum_add_fusion, f32[1,3,16,128,128]{4,3,2,1,0:T(8,128)S(1)} %fusion.30), kind=kLoop, calls=%fused_computation.29 | loop fusion | flops 4681728 | bytes 28164096 | tf_op jit(solution)/shard_map/stack | solution.py:231
  680.6 31.7 %fusion.11 = bf16[1,3,3,16,128,128]{5,4,3,2,1,0:T(8,128)(2,1)} fusion(f32[2,3,16,128,128]{4,3,2,1,0:T(8,128)} %copy-done, f32[1,3,16,128,128]{4,3,2,1,0:T(8,128)S(1)} %fusion.30, f32[3,16,128,128]{3,2,1,0:T(8,128)} %get-tuple-element.12, f32[3,3,16,128,127]{4,3,2,1,0:T(8,128)} %get-tuple-element.18, f32[3,3,16,128,1]{4,3,2,1,0:T(8,128)} %get-tuple-element.20, ...), kind=kLoop, calls=%fused_computation.56 | loop fusion | flops 63700992 | bytes 62521344 | tf_op jit(solution)/shard_map/broadcast_in_dim | solution.py:233
  (169 shorter events, 199.1 us)
Async XLA Ops:
  0.6 20.7 %slice-start = ((s8[9437184]{0:T(1024)(128)(4,1)}), s8[4194304]{0:T(1024)(128)(4,1)S(1)}, s32[]{:S(2)}) async-start(s8[9437184]{0:T(1024)(128)(4,1)} %bitcast.222), calls=%async_computation.2 | async-start | bytes 8388608
  3.1 51.8 %collective-permute-start = (f32[3,3,1,128,128]{4,3,2,1,0:T(8,128)}, f32[3,3,1,128,128]{4,3,2,1,0:T(8,128)}, u32[]{:S(2)}, u32[]{:S(2)}) collective-permute-start(f32[3,3,1,128,128]{4,3,2,1,0:T(8,128)} %get-tuple-element.25), channel_id=1, source_target_pairs={{4,0},{8,4},{12,8},{16,12},{20,16},{24,20},{28,24},{0,28},{5,1},{9... | collective-permute-start | bytes 1769480 | tf_op jit(solution)/shard_map/ppermute | solution.py:24
  8.3 13.1 %slice-start.1 = ((s8[9437184]{0:T(1024)(128)(4,1)}), s8[4194304]{0:T(1024)(128)(4,1)S(1)}, s32[]{:S(2)}) async-start(s8[9437184]{0:T(1024)(128)(4,1)} %bitcast.222), calls=%async_computation.3 | async-start | bytes 8388608
  8.3 13.1 %slice-start.2 = ((s8[9437184]{0:T(1024)(128)(4,1)}), s8[1048576]{0:T(1024)(128)(4,1)S(1)}, s32[]{:S(2)}) async-start(s8[9437184]{0:T(1024)(128)(4,1)} %bitcast.222), calls=%async_computation.4 | async-start | bytes 2097152
  8.3 46.7 %collective-permute-start.1 = (f32[3,3,1,128,128]{4,3,2,1,0:T(8,128)}, f32[3,3,1,128,128]{4,3,2,1,0:T(8,128)}, u32[]{:S(2)}, u32[]{:S(2)}) collective-permute-start(f32[3,3,1,128,128]{4,3,2,1,0:T(8,128)} %get-tuple-element.24), channel_id=1, source_target_pairs={{0,4},{4,8},{8,12},{12,16},{16,20},{20,24},{24,28},{28,0},{1,5},{5... | collective-permute-start | bytes 1769480 | tf_op jit(solution)/shard_map/ppermute | solution.py:23
  97.0 16.8 %copy-start.1 = (f32[1,3,16,128,128]{4,3,2,1,0:T(8,128)}, f32[1,3,16,128,128]{4,3,2,1,0:T(8,128)S(1)}, u32[]{:S(2)}) copy-start(f32[1,3,16,128,128]{4,3,2,1,0:T(8,128)S(1)} %bitcast_add_fusion) | copy-start | bytes 9437188
  110.8 9.5 %collective-permute-start.2 = (f32[1,3,1,128,128]{4,3,2,1,0:T(8,128)}, f32[1,3,1,128,128]{4,3,2,1,0:T(8,128)S(1)}, u32[]{:S(2)}, u32[]{:S(2)}) collective-permute-start(f32[1,3,1,128,128]{4,3,2,1,0:T(8,128)} %get-tuple-element.47), channel_id=1, source_target_pairs={{4,0},{8,4},{12,8},{16,12},{20,16},{24,20},{28,24},{0,28},{5,1},{9... | collective-permute-start | bytes 589832 | tf_op jit(solution)/shard_map/ppermute | solution.py:24
  113.8 7.9 %collective-permute-start.3 = (f32[1,3,1,128,128]{4,3,2,1,0:T(8,128)}, f32[1,3,1,128,128]{4,3,2,1,0:T(8,128)}, u32[]{:S(2)}, u32[]{:S(2)}) collective-permute-start(f32[1,3,1,128,128]{4,3,2,1,0:T(8,128)} %get-tuple-element.48), channel_id=1, source_target_pairs={{0,4},{4,8},{8,12},{12,16},{16,20},{20,24},{24,28},{28,0},{1,5},{5... | collective-permute-start | bytes 589832 | tf_op jit(solution)/shard_map/ppermute | solution.py:23
  116.3 5.3 copy-start.2
  163.6 14.5 %copy-start.4 = (f32[3,3,8,64,64]{4,3,2,1,0:T(8,128)}, f32[3,3,8,64,64]{4,3,2,1,0:T(8,128)S(1)}, u32[]{:S(2)}) copy-start(f32[3,3,8,64,64]{4,3,2,1,0:T(8,128)S(1)} %fusion.9) | copy-start | bytes 3538948
  168.3 15.3 %copy-start.12 = (f32[1,3,16,127,128]{4,3,2,1,0:T(8,128)S(1)}, f32[1,3,16,127,128]{4,3,2,1,0:T(8,128)}, u32[]{:S(2)}) copy-start(f32[1,3,16,127,128]{4,3,2,1,0:T(8,128)} %get-tuple-element.39) | copy-start | bytes 9363460
  170.2 13.4 %copy-start.8 = (f32[1,3,16,128,128]{4,3,2,1,0:T(8,128)S(1)}, f32[1,3,16,128,128]{4,3,2,1,0:T(8,128)}, u32[]{:S(2)}) copy-start(f32[1,3,16,128,128]{4,3,2,1,0:T(8,128)} %get-tuple-element.7) | copy-start | bytes 9437188
  171.0 7.7 %collective-permute-start.4 = (f32[1,3,1,128,128]{4,3,2,1,0:T(8,128)}, f32[1,3,1,128,128]{4,3,2,1,0:T(8,128)S(1)}, u32[]{:S(2)}, u32[]{:S(2)}) collective-permute-start(f32[1,3,1,128,128]{4,3,2,1,0:T(8,128)} %get-tuple-element.34), channel_id=1, source_target_pairs={{4,0},{8,4},{12,8},{16,12},{20,16},{24,20},{28,24},{0,28},{5,1},{9... | collective-permute-start | bytes 589832 | tf_op jit(solution)/shard_map/ppermute | solution.py:24
  173.9 9.7 %collective-permute-start.5 = (f32[1,3,1,128,128]{4,3,2,1,0:T(8,128)}, f32[1,3,1,128,128]{4,3,2,1,0:T(8,128)}, u32[]{:S(2)}, u32[]{:S(2)}) collective-permute-start(f32[1,3,1,128,128]{4,3,2,1,0:T(8,128)} %get-tuple-element.35), channel_id=1, source_target_pairs={{0,4},{4,8},{8,12},{12,16},{16,20},{20,24},{24,28},{28,0},{1,5},{5... | collective-permute-start | bytes 589832 | tf_op jit(solution)/shard_map/ppermute | solution.py:23
  173.9 57.1 %collective-permute-start.6 = (f32[2,3,1,64,64]{4,3,2,1,0:T(8,128)}, f32[2,3,1,64,64]{4,3,2,1,0:T(8,128)S(1)}, u32[]{:S(2)}, u32[]{:S(2)}) collective-permute-start(f32[2,3,1,64,64]{4,3,2,1,0:T(8,128)} %get-tuple-element.68), channel_id=1, source_target_pairs={{4,0},{8,4},{12,8},{16,12},{20,16},{24,20},{28,24},{0,28},{5,1},{9... | collective-permute-start | bytes 294920 | tf_op jit(solution)/shard_map/ppermute | solution.py:24
  178.1 52.9 %collective-permute-start.7 = (f32[2,3,1,64,64]{4,3,2,1,0:T(8,128)}, f32[2,3,1,64,64]{4,3,2,1,0:T(8,128)}, u32[]{:S(2)}, u32[]{:S(2)}) collective-permute-start(f32[2,3,1,64,64]{4,3,2,1,0:T(8,128)} %get-tuple-element.69), channel_id=1, source_target_pairs={{0,4},{4,8},{8,12},{12,16},{16,20},{20,24},{24,28},{28,0},{1,5},{5... | collective-permute-start | bytes 294920 | tf_op jit(solution)/shard_map/ppermute | solution.py:23
  222.1 8.9 %copy-start.19 = (f32[2,3,8,1,64]{4,3,2,1,0:T(1,128)S(1)}, f32[2,3,8,1,64]{4,3,2,1,0:T(1,128)}, u32[]{:S(2)}) copy-start(f32[2,3,8,1,64]{4,3,2,1,0:T(1,128)} %get-tuple-element.64) | copy-start | bytes 36868
  222.1 8.9 %copy-start.20 = (f32[2,3,8,1,64]{4,3,2,1,0:T(1,128)S(1)}, f32[2,3,8,1,64]{4,3,2,1,0:T(1,128)}, u32[]{:S(2)}) copy-start(f32[2,3,8,1,64]{4,3,2,1,0:T(1,128)} %get-tuple-element.65) | copy-start | bytes 36868
  226.9 4.7 copy-start.15
  231.7 7.7 %slice-start.4 = ((f32[3,3,8,64,64]{4,3,2,1,0:T(8,128)}), f32[1,3,8,64,64]{4,3,2,1,0:T(8,128)S(1)}, s32[]{:S(2)}) async-start(f32[3,3,8,64,64]{4,3,2,1,0:T(8,128)} %copy-done.4), calls=%async_computation.6 | async-start | bytes 1572864 | tf_op jit(solution)/shard_map/slice | solution.py:195
  301.9 55.2 %all-to-all-start = ((f32[8,1,73728]{2,1,0:T(1,128)}), f32[8,1,73728]{2,1,0:T(1,128)}, u32[]{:S(2)}, u32[]{:S(2)}) async-start(f32[8,1,73728]{2,1,0:T(1,128)} %reshape.690), calls=%async_computation | async-start | bytes 4718592 | tf_op jit(solution)/shard_map/all_to_all | solution.py:197
  455.8 17.1 %collective-permute-start.8 = (f32[3,64,1024]{2,1,0:T(8,128)}, f32[3,64,1024]{2,1,0:T(8,128)}, u32[]{:S(2)}, u32[]{:S(2)}) collective-permute-start(f32[3,64,1024]{2,1,0:T(8,128)} %add_divide_fusion.3), channel_id=1, source_target_pairs={{0,1},{1,2},{2,3},{4,5},{5,6},{6,7},{8,9},{9,10},{10,11},{12,13},{... | collective-permute-start | bytes 2359304 | tf_op jit(solution)/shard_map/ppermute | solution.py:38
  463.7 24.7 %copy-start.7 = (f32[9,64,1024]{2,1,0:T(8,128)S(1)}, f32[9,64,1024]{2,1,0:T(8,128)}, u32[]{:S(2)}) copy-start(f32[9,64,1024]{2,1,0:T(8,128)} %copy-done.6) | copy-start | bytes 7077892
  475.1 13.3 %collective-permute-start.9 = (f32[3,64,1024]{2,1,0:T(8,128)S(1)}, f32[3,64,1024]{2,1,0:T(8,128)S(1)}, u32[]{:S(2)}, u32[]{:S(2)}) collective-permute-start(f32[3,64,1024]{2,1,0:T(8,128)S(1)} %add_divide_fusion.2), channel_id=1, source_target_pairs={{0,1},{1,2},{2,3},{4,5},{5,6},{6,7},{8,9},{9,10},{10,11},{12,13},{... | collective-permute-start | bytes 2359304 | tf_op jit(solution)/shard_map/ppermute | solution.py:38
  488.7 13.3 %collective-permute-start.10 = (f32[3,64,1024]{2,1,0:T(8,128)S(1)}, f32[3,64,1024]{2,1,0:T(8,128)S(1)}, u32[]{:S(2)}, u32[]{:S(2)}) collective-permute-start(f32[3,64,1024]{2,1,0:T(8,128)S(1)} %add_divide_fusion.1), channel_id=1, source_target_pairs={{0,1},{1,2},{2,3},{4,5},{5,6},{6,7},{8,9},{9,10},{10,11},{12,13},{... | collective-permute-start | bytes 2359304 | tf_op jit(solution)/shard_map/ppermute | solution.py:38
  516.4 44.8 %all-to-all-start.1 = ((f32[6,64,1024]{2,0,1:T(8,128)}), f32[6,64,1024]{2,0,1:T(8,128)}, u32[]{:S(2)}, u32[]{:S(2)}) async-start(f32[6,64,1024]{2,0,1:T(8,128)} %copy.48), calls=%async_computation.1 | async-start | bytes 4194304 | tf_op jit(solution)/shard_map/all_to_all | solution.py:224
  575.1 4.8 collective-permute-start.11
  581.2 5.1 copy-start.3
  596.8 71.5 %copy-start = (f32[2,3,16,128,128]{4,3,2,1,0:T(8,128)}, f32[2,3,16,128,128]{4,3,2,1,0:T(8,128)S(1)}, u32[]{:S(2)}) copy-start(f32[2,3,16,128,128]{4,3,2,1,0:T(8,128)S(1)} %maximum_add_fusion) | copy-start | bytes 18874372
  597.1 39.1 %collective-permute-start.12 = (f32[3,16,128,128]{3,2,1,0:T(8,128)S(1)}, f32[3,16,128,128]{3,2,1,0:T(8,128)S(1)}, u32[]{:S(2)}, u32[]{:S(2)}) collective-permute-start(f32[3,16,128,128]{3,2,1,0:T(8,128)S(1)} %slice_bitcast_fusion.3), channel_id=1, source_target_pairs={{0,1},{1,2},{2,3},{4,5},{5,6},{6,7},{8,9},{9,10},{10,11},{12,13},{... | collective-permute-start | bytes 9437192 | tf_op jit(solution)/shard_map/ppermute | solution.py:38
  663.7 12.7 %collective-permute-start.13 = (f32[3,3,1,128,128]{4,3,2,1,0:T(8,128)S(1)}, f32[3,3,1,128,128]{4,3,2,1,0:T(8,128)S(1)}, u32[]{:S(2)}, u32[]{:S(2)}) collective-permute-start(f32[3,3,1,128,128]{4,3,2,1,0:T(8,128)S(1)} %get-tuple-element.8), channel_id=1, source_target_pairs={{4,0},{8,4},{12,8},{16,12},{20,16},{24,20},{28,24},{0,28},{5,1},{9... | collective-permute-start | bytes 1769480 | tf_op jit(solution)/shard_map/ppermute | solution.py:24
  668.1 11.6 %collective-permute-start.14 = (f32[3,3,1,128,128]{4,3,2,1,0:T(8,128)S(1)}, f32[3,3,1,128,128]{4,3,2,1,0:T(8,128)S(1)}, u32[]{:S(2)}, u32[]{:S(2)}) collective-permute-start(f32[3,3,1,128,128]{4,3,2,1,0:T(8,128)S(1)} %get-tuple-element.9), channel_id=1, source_target_pairs={{0,4},{4,8},{8,12},{12,16},{16,20},{20,24},{24,28},{28,0},{1,5},{5... | collective-permute-start | bytes 1769480 | tf_op jit(solution)/shard_map/ppermute | solution.py:23
  (16 other events, 46.1 us)
where the time goes:
time: 723 us; the launch traced here: 712 us
  local copies, waits for them, and re-layouts  247 us (34%)
  other arithmetic  182 us (25%)
  waiting for transfers between devices  164 us (23%)
  matrix products  66.1 us (9%)
  starting transfers between devices  52.7 us (7%)
    unnamed x65, local copies, waits for them, and re-layouts  100 us
    dot_general x18, matrix products, along(): return jnp.einsum(form, values, table, precision=highest)  66.1 us
    ppermute x4, waiting for transfers between devices, shifted_2(): lax.ppermute(value, axis, [(source, source + steps) for source in range(i...  61.1 us
    all_to_all x1, waiting for transfers between devices, per_device(): lax.all_to_all(flattened, 'space', split_axis=2, concat_axis=1, tiled=True)  50 us
    all_to_all x1, waiting for transfers between devices, per_device(): lax.all_to_all(inverted, 'space', split_axis=1, concat_axis=2, tiled=True)  40.2 us
    broadcast_in_dim x2, other arithmetic, per_device(): return (new_nodes[None], new_rhs[None])  36.8 us
    add x1, other arithmetic, fine_rhs(): return advect + viscosity * laplace  35.6 us
    slice x6, local copies, waits for them, and re-layouts, local_neighbours(): jnp.roll(stacked, -1, 4)  31.8 us
  transfers between devices with their start and end apart: 17, of which 10 were waited for; matrix products, arithmetic and copies ran while one was open for 15% of the time, Pallas kernels for 0%

commit v1 on v0

v1 whole, which is shorter than its diff:
```python
import functools

import jax
import jax.numpy as jnp
import ml_dtypes
import numpy as np
from jax import lax
from jax.experimental import pallas as pl
from jax.experimental.pallas import tpu as pltpu
from jax.sharding import PartitionSpec as P

viscosity = 1.0
coarse_viscosity = 10.0
time_step = 0.3
weights_first = (5.0 / 24.0, 1.0 / 3.0, -1.0 / 24.0)
weights_second = (-1.0 / 24.0, 1.0 / 3.0, 5.0 / 24.0)
half_step = 0.5 * time_step
first = tuple(time_step * w for w in weights_first)
second = tuple(time_step * w for w in weights_second)
lanes = 128
pad = 8
rows_at_once = 32
params = pltpu.CompilerParams(vmem_limit_bytes=50 * 1024 * 1024)
f32 = jnp.float32
bf16 = jnp.bfloat16


def round_up(value, multiple):
    return -(-value // multiple) * multiple


def frequencies(length):
    index = np.arange(length)
    return np.where(index <= length // 2, index, index - length // 2)


def basis(length):
    index = np.arange(length)
    waves = frequencies(length)
    angles = 2.0 * np.pi * (waves[:, None] * index[None, :] % length) / length
    table = np.where(index[:, None] <= length // 2, np.cos(angles), np.sin(angles))
    edge = (waves == 0) | (2 * waves == length)
    return table * np.sqrt(np.where(edge, 1.0, 2.0) / length)[:, None]


def wave_squares(length):
    return np.sin(np.pi * frequencies(length) / length) ** 2


def refine_matrix(length):
    table = np.zeros((2 * length, length))
    for i in range(length):
        table[2 * i, i] += 1.0
        table[2 * i + 1, i] += 0.5
        table[2 * i + 1, (i + 1) % length] += 0.5
    return table


def pair_matrix(length):
    return np.repeat(np.eye(length), 2, axis=0)


def split(table):
    high = table.astype(np.float32).astype(ml_dtypes.bfloat16)
    low = (table - high.astype(np.float64)).astype(np.float32).astype(ml_dtypes.bfloat16)
    return high, low


def left_table(table):
    high, low = split(table)
    return np.concatenate([high, low, high], axis=1)


def right_table(table):
    high, low = split(table)
    return np.concatenate([high, low, high], axis=0)


def split_value(value):
    high = value.astype(bf16)
    return high, (value - high.astype(f32)).astype(bf16)


def left_dot(table, value):
    high, low = split_value(value)
    return jnp.dot(table, jnp.concatenate([high, high, low], axis=0), preferred_element_type=f32)


def right_dot(value, table):
    high, low = split_value(value)
    return jnp.dot(
        jnp.concatenate([high, high, low], axis=1), table, preferred_element_type=f32
    )


def wrap_rows(ref, plane, count):
    size = ref.shape[2] - 2 * pad
    for field in range(count):
        ref[field, plane, pad - 1 : pad, :] = ref[field, plane, pad + size - 1 : pad + size, :]
        ref[field, plane, pad + size : pad + size + 1, :] = ref[field, plane, pad : pad + 1, :]


def rhs_rows(ref, base, plane, start):
    stop = start + rows_at_once
    center = [ref[base + c, plane, start:stop, :] for c in range(3)]
    size = ref.shape[3]
    results = []
    for c in range(3):
        x_up = ref[base + c, plane + 1, start:stop, :]
        x_down = ref[base + c, plane - 1, start:stop, :]
        y_up = ref[base + c, plane, start + 1 : stop + 1, :]
        y_down = ref[base + c, plane, start - 1 : stop - 1, :]
        z_up = pltpu.roll(center[c], size - 1, 1)
        z_down = pltpu.roll(center[c], 1, 1)
        advect = (
            center[0] * (x_up - x_down) + center[1] * (y_up - y_down) + center[2] * (z_up - z_down)
        )
        laplace = (x_up + x_down) + (y_up + y_down) + (z_up + z_down) - 6.0 * center[c]
        results.append(viscosity * laplace - 0.5 * advect)
    return center, results


def planes_in(source, low, high, held, sems):
    length = source.shape[1]
    size = source.shape[2]
    rows = pl.ds(pad, size)

    def inner(plane):
        return pltpu.make_async_copy(
            source.at[:, plane], held.at[:, plane + 1, rows, :], sems.at[plane]
        )

    below = pltpu.make_async_copy(low, held.at[:, 0, rows, :], sems.at[length])
    above = pltpu.make_async_copy(high, held.at[:, length + 1, rows, :], sems.at[length + 1])
    return inner, below, above


def arrive(step, source, low, high, held, sems):
    length = source.shape[1]
    count = source.shape[0]
    inner, below, above = planes_in(source, low, high, held, sems)

    @pl.when(step == 0)
    def _():
        below.start()

        def launch(plane, carry):
            inner(plane).start()
            return carry

        lax.fori_loop(0, length, launch, 0)
        above.start()
        below.wait()
        inner(0).wait()
        wrap_rows(held, 1, count)

    inner(2 * step + 1).wait()
    wrap_rows(held, 2 * step + 2, count)

    @pl.when(2 * step + 2 < length)
    def _():
        inner(2 * step + 2).wait()
        wrap_rows(held, 2 * step + 3, count)

    @pl.when(2 * step + 2 >= length)
    def _():
        above.wait()


def chunks(size):
    return range(0, size, rows_at_once)


def spectral(pairs, z_table, y_table, count):
    size = pairs.shape[1]
    half = size // 2
    summed = [
        pairs[k, pl.ds(0, half, 2), :] + pairs[k, pl.ds(1, half, 2), :] for k in range(count)
    ]
    couples = []
    for k in range(0, count, 2):
        other = summed[min(k + 1, count - 1)]
        couples.append(jnp.concatenate([summed[k], other], axis=1))
    in_z = right_dot(jnp.concatenate(couples, axis=0), z_table)
    in_z = [in_z[k * half : (k + 1) * half] for k in range(len(couples))]
    in_y = left_dot(y_table, jnp.concatenate(in_z, axis=1))
    blocks = half // 2
    lane = lax.broadcasted_iota(jnp.int32, (blocks, lanes), 1)
    results = []
    for k in range(count):
        both = in_y[:, (k // 2) * lanes : (k // 2 + 1) * lanes]
        upper, lower = both[:blocks], both[blocks:]
        if k % 2 == 0:
            results.append(jnp.where(lane < lanes // 2, upper, pltpu.roll(lower, lanes // 2, 1)))
        else:
            results.append(jnp.where(lane < lanes // 2, pltpu.roll(upper, lanes // 2, 1), lower))
    return results


def sweep_one_kernel(is_first, source, low, high, s1, w, u, v, held, sems):
    step = pl.program_id(0)
    size = source.shape[2]
    arrive(step, source, low, high, held, sems)
    for row in chunks(size):
        rows = slice(row, row + rows_at_once)
        for part in range(2):
            plane = 2 * step + part + 1
            total_first, total_second, start, initial = None, None, None, None
            for node in range(3):
                center, old = rhs_rows(held, 3 * node, plane, pad + row)
                a, b = first[node], second[node] - (half_step if node == 1 else 0.0)
                if node == 0:
                    start, initial = center, old
                    total_first = [start[c] + a * old[c] for c in range(3)]
                    total_second = [b * old[c] for c in range(3)]
                else:
                    total_first = [total_first[c] + a * old[c] for c in range(3)]
                    total_second = [total_second[c] + b * old[c] for c in range(3)]
                if node == 0:
                    for c in range(3):
                        mine = first[0] * old[c] + is_first[0] * start[c]
                        other = second[0] * old[c]
                        if part == 1:
                            mine = mine + u[c, 0, rows, :]
                            other = other + v[c, 0, rows, :]
                        u[c, 0, rows, :] = mine
                        v[c, 0, rows, :] = other
            for c in range(3):
                s1[c, part, rows, :] = total_first[c]
                w[c, part, rows, :] = total_first[c] + total_second[c]
                u[c, 0, rows, :] = u[c, 0, rows, :] - total_first[c]
                v[c, 0, rows, :] = v[c, 0, rows, :] + total_first[c]


def sweep_two_kernel(
    group, source, low, high, w, u, v, z_table, y_table, s2, u_out, v_out, g, held, pairs, sems
):
    step = pl.program_id(0)
    size = source.shape[2]
    arrive(step, source, low, high, held, sems)
    for row in chunks(size):
        rows = slice(row, row + rows_at_once)
        fresh_sum, sweep_sum = None, None
        for part in range(2):
            _, fresh = rhs_rows(held, 0, 2 * step + part + 1, pad + row)
            swept = [w[c, part, rows, :] + half_step * fresh[c] for c in range(3)]
            for c in range(3):
                s2[c, part, rows, :] = swept[c]
            if part == 0:
                fresh_sum, sweep_sum = fresh, swept
            else:
                fresh_sum = [fresh_sum[c] + fresh[c] for c in range(3)]
                sweep_sum = [sweep_sum[c] + swept[c] for c in range(3)]
        for c in range(3):
            u_out[c, 0, rows, :] = u[c, 0, rows, :] + first[1] * fresh_sum[c]
            v_out[c, 0, rows, :] = v[c, 0, rows, :] + second[1] * fresh_sum[c] - sweep_sum[c]
            pairs[c, rows, :] = sweep_sum[c]
    planes = source.shape[1] // 2
    blocks = g.shape[0] // group
    for c, value in enumerate(spectral(pairs, z_table[...], y_table[...], 3)):
        g[pl.ds(c * planes + step, blocks, group), :] = value


def source_kernel(
    group, g_group, source, low, high, u, v, g, z_table, y_table, out, held, pairs, sems
):
    step = pl.program_id(0)
    size = source.shape[2]
    arrive(step, source, low, high, held, sems)
    for row in chunks(size):
        rows = slice(row, row + rows_at_once)
        _, fresh = rhs_rows(held, 0, 2 * step + 1, pad + row)
        _, other = rhs_rows(held, 0, 2 * step + 2, pad + row)
        for c in range(3):
            total = fresh[c] + other[c]
            pairs[c, rows, :] = u[c, 0, rows, :] + first[2] * total
            pairs[3 + c, rows, :] = v[c, 0, rows, :] + second[2] * total
    planes = source.shape[1] // 2
    blocks = out.shape[0] // group
    for k, value in enumerate(spectral(pairs, z_table[...], y_table[...], 6)):
        if k < 3:
            value = value + g[pl.ds(k * planes + step, blocks, g_group), :]
        out[pl.ds(k * planes + step, blocks, group), :] = value


def solve_kernel(peers, intervals, planes, group, back, values, inverse, forward, backward, out):
    start = [None] * 3
    for interval in range(intervals):
        loaded = []
        for field in range(6):
            parts = [
                values[
                    pl.ds(interval * group + field * planes + p, peers, intervals * group), :
                ]
                for p in range(planes)
            ]
            loaded.append(jnp.concatenate(parts, axis=0))
        spectra = left_dot(forward[...], jnp.concatenate(loaded, axis=1))
        rates = inverse[...]
        wanted = []
        for field in range(6):
            c = field % 3
            value = spectra[:, field * lanes : (field + 1) * lanes]
            if start[c] is not None:
                value = value + start[c]
            start[c] = value * rates
            wanted.append(start[c])
        physical = left_dot(backward[...], jnp.concatenate(wanted, axis=1))
        for field in range(6):
            base = (field // 3) * (back // 2) + (field % 3) * (planes + 2)
            for e in range(planes + 2):
                out[pl.ds(interval * back + base + e, peers, intervals * back), :] = physical[
                    e * peers : (e + 1) * peers, field * lanes : (field + 1) * lanes
                ]


def corrected_kernel(
    nodes, group, *refs
):
    count = 3 * len(nodes)
    spectra, z_table, y_table = refs[:3]
    fields = [refs[3 + 3 * k : 6 + 3 * k] for k in range(len(nodes))]
    new_velocity, new_rhs, held, coarse, result, sems, out_sems, rhs_sems = refs[-8:]
    length = fields[0][0].shape[1]
    size = fields[0][0].shape[2]
    planes = length // 2
    rows_all = pl.ds(pad, size)
    inner_copies, edge_copies = [], []
    for k, (source, low, high) in enumerate(fields):
        place = held.at[3 * k : 3 * k + 3]
        edge_copies.append(
            pltpu.make_async_copy(low, place.at[:, 0, rows_all, :], sems.at[k, length])
        )
        edge_copies.append(
            pltpu.make_async_copy(high, place.at[:, length + 1, rows_all, :], sems.at[k, length + 1])
        )
        for plane in range(length):
            inner_copies.append(
                pltpu.make_async_copy(
                    source.at[:, plane], place.at[:, plane + 1, rows_all, :], sems.at[k, plane]
                )
            )
    for copy in edge_copies + inner_copies:
        copy.start()
    blocks = spectra.shape[0] // group
    for k in range(len(nodes)):
        for c in range(3):
            base = k * (group // len(nodes)) + c * (planes + 2)
            parts = [spectra[pl.ds(base + e, blocks, group), :] for e in range(planes + 2)]
            in_z = right_dot(jnp.concatenate(parts, axis=0), z_table[...])
            for e in range(planes + 2):
                mine = in_z[e * blocks : (e + 1) * blocks]
                stacked = jnp.concatenate([mine[:, :size], mine[:, size:]], axis=0)
                coarse[3 * k + c, e] = left_dot(y_table[...], stacked)
    for copy in edge_copies + inner_copies:
        copy.wait()

    def out_copy(k, plane):
        return pltpu.make_async_copy(
            held.at[3 * k : 3 * k + 3, plane + 1, rows_all, :],
            new_velocity.at[nodes[k], :, plane],
            out_sems.at[k, plane],
        )

    def rhs_copy(k, plane):
        return pltpu.make_async_copy(
            result.at[3 * k : 3 * k + 3, plane],
            new_rhs.at[nodes[k], :, plane],
            rhs_sems.at[k, plane],
        )

    def correct(plane, cell, odd):
        for field in range(count):
            for row in chunks(size):
                rows = slice(row, row + rows_at_once)
                held_rows = slice(pad + row, pad + row + rows_at_once)
                value = coarse[field, cell, rows, :]
                if odd:
                    value = 0.5 * (value + coarse[field, cell + 1, rows, :])
                held[field, plane, held_rows, :] = held[field, plane, held_rows, :] + value
        wrap_rows(held, plane, count)

    correct(0, 0, True)
    correct(1, 1, False)
    for k in range(len(nodes)):
        out_copy(k, 0).start()

    def body(q, carry):
        correct(2 * q + 2, q + 1, True)
        correct(2 * q + 3, q + 2, False)
        for k in range(len(nodes)):
            out_copy(k, 2 * q + 1).start()

            @pl.when(2 * q + 2 < length)
            def _():
                out_copy(k, 2 * q + 2).start()

        for part in range(2):
            plane = 2 * q + part
            for k in range(len(nodes)):
                for row in chunks(size):
                    _, fresh = rhs_rows(held, 3 * k, plane + 1, pad + row)
                    for c in range(3):
                        result[3 * k + c, plane, row : row + rows_at_once, :] = fresh[c].astype(bf16)
                rhs_copy(k, plane).start()
        return carry

    lax.fori_loop(0, planes, body, 0)

    def finish(plane, carry):
        for k in range(len(nodes)):
            out_copy(k, plane).wait()
            rhs_copy(k, plane).wait()
        return carry

    lax.fori_loop(0, length, finish, 0)


anywhere = pl.BlockSpec(memory_space=pl.ANY)


def whole(shape):
    return pl.BlockSpec(shape, lambda *index: (0,) * len(shape))


def struct(shape, dtype=f32):
    return jax.ShapeDtypeStruct(shape, dtype)


def slab(shape):
    return pl.BlockSpec(shape, lambda q: (0, q, 0, 0))


def held_planes(count, length, size_y, size_z):
    return pltpu.VMEM((count, length + 2, size_y + 2 * pad, size_z), f32)


def neighbours(low_plane, high_plane):
    count = lax.axis_size("space")
    up = [(i, (i + 1) % count) for i in range(count)]
    down = [(j, i) for i, j in up]
    return lax.ppermute(high_plane, "space", up), lax.ppermute(low_plane, "space", down)


def later_interval(value):
    count = lax.axis_size("tm")
    return lax.ppermute(value, "tm", [(i, i + 1) for i in range(count - 1)])


def corrected(nodes, spectra, tables, fields, outs):
    length, size_y, size_z = fields[0][0].shape[1:]
    count = 3 * len(nodes)
    planes = length // 2
    group = spectra.shape[1]
    operands = [spectra.reshape(-1, lanes), *tables]
    for field in fields:
        operands.extend(field)
    specs = [whole(o.shape) for o in operands[:3]] + [anywhere] * (len(operands) - 3)
    shape = (3, 3, length, size_y, size_z)
    aliases = {}
    if outs is not None:
        aliases = {len(operands): 0, len(operands) + 1: 1}
        operands.extend(outs)
        specs += [anywhere] * 2
    return pl.pallas_call(
        functools.partial(corrected_kernel, nodes, group),
        out_shape=(struct(shape), struct(shape, bf16)),
        in_specs=specs,
        out_specs=(anywhere, anywhere),
        input_output_aliases=aliases,
        scratch_shapes=[
            held_planes(count, length, size_y, size_z),
            pltpu.VMEM((count, planes + 2, size_y, size_z), f32),
            pltpu.VMEM((count, length, size_y, size_z), bf16),
            pltpu.SemaphoreType.DMA((len(nodes), length + 2)),
            pltpu.SemaphoreType.DMA((len(nodes), length)),
            pltpu.SemaphoreType.DMA((len(nodes), length)),
        ],
        compiler_params=params,
        name="corrected",
    )(*operands)


def per_device(velocity):
    length, size_y, size_z = velocity.shape[3:]
    planes = length // 2
    peers, intervals = lax.axis_size("space"), lax.axis_size("tm")
    devices = peers * intervals
    coarse_x, coarse_y, coarse_z = peers * planes, size_y // 2, size_z // 2
    blocks = coarse_y * coarse_z // lanes
    per_block = devices // blocks
    columns = lanes // per_block
    device = lax.axis_index("space") * intervals + lax.axis_index("tm")
    tm_first = lax.axis_index("tm") == 0
    fields = velocity.reshape(9, length, size_y, size_z)

    x_basis, y_basis, z_basis = basis(coarse_x), basis(coarse_y), basis(coarse_z)
    z_forward = 0.25 * pair_matrix(coarse_z) @ z_basis.T
    z_table = right_table(np.kron(np.eye(2), z_forward))
    y_table = left_table(0.5 * y_basis)
    order = np.arange(coarse_x).reshape(peers, planes).T.reshape(-1)
    x_forward = left_table(x_basis[:, order])
    wanted_x = np.arange(peers)[None, :] * planes + np.arange(-1, planes + 1)[:, None]
    x_backward = left_table(x_basis.T[wanted_x.reshape(-1) % coarse_x])
    z_back = (refine_matrix(coarse_z) @ z_basis.T).T
    z_back_table = right_table(np.kron(np.eye(2), z_back))
    y_back_table = left_table(refine_matrix(coarse_y) @ y_basis.T)
    y_of = np.arange(2)[:, None] * blocks + np.arange(blocks)[None, :]
    waves = wave_squares(coarse_y)[y_of.T][:, :, None] + wave_squares(coarse_z)[None, None, :]
    waves = waves.reshape(devices, columns)
    waves = np.pad(waves, ((0, 0), (0, lanes - columns)))
    mine = lax.dynamic_slice_in_dim(jnp.asarray(waves, f32), device, 1, axis=0)
    total = jnp.asarray(wave_squares(coarse_x), f32)[:, None] + mine
    rates = 1.0 / (1.0 + half_step * coarse_viscosity * (4.0 / (2.0 * 2.0)) * total)

    low, high = neighbours(fields[:, 0], fields[:, length - 1])
    fine = (3, length, size_y, size_z)
    halved = (3, planes, size_y, size_z)
    two = (3, 2, size_y, size_z)
    one = (3, 1, size_y, size_z)
    in_sems = pltpu.SemaphoreType.DMA((length + 2,))
    swept_1, w, u, v = pl.pallas_call(
        sweep_one_kernel,
        grid=(planes,),
        out_shape=(struct(fine), struct(fine), struct(halved), struct(halved)),
        in_specs=[pl.BlockSpec(memory_space=pltpu.SMEM), anywhere, anywhere, anywhere],
        out_specs=(slab(two), slab(two), slab(one), slab(one)),
        scratch_shapes=[held_planes(9, length, size_y, size_z), in_sems],
        compiler_params=params,
        name="sweep_one",
    )(tm_first.astype(f32).reshape(1), fields, low, high)
    low_1, high_1 = neighbours(swept_1[:, 0], swept_1[:, length - 1])

    g_group = round_up(3 * planes, 8)
    swept_2, u, v, g = pl.pallas_call(
        functools.partial(sweep_two_kernel, g_group),
        grid=(planes,),
        out_shape=(struct(fine), struct(halved), struct(halved), struct((blocks * g_group, lanes))),
        in_specs=[anywhere, anywhere, anywhere, slab(two), slab(one), slab(one)]
        + [whole(z_table.shape), whole(y_table.shape)],
        out_specs=(slab(two), slab(one), slab(one), whole((blocks * g_group, lanes))),
        scratch_shapes=[
            held_planes(3, length, size_y, size_z),
            pltpu.VMEM((3, size_y, size_z), f32),
            in_sems,
        ],
        compiler_params=params,
        name="sweep_two",
    )(swept_1, low_1, high_1, w, u, v, z_table, y_table)
    low_2, high_2 = neighbours(swept_2[:, 0], swept_2[:, length - 1])
    g = later_interval(g)

    group = round_up(6 * planes, 8)
    sources = pl.pallas_call(
        functools.partial(source_kernel, group, g_group),
        grid=(planes,),
        out_shape=struct((blocks * group, lanes)),
        in_specs=[anywhere, anywhere, anywhere, slab(one), slab(one), whole(g.shape)]
        + [whole(z_table.shape), whole(y_table.shape)],
        out_specs=whole((blocks * group, lanes)),
        scratch_shapes=[
            held_planes(3, length, size_y, size_z),
            pltpu.VMEM((6, size_y, size_z), f32),
            in_sems,
        ],
        compiler_params=params,
        name="sources",
    )(swept_2, low_2, high_2, u, v, g, z_table, y_table)
    carried = later_interval(swept_2)
    carried_low = later_interval(low_2)
    carried_high = later_interval(high_2)

    both = ("space", "tm")

    def to_columns(value, rows):
        if per_block > 1:
            value = value.reshape(blocks, rows, per_block, columns).swapaxes(1, 2)
        value = value.reshape(devices, rows, columns)
        value = lax.all_to_all(value, both, split_axis=0, concat_axis=0, tiled=True)
        value = jnp.pad(value, ((0, 0), (0, 0), (0, lanes - columns)))
        return value.reshape(devices * rows, lanes)

    def to_planes(value, rows):
        value = value.reshape(devices, rows, lanes)[:, :, :columns]
        value = lax.all_to_all(value, both, split_axis=0, concat_axis=0, tiled=True)
        if per_block > 1:
            value = value.reshape(blocks, per_block, rows, columns).swapaxes(1, 2)
        return value.reshape(blocks, rows, lanes)

    back = 2 * round_up(3 * (planes + 2), 8)
    solved = pl.pallas_call(
        functools.partial(solve_kernel, peers, intervals, planes, group, back),
        out_shape=struct((devices * back, lanes)),
        compiler_params=params,
        name="solve",
    )(to_columns(sources, group), rates, x_forward, x_backward)
    spectra = to_planes(solved, back)
    carried_spectra = later_interval(spectra[:, back // 2 :])

    outs = corrected(
        (1, 2),
        spectra,
        (z_back_table, y_back_table),
        ((swept_1, low_1, high_1), (swept_2, low_2, high_2)),
        None,
    )
    new_velocity, new_rhs = corrected(
        (0,),
        carried_spectra,
        (z_back_table, y_back_table),
        (
            (
                jnp.where(tm_first, fields[:3], carried),
                jnp.where(tm_first, low[:3], carried_low),
                jnp.where(tm_first, high[:3], carried_high),
            ),
        ),
        outs,
    )
    return (new_velocity[None], new_rhs[None])


def solution(mesh):
    placed = P("tm", None, None, "space", None, None)
    return jax.shard_map(
        per_device,
        mesh=mesh,
        in_specs=(placed,),
        out_specs=(placed, placed),
        check_vma=False,
    )
```

time: 723 us -> 185 us (0.26); the launches traced: 712 us -> 184 us
  local copies, waits for them, and re-layouts: 247 us -> 8.5 us
  other arithmetic: 182 us -> 5.44 us
  waiting for transfers between devices: 164 us -> 80.8 us
  matrix products: 66.1 us -> 0 us
  Pallas kernels: 0 us -> 53.3 us
  starting transfers between devices: 52.7 us -> 35.4 us
    unnamed x65 -> x17, local copies, waits for them, and re-layouts: 100 us -> 5.58 us
    all_to_all x2, waiting for transfers between devices: 90.2 us -> 15.8 us  [the longest x1 15.8 us: to_columns(): value = lax.all_to_all(value, both, split_axis=0, concat_axis=0, tiled=True)]
    dot_general x18 -> x0, matrix products: 66.1 us -> none  [along(): return jnp.einsum(form, values, table, precision=highest)]
    slice x26 -> x1, local copies, waits for them, and re-layouts: 64.8 us -> 0.04 us  [per_device(): carried_spectra = later_interval(spectra[:, back // 2:])]
    add x5 -> x0, other arithmetic: 57.2 us -> none  [the longest x1 35.6 us: fine_rhs(): return advect + viscosity * laplace]
    pallas_call x0 -> x6, Pallas kernels: none -> 53.3 us  [the longest x2 19 us: corrected(): pl.pallas_call(functools.partial(corrected_kernel, nodes, group), out_sha...]
    mul x7 -> x0, other arithmetic: 46 us -> none  [the longest x2 29.7 us: integrate(): time_step * (weights[0] * stacked[0] + weights[1] * stacked[1] + weights[...]
    broadcast_in_dim x2 -> x0, other arithmetic: 36.8 us -> none  [per_device(): return (new_nodes[None], new_rhs[None])]
  transfers between devices with their start and end apart: 17 -> 13, of which waited for: 10 -> 8; matrix products, arithmetic and copies ran while one was open for 15% -> 4% of each run, Pallas kernels for 0% -> 8%
where the time goes in v1:
time: 185 us; the launch traced here: 184 us
  waiting for transfers between devices  80.8 us (44%)
  Pallas kernels  53.3 us (29%)
  starting transfers between devices  35.4 us (19%)
  local copies, waits for them, and re-layouts  8.5 us (5%)
  other arithmetic  5.44 us (3%)
    ppermute x3, waiting for transfers between devices, neighbours(): lax.ppermute(low_plane, 'space', down)  30.3 us
    ppermute x5, waiting for transfers between devices, later_interval(): return lax.ppermute(value, 'tm', [(i, i + 1) for i in range(count - 1)])  24.4 us
    pallas_call x2, Pallas kernels, corrected(): pl.pallas_call(functools.partial(corrected_kernel, nodes, group), out_sha...  19 us
    ppermute x5, starting transfers between devices, later_interval(): return lax.ppermute(value, 'tm', [(i, i + 1) for i in range(count - 1)])  18.5 us
    all_to_all x1, waiting for transfers between devices, to_columns(): value = lax.all_to_all(value, both, split_axis=0, concat_axis=0, tiled=True)  15.8 us
    pallas_call x1, Pallas kernels, per_device(): pl.pallas_call(functools.partial(sweep_two_kernel, g_group), grid=(planes...  11.3 us
    pallas_call x1, Pallas kernels, per_device(): pl.pallas_call(sweep_one_kernel, grid=(planes,), out_shape=(struct(fine),...  10.6 us
    ppermute x3, waiting for transfers between devices, neighbours(): lax.ppermute(high_plane, 'space', up)  10.3 us
  transfers between devices with their start and end apart: 13, of which 8 were waited for; matrix products, arithmetic and copies ran while one was open for 4% of the time, Pallas kernels for 8%

profile of v1, /device:TPU:1, one launch (start us, length us, event | category | flops | bytes accessed | tf_op | source)
XLA Modules:
  0.0 184.5 jit_solution(12792907004860092121)
XLA Ops:
  0.6 4.4 %copy.13 = f32[1,3,3,16,128,128]{5,4,2,1,3,0:T(8,128)S(1)} copy(f32[1,3,3,16,128,128]{5,4,3,2,1,0:T(8,128)} %param.9) | data formatting | bytes 18874368 | tf_op args[0]
  5.0 0.1 slice_bitcast_fusion
  5.1 5.2 %collective-permute-start.1 = (f32[9,128,128]{2,1,0:T(8,128)S(1)}, f32[9,128,128]{2,1,0:T(8,128)S(1)}, u32[]{:S(2)}, u32[]{:S(2)}) collective-permute-start(f32[9,128,128]{2,1,0:T(8,128)S(1)} %get-tuple-element.26), channel_id=1, source_target_pairs={{4,0},{8,4},{12,8},{16,12},{20,16},{24,20},{28,24},{0,28},{5,1},{9... | collective-permute-start | bytes 1769480 | tf_op jit(solution)/shard_map/ppermute | solution.py:442
  10.3 22.7 %collective-permute-done.1.high = f32[9,128,128]{2,1,0:T(8,128)S(1)} collective-permute-done((f32[9,128,128]{2,1,0:T(8,128)S(1)}, f32[9,128,128]{2,1,0:T(8,128)S(1)}, u32[]{:S(2)}, u32[]{:S(2)}) %collective-permute-start.1) | collective-permute-done | bytes 589856 | tf_op jit(solution)/shard_map/ppermute | solution.py:442
  32.9 0.9 collective-permute-done.low
  33.8 10.6 %sweep_one.1 = (f32[3,16,128,128]{3,2,1,0:T(8,128)}, f32[3,16,128,128]{3,2,1,0:T(8,128)}, f32[3,8,128,128]{3,2,1,0:T(8,128)S(1)}, f32[3,8,128,128]{3,2,1,0:T(8,128)}) custom-call(f32[1]{0:T(128)} %bitcast.is_first, f32[9,16,128,128]{3,2,1,0:T(8,128)} %bitcast.29, f32[9,128,128]{2,1,0:T(8,128)S(1)} %collective-permute-done.low, ...), custom_call_target="tpu_custom_call" | custom-call | tf_op jit(solution)/shard_map/sweep_one/pallas_call | solution.py:522
  44.4 1.1 copy-done
  45.6 1.0 slice_bitcast_fusion.4
  46.6 3.2 %collective-permute-start.3 = (f32[3,128,128]{2,1,0:T(8,128)S(1)}, f32[3,128,128]{2,1,0:T(8,128)S(1)}, u32[]{:S(2)}, u32[]{:S(2)}) collective-permute-start(f32[3,128,128]{2,1,0:T(8,128)S(1)} %get-tuple-element.30), channel_id=1, source_target_pairs={{4,0},{8,4},{12,8},{16,12},{20,16},{24,20},{28,24},{0,28},{5,1},{9... | collective-permute-start | bytes 589832 | tf_op jit(solution)/shard_map/ppermute | solution.py:442
  49.9 3.8 %collective-permute-done.3.high.refs_5_ = f32[3,128,128]{2,1,0:T(8,128)S(1)} collective-permute-done((f32[3,128,128]{2,1,0:T(8,128)S(1)}, f32[3,128,128]{2,1,0:T(8,128)S(1)}, u32[]{:S(2)}, u32[]{:S(2)}) %collective-permute-start.3) | collective-permute-done | bytes 196640 | tf_op jit(solution)/shard_map/ppermute | solution.py:442
  53.7 4.9 %collective-permute-done.2.low.refs_4_ = f32[3,128,128]{2,1,0:T(8,128)S(1)} collective-permute-done((f32[3,128,128]{2,1,0:T(8,128)S(1)}, f32[3,128,128]{2,1,0:T(8,128)S(1)}, u32[]{:S(2)}, u32[]{:S(2)}) %collective-permute-start.2) | collective-permute-done | bytes 196640 | tf_op jit(solution)/shard_map/ppermute | solution.py:442
  58.6 11.3 %sweep_two.1 = (f32[3,16,128,128]{3,2,1,0:T(8,128)}, f32[3,8,128,128]{3,2,1,0:T(8,128)S(1)}, f32[3,8,128,128]{3,2,1,0:T(8,128)}, f32[768,128]{1,0:T(8,128)S(1)}) custom-call(f32[3,16,128,128]{3,2,1,0:T(8,128)} %get-tuple-element.14.source.refs_3_, f32[3,128,128]{2,1,0:T(8,128)S(1)} %collective-permute-done.2.low.refs_4_, ...), custom_call_target="tpu_custom_call" | custom-call | tf_op jit(solution)/shard_map/sweep_two/pallas_call | solution.py:535
  69.9 4.8 %collective-permute-start.6 = (f32[768,128]{1,0:T(8,128)S(1)}, f32[768,128]{1,0:T(8,128)S(1)}, u32[]{:S(2)}, u32[]{:S(2)}) collective-permute-start(f32[768,128]{1,0:T(8,128)S(1)} %get-tuple-element.21), channel_id=1, source_target_pairs={{0,1},{1,2},{2,3},{4,5},{5,6},{6,7},{8,9},{9,10},{10,11},{12,13},{... | collective-permute-start | bytes 1179656 | tf_op jit(solution)/shard_map/ppermute | solution.py:447
  74.7 1.1 slice_bitcast_fusion.2
  75.8 1.6 collective-permute-start.5
  77.4 3.8 %collective-permute-done.5.high.refs_8_ = f32[3,128,128]{2,1,0:T(8,128)S(1)} collective-permute-done((f32[3,128,128]{2,1,0:T(8,128)S(1)}, f32[3,128,128]{2,1,0:T(8,128)S(1)}, u32[]{:S(2)}, u32[]{:S(2)}) %collective-permute-start.5) | collective-permute-done | bytes 196640 | tf_op jit(solution)/shard_map/ppermute | solution.py:442
  81.2 4.5 %collective-permute-done.4.low.refs_7_ = f32[3,128,128]{2,1,0:T(8,128)S(1)} collective-permute-done((f32[3,128,128]{2,1,0:T(8,128)S(1)}, f32[3,128,128]{2,1,0:T(8,128)S(1)}, u32[]{:S(2)}, u32[]{:S(2)}) %collective-permute-start.4) | collective-permute-done | bytes 196640 | tf_op jit(solution)/shard_map/ppermute | solution.py:442
  85.7 10.0 %sources.1 = f32[1536,128]{1,0:T(8,128)} custom-call(f32[3,16,128,128]{3,2,1,0:T(8,128)} %get-tuple-element.18.source.refs_6_, f32[3,128,128]{2,1,0:T(8,128)S(1)} %collective-permute-done.4.low.refs_7_, f32[3,128,128]{2,1,0:T(8,128)S(1)} %collective-permute-done.5.high.refs_8_, f32[3,8,128,128]{3,2,1,0:T(8,128)S(1)} %get-tuple-element.19.u, ...), custom_call_target="tpu_custom_call" | custom-call | tf_op jit(solution)/shard_map/sources/pallas_call | solution.py:554
  95.7 2.8 %all-to-all-start = ((f32[32,48,128]{2,1,0:T(8,128)}), f32[32,48,128]{2,1,0:T(8,128)S(1)}, u32[]{:S(2)}, u32[]{:S(2)}) async-start(f32[32,48,128]{2,1,0:T(8,128)} %bitcast.9), calls=%async_computation | async-start | bytes 1572864 | tf_op jit(solution)/shard_map/all_to_all | solution.py:579
  98.5 3.5 %collective-permute-start.8 = (f32[3,16,128,128]{3,2,1,0:T(8,128)}, f32[3,16,128,128]{3,2,1,0:T(8,128)}, u32[]{:S(2)}, u32[]{:S(2)}) collective-permute-start(f32[3,16,128,128]{3,2,1,0:T(8,128)} %get-tuple-element.18.source.refs_6_), channel_id=1, source_target_pairs={{0,1},{1,2},{2,3},{4,5},{5,6},{6,7},{8,9},{9,10},{10,11},{12,13},{... | collective-permute-start | bytes 9437192 | tf_op jit(solution)/shard_map/ppermute | solution.py:447
  102.1 0.7 dynamic-slice_bitcast_fusion
  102.8 0.1 add_divide_fusion.inverse
  102.9 15.8 %all-to-all-done = f32[32,48,128]{2,1,0:T(8,128)S(1)} async-done(((f32[32,48,128]{2,1,0:T(8,128)}), f32[32,48,128]{2,1,0:T(8,128)S(1)}, u32[]{:S(2)}, u32[]{:S(2)}) %all-to-all-start) | async-done | bytes 786464 | tf_op jit(solution)/shard_map/all_to_all | solution.py:579
  118.7 2.4 %solve.1 = f32[2048,128]{1,0:T(8,128)} custom-call(f32[1536,128]{1,0:T(8,128)S(1)} %bitcast.27, f32[64,128]{1,0:T(8,128)S(1)} %add_divide_fusion.inverse, bf16[64,192]{1,0:T(8,128)(2,1)S(1)} %copy-done.6, bf16[80,192]{1,0:T(8,128)(2,1)S(1)} %copy-done.5), custom_call_target="tpu_custom_call" | custom-call | tf_op jit(solution)/shard_map/solve/pallas_call | solution.py:591
  121.1 4.1 %all-to-all-start.1 = ((f32[32,64,128]{2,1,0:T(8,128)}), f32[32,64,128]{2,1,0:T(8,128)S(1)}, u32[]{:S(2)}, u32[]{:S(2)}) async-start(f32[32,64,128]{2,1,0:T(8,128)} %bitcast.12), calls=%async_computation.1 | async-start | bytes 2097152 | tf_op jit(solution)/shard_map/all_to_all | solution.py:585
  125.2 3.5 %collective-permute-start.10 = (f32[3,128,128]{2,1,0:T(8,128)S(1)}, f32[3,128,128]{2,1,0:T(8,128)S(1)}, u32[]{:S(2)}, u32[]{:S(2)}) collective-permute-start(f32[3,128,128]{2,1,0:T(8,128)S(1)} %collective-permute-done.5.high.refs_8_), channel_id=1, source_target_pairs={{0,1},{1,2},{2,3},{4,5},{5,6},{6,7},{8,9},{9,10},{10,11},{12,13},{... | collective-permute-start | bytes 589832 | tf_op jit(solution)/shard_map/ppermute | solution.py:447
  128.8 2.1 %collective-permute-start.9 = (f32[3,128,128]{2,1,0:T(8,128)S(1)}, f32[3,128,128]{2,1,0:T(8,128)S(1)}, u32[]{:S(2)}, u32[]{:S(2)}) collective-permute-start(f32[3,128,128]{2,1,0:T(8,128)S(1)} %collective-permute-done.4.low.refs_7_), channel_id=1, source_target_pairs={{0,1},{1,2},{2,3},{4,5},{5,6},{6,7},{8,9},{9,10},{10,11},{12,13},{... | collective-permute-start | bytes 589832 | tf_op jit(solution)/shard_map/ppermute | solution.py:447
  130.8 24.4 %collective-permute-done.10 = f32[3,128,128]{2,1,0:T(8,128)S(1)} collective-permute-done((f32[3,128,128]{2,1,0:T(8,128)S(1)}, f32[3,128,128]{2,1,0:T(8,128)S(1)}, u32[]{:S(2)}, u32[]{:S(2)}) %collective-permute-start.10) | collective-permute-done | bytes 196640 | tf_op jit(solution)/shard_map/ppermute | solution.py:447
  155.3 4.6 %collective-permute-start.7 = (f32[32,32,128]{2,1,0:T(8,128)S(1)}, f32[32,32,128]{2,1,0:T(8,128)S(1)}, u32[]{:S(2)}, u32[]{:S(2)}) collective-permute-start(f32[32,32,128]{2,1,0:T(8,128)S(1)} %slice.50), channel_id=1, source_target_pairs={{0,1},{1,2},{2,3},{4,5},{5,6},{6,7},{8,9},{9,10},{10,11},{12,13},{... | collective-permute-start | bytes 1572872 | tf_op jit(solution)/shard_map/ppermute | solution.py:447
  159.9 5.3 %bitcast_select_fusion.refs_3_ = f32[3,16,128,128]{3,2,1,0:T(8,128)} fusion(f32[3,16,128,128]{3,2,1,0:T(8,128)} %collective-permute-done.8, f32[1,3,3,16,128,128]{5,4,3,2,1,0:T(8,128)} %param.9, pred[]{:T(512)S(6)} %eq.3), kind=kLoop, calls=%fused_computation | loop fusion | flops 786432 | bytes 9437185 | tf_op jit(solution)/shard_map/jit(_where)/select_n | solution.py:613
  165.2 12.0 %corrected.2 = (f32[3,3,16,128,128]{4,3,2,1,0:T(8,128)}, bf16[3,3,16,128,128]{4,3,2,1,0:T(8,128)(2,1)}) custom-call(f32[2048,128]{1,0:T(8,128)S(1)} %bitcast.26, bf16[384,256]{1,0:T(8,128)(2,1)S(1)} %copy-done.1, bf16[128,192]{1,0:T(8,128)(2,1)S(1)} %copy-done.3, f32[3,16,128,128]{3,2,1,0:T(8,128)} %get-tuple-element.14.source.refs_3_, ...), custom_call_target="tpu_custom_call" | custom-call | tf_op jit(solution)/shard_map/corrected/pallas_call | solution.py:465
  177.3 7.0 %corrected.3 = (f32[3,3,16,128,128]{4,3,2,1,0:T(8,128)}, bf16[3,3,16,128,128]{4,3,2,1,0:T(8,128)(2,1)}) custom-call(f32[1024,128]{1,0:T(8,128)S(1)} %bitcast.28, bf16[384,256]{1,0:T(8,128)(2,1)S(1)} %copy-done.1, bf16[128,192]{1,0:T(8,128)(2,1)S(1)} %copy-done.3, ...), custom_call_target="tpu_custom_call", output_to_operand_aliasing={{0}: (6, {}), {1}: (7, {})} | custom-call | tf_op jit(solution)/shard_map/corrected/pallas_call | solution.py:465
  (26 shorter events, 0.1 us)
Async XLA Ops:
  5.1 27.8 %collective-permute-start.1 = (f32[9,128,128]{2,1,0:T(8,128)S(1)}, f32[9,128,128]{2,1,0:T(8,128)S(1)}, u32[]{:S(2)}, u32[]{:S(2)}) collective-permute-start(f32[9,128,128]{2,1,0:T(8,128)S(1)} %get-tuple-element.26), channel_id=1, source_target_pairs={{4,0},{8,4},{12,8},{16,12},{20,16},{24,20},{28,24},{0,28},{5,1},{9... | collective-permute-start | bytes 1769480 | tf_op jit(solution)/shard_map/ppermute | solution.py:442
  10.3 23.5 %collective-permute-start = (f32[9,128,128]{2,1,0:T(8,128)S(1)}, f32[9,128,128]{2,1,0:T(8,128)S(1)}, u32[]{:S(2)}, u32[]{:S(2)}) collective-permute-start(f32[9,128,128]{2,1,0:T(8,128)S(1)} %get-tuple-element.27), channel_id=1, source_target_pairs={{0,4},{4,8},{8,12},{12,16},{16,20},{20,24},{24,28},{28,0},{1,5},{5... | collective-permute-start | bytes 1769480 | tf_op jit(solution)/shard_map/ppermute | solution.py:442
  33.8 24.8 %copy-start.2 = (bf16[768,128]{1,0:T(8,128)(2,1)S(1)}, bf16[768,128]{1,0:T(8,128)(2,1)}, u32[]{:S(2)}) copy-start(bf16[768,128]{1,0:T(8,128)(2,1)} %constant.37.clone.z_table) | copy-start | bytes 589828
  33.8 24.8 %copy-start.4 = (bf16[64,192]{1,0:T(8,128)(2,1)S(1)}, bf16[64,192]{1,0:T(8,128)(2,1)}, u32[]{:S(2)}) copy-start(bf16[64,192]{1,0:T(8,128)(2,1)} %constant.38.clone.y_table) | copy-start | bytes 73732
  44.4 1.2 copy-start
  46.6 7.1 %collective-permute-start.3 = (f32[3,128,128]{2,1,0:T(8,128)S(1)}, f32[3,128,128]{2,1,0:T(8,128)S(1)}, u32[]{:S(2)}, u32[]{:S(2)}) collective-permute-start(f32[3,128,128]{2,1,0:T(8,128)S(1)} %get-tuple-element.30), channel_id=1, source_target_pairs={{4,0},{8,4},{12,8},{16,12},{20,16},{24,20},{28,24},{0,28},{5,1},{9... | collective-permute-start | bytes 589832 | tf_op jit(solution)/shard_map/ppermute | solution.py:442
  49.9 8.7 %collective-permute-start.2 = (f32[3,128,128]{2,1,0:T(8,128)S(1)}, f32[3,128,128]{2,1,0:T(8,128)S(1)}, u32[]{:S(2)}, u32[]{:S(2)}) collective-permute-start(f32[3,128,128]{2,1,0:T(8,128)S(1)} %get-tuple-element.31), channel_id=1, source_target_pairs={{0,4},{4,8},{8,12},{12,16},{16,20},{20,24},{24,28},{28,0},{1,5},{5... | collective-permute-start | bytes 589832 | tf_op jit(solution)/shard_map/ppermute | solution.py:442
  69.9 15.8 %collective-permute-start.6 = (f32[768,128]{1,0:T(8,128)S(1)}, f32[768,128]{1,0:T(8,128)S(1)}, u32[]{:S(2)}, u32[]{:S(2)}) collective-permute-start(f32[768,128]{1,0:T(8,128)S(1)} %get-tuple-element.21), channel_id=1, source_target_pairs={{0,1},{1,2},{2,3},{4,5},{5,6},{6,7},{8,9},{9,10},{10,11},{12,13},{... | collective-permute-start | bytes 1179656 | tf_op jit(solution)/shard_map/ppermute | solution.py:447
  75.8 5.4 %collective-permute-start.5 = (f32[3,128,128]{2,1,0:T(8,128)S(1)}, f32[3,128,128]{2,1,0:T(8,128)S(1)}, u32[]{:S(2)}, u32[]{:S(2)}) collective-permute-start(f32[3,128,128]{2,1,0:T(8,128)S(1)} %get-tuple-element.28), channel_id=1, source_target_pairs={{4,0},{8,4},{12,8},{16,12},{20,16},{24,20},{28,24},{0,28},{5,1},{9... | collective-permute-start | bytes 589832 | tf_op jit(solution)/shard_map/ppermute | solution.py:442
  77.4 8.4 %collective-permute-start.4 = (f32[3,128,128]{2,1,0:T(8,128)S(1)}, f32[3,128,128]{2,1,0:T(8,128)S(1)}, u32[]{:S(2)}, u32[]{:S(2)}) collective-permute-start(f32[3,128,128]{2,1,0:T(8,128)S(1)} %get-tuple-element.29), channel_id=1, source_target_pairs={{0,4},{4,8},{8,12},{12,16},{16,20},{20,24},{24,28},{28,0},{1,5},{5... | collective-permute-start | bytes 589832 | tf_op jit(solution)/shard_map/ppermute | solution.py:442
  85.7 17.0 %copy-start.7 = (f32[64]{0:T(128)S(1)}, f32[64]{0:T(128)}, u32[]{:S(2)}) copy-start(f32[64]{0:T(128)} %constant.36.clone) | copy-start | bytes 772
  85.7 32.9 %copy-start.5 = (bf16[80,192]{1,0:T(8,128)(2,1)S(1)}, bf16[80,192]{1,0:T(8,128)(2,1)}, u32[]{:S(2)}) copy-start(bf16[80,192]{1,0:T(8,128)(2,1)} %constant.40.clone.backward) | copy-start | bytes 92164
  85.7 32.9 %copy-start.6 = (bf16[64,192]{1,0:T(8,128)(2,1)S(1)}, bf16[64,192]{1,0:T(8,128)(2,1)}, u32[]{:S(2)}) copy-start(bf16[64,192]{1,0:T(8,128)(2,1)} %constant.39.clone.forward) | copy-start | bytes 73732
  95.7 22.9 %all-to-all-start = ((f32[32,48,128]{2,1,0:T(8,128)}), f32[32,48,128]{2,1,0:T(8,128)S(1)}, u32[]{:S(2)}, u32[]{:S(2)}) async-start(f32[32,48,128]{2,1,0:T(8,128)} %bitcast.9), calls=%async_computation | async-start | bytes 1572864 | tf_op jit(solution)/shard_map/all_to_all | solution.py:579
  98.5 61.4 %collective-permute-start.8 = (f32[3,16,128,128]{3,2,1,0:T(8,128)}, f32[3,16,128,128]{3,2,1,0:T(8,128)}, u32[]{:S(2)}, u32[]{:S(2)}) collective-permute-start(f32[3,16,128,128]{3,2,1,0:T(8,128)} %get-tuple-element.18.source.refs_6_), channel_id=1, source_target_pairs={{0,1},{1,2},{2,3},{4,5},{5,6},{6,7},{8,9},{9,10},{10,11},{12,13},{... | collective-permute-start | bytes 9437192 | tf_op jit(solution)/shard_map/ppermute | solution.py:447
  121.1 34.1 %all-to-all-start.1 = ((f32[32,64,128]{2,1,0:T(8,128)}), f32[32,64,128]{2,1,0:T(8,128)S(1)}, u32[]{:S(2)}, u32[]{:S(2)}) async-start(f32[32,64,128]{2,1,0:T(8,128)} %bitcast.12), calls=%async_computation.1 | async-start | bytes 2097152 | tf_op jit(solution)/shard_map/all_to_all | solution.py:585
  125.2 30.0 %collective-permute-start.10 = (f32[3,128,128]{2,1,0:T(8,128)S(1)}, f32[3,128,128]{2,1,0:T(8,128)S(1)}, u32[]{:S(2)}, u32[]{:S(2)}) collective-permute-start(f32[3,128,128]{2,1,0:T(8,128)S(1)} %collective-permute-done.5.high.refs_8_), channel_id=1, source_target_pairs={{0,1},{1,2},{2,3},{4,5},{5,6},{6,7},{8,9},{9,10},{10,11},{12,13},{... | collective-permute-start | bytes 589832 | tf_op jit(solution)/shard_map/ppermute | solution.py:447
  128.8 31.1 %collective-permute-start.9 = (f32[3,128,128]{2,1,0:T(8,128)S(1)}, f32[3,128,128]{2,1,0:T(8,128)S(1)}, u32[]{:S(2)}, u32[]{:S(2)}) collective-permute-start(f32[3,128,128]{2,1,0:T(8,128)S(1)} %collective-permute-done.4.low.refs_7_), channel_id=1, source_target_pairs={{0,1},{1,2},{2,3},{4,5},{5,6},{6,7},{8,9},{9,10},{10,11},{12,13},{... | collective-permute-start | bytes 589832 | tf_op jit(solution)/shard_map/ppermute | solution.py:447
  155.3 22.0 %collective-permute-start.7 = (f32[32,32,128]{2,1,0:T(8,128)S(1)}, f32[32,32,128]{2,1,0:T(8,128)S(1)}, u32[]{:S(2)}, u32[]{:S(2)}) collective-permute-start(f32[32,32,128]{2,1,0:T(8,128)S(1)} %slice.50), channel_id=1, source_target_pairs={{0,1},{1,2},{2,3},{4,5},{5,6},{6,7},{8,9},{9,10},{10,11},{12,13},{... | collective-permute-start | bytes 1572872 | tf_op jit(solution)/shard_map/ppermute | solution.py:447
  159.9 5.3 %copy-start.1 = (bf16[384,256]{1,0:T(8,128)(2,1)S(1)}, bf16[384,256]{1,0:T(8,128)(2,1)}, u32[]{:S(2)}) copy-start(bf16[384,256]{1,0:T(8,128)(2,1)} %constant.41.clone.refs_1_) | copy-start | bytes 589828
  159.9 5.3 %copy-start.3 = (bf16[128,192]{1,0:T(8,128)(2,1)S(1)}, bf16[128,192]{1,0:T(8,128)(2,1)}, u32[]{:S(2)}) copy-start(bf16[128,192]{1,0:T(8,128)(2,1)} %constant.42.clone.refs_2_) | copy-start | bytes 147460

commit v2 on v1

--- a/solution.py
+++ b/solution.py
@@ -171,19 +171,14 @@
     return range(0, size, rows_at_once)
 
 
-def spectral(pairs, z_table, y_table, count):
-    size = pairs.shape[1]
-    half = size // 2
-    summed = [
-        pairs[k, pl.ds(0, half, 2), :] + pairs[k, pl.ds(1, half, 2), :] for k in range(count)
-    ]
+def transform(summed, z_table, y_table):
+    count, half = len(summed), summed[0].shape[0]
     couples = []
     for k in range(0, count, 2):
-        other = summed[min(k + 1, count - 1)]
-        couples.append(jnp.concatenate([summed[k], other], axis=1))
-    in_z = right_dot(jnp.concatenate(couples, axis=0), z_table)
+        couples.append(jnp.concatenate([summed[k], summed[min(k + 1, count - 1)]], axis=1))
+    in_z = right_dot(jnp.concatenate(couples, axis=0), z_table[...])
     in_z = [in_z[k * half : (k + 1) * half] for k in range(len(couples))]
-    in_y = left_dot(y_table, jnp.concatenate(in_z, axis=1))
+    in_y = left_dot(y_table[...], jnp.concatenate(in_z, axis=1))
     blocks = half // 2
     lane = lax.broadcasted_iota(jnp.int32, (blocks, lanes), 1)
     results = []
@@ -195,6 +190,14 @@
         else:
             results.append(jnp.where(lane < lanes // 2, pltpu.roll(upper, lanes // 2, 1), lower))
     return results
+
+
+def spectral(pairs, z_table, y_table, count):
+    half = pairs.shape[1] // 2
+    summed = [
+        pairs[k, pl.ds(0, half, 2), :] + pairs[k, pl.ds(1, half, 2), :] for k in range(count)
+    ]
+    return transform(summed, z_table, y_table)
 
 
 def sweep_one_kernel(is_first, source, low, high, s1, w, u, v, held, sems):
@@ -257,7 +260,7 @@
             pairs[c, rows, :] = sweep_sum[c]
     planes = source.shape[1] // 2
     blocks = g.shape[0] // group
-    for c, value in enumerate(spectral(pairs, z_table[...], y_table[...], 3)):
+    for c, value in enumerate(spectral(pairs, z_table, y_table, 3)):
         g[pl.ds(c * planes + step, blocks, group), :] = value
 
 
@@ -277,13 +280,15 @@
             pairs[3 + c, rows, :] = v[c, 0, rows, :] + second[2] * total
     planes = source.shape[1] // 2
     blocks = out.shape[0] // group
-    for k, value in enumerate(spectral(pairs, z_table[...], y_table[...], 6)):
+    for k, value in enumerate(spectral(pairs, z_table, y_table, 6)):
         if k < 3:
             value = value + g[pl.ds(k * planes + step, blocks, g_group), :]
         out[pl.ds(k * planes + step, blocks, group), :] = value
 
 
-def solve_kernel(peers, intervals, planes, group, back, values, inverse, forward, backward, out):
+def solve_kernel(
+    peers, intervals, planes, group, back, values, inverse, forward, backward, out_1, out_2
+):
     start = [None] * 3
     for interval in range(intervals):
         loaded = []
@@ -307,116 +312,406 @@
             wanted.append(start[c])
         physical = left_dot(backward[...], jnp.concatenate(wanted, axis=1))
         for field in range(6):
-            base = (field // 3) * (back // 2) + (field % 3) * (planes + 2)
+            out = (out_1, out_2)[field // 3]
+            base = (field % 3) * (planes + 2)
             for e in range(planes + 2):
                 out[pl.ds(interval * back + base + e, peers, intervals * back), :] = physical[
                     e * peers : (e + 1) * peers, field * lanes : (field + 1) * lanes
                 ]
 
 
-def corrected_kernel(
-    nodes, group, *refs
+def edges_kernel(source, low, high, sems):
+    length = source.shape[1]
+    copies = [
+        pltpu.make_async_copy(source.at[:, 0], low, sems.at[0]),
+        pltpu.make_async_copy(source.at[:, length - 1], high, sems.at[1]),
+    ]
+    for copy in copies:
+        copy.start()
+    for copy in copies:
+        copy.wait()
+
+
+def sweep_one_plane(is_first, held, slot, put_s1, put_w, uv, cell):
+    size = held.shape[2] - 2 * pad
+    for row in chunks(size):
+        rows = slice(row, row + rows_at_once)
+        total_first, total_second = [], []
+        for node in range(3):
+            start, old = rhs_rows(held, 3 * node, slot, pad + row)
+            a, b = first[node], second[node] - (half_step if node == 1 else 0.0)
+            if node == 0:
+                for c in range(3):
+                    uv[c, cell, rows, :] += first[0] * old[c] + is_first[0] * start[c]
+                    uv[3 + c, cell, rows, :] += second[0] * old[c]
+                total_first = [start[c] + a * old[c] for c in range(3)]
+                total_second = [b * old[c] for c in range(3)]
+            else:
+                total_first = [total_first[c] + a * old[c] for c in range(3)]
+                total_second = [total_second[c] + b * old[c] for c in range(3)]
+        for c in range(3):
+            put_s1(c, row, total_first[c])
+            put_w(c, row, total_first[c] + total_second[c])
+            uv[c, cell, rows, :] -= total_first[c]
+            uv[3 + c, cell, rows, :] += total_first[c]
+
+
+def sweep_two_plane(held, slot, get_w, put_s2, uv, cell):
+    size = held.shape[2] - 2 * pad
+    for row in chunks(size):
+        rows = slice(row, row + rows_at_once)
+        _, fresh = rhs_rows(held, 0, slot, pad + row)
+        for c in range(3):
+            swept = get_w(c, row) + half_step * fresh[c]
+            put_s2(c, row, swept)
+            uv[c, cell, rows, :] += first[1] * fresh[c]
+            uv[3 + c, cell, rows, :] += second[1] * fresh[c] - swept
+
+
+def last_rhs_pair(held, slot, uv, cell):
+    size = held.shape[2] - 2 * pad
+    for row in chunks(size):
+        rows = slice(row, row + rows_at_once)
+        _, fresh = rhs_rows(held, 0, slot, pad + row)
+        _, other = rhs_rows(held, 0, slot + 1, pad + row)
+        for c in range(3):
+            total = fresh[c] + other[c]
+            uv[c, cell, rows, :] += first[2] * total
+            uv[3 + c, cell, rows, :] += second[2] * total
+
+
+def uv_halves(uv, k, cell):
+    half = uv.shape[2] // 2
+    return uv[k, cell, pl.ds(0, half, 2), :] + uv[k, cell, pl.ds(1, half, 2), :]
+
+
+def held_halves(held, c, slot):
+    half = (held.shape[2] - 2 * pad) // 2
+    total = held[c, slot, pl.ds(pad, half, 2), :] + held[c, slot, pl.ds(pad + 1, half, 2), :]
+    total = total + held[c, slot + 1, pl.ds(pad, half, 2), :]
+    return total + held[c, slot + 1, pl.ds(pad + 1, half, 2), :]
+
+
+def interior_kernel(
+    group, g_group, is_first, source, z_table, y_table,
+    s1_out, s2_out, w_out, uv_end, uv_next, out, g,
+    held, held_1, held_2, w, uv, sems, out_sems
 ):
-    count = 3 * len(nodes)
+    length, size = source.shape[1], source.shape[2]
+    planes = length // 2
+    blocks = out.shape[0] // group
+    rows_all = pl.ds(pad, size)
+
+    def arriving(plane):
+        return pltpu.make_async_copy(
+            source.at[:, plane], held.at[:, plane, rows_all, :], sems.at[plane]
+        )
+
+    def launch(plane, carry):
+        arriving(plane).start()
+        return carry
+
+    lax.fori_loop(0, length, launch, 0)
+    uv[...] = jnp.zeros(uv.shape, f32)
+    arriving(0).wait()
+    arriving(1).wait()
+    wrap_rows(held, 1, 9)
+
+    def s1_copy(plane):
+        return pltpu.make_async_copy(
+            held_1.at[:, plane, rows_all, :], s1_out.at[:, plane - 1], out_sems.at[0, plane]
+        )
+
+    def s2_copy(plane):
+        return pltpu.make_async_copy(
+            held_2.at[:, plane, rows_all, :], s2_out.at[:, plane - 2], out_sems.at[1, plane]
+        )
+
+    def phase_one(plane, carry):
+        arriving(plane + 1).wait()
+        wrap_rows(held, plane + 1, 9)
+
+        def put_s1(c, row, value):
+            held_1[c, plane, pad + row : pad + row + rows_at_once, :] = value
+
+        def put_w(c, row, value):
+            w[c, plane, row : row + rows_at_once, :] = value
+
+        sweep_one_plane(is_first, held, plane, put_s1, put_w, uv, plane // 2)
+        wrap_rows(held_1, plane, 3)
+        s1_copy(plane).start()
+        return carry
+
+    lax.fori_loop(1, length - 1, phase_one, 0)
+
+    def phase_two(plane, carry):
+        def get_w(c, row):
+            return w[c, plane, row : row + rows_at_once, :]
+
+        def put_s2(c, row, value):
+            held_2[c, plane, pad + row : pad + row + rows_at_once, :] = value
+
+        sweep_two_plane(held_1, plane, get_w, put_s2, uv, plane // 2)
+        wrap_rows(held_2, plane, 3)
+        s2_copy(plane).start()
+        return carry
+
+    lax.fori_loop(2, length - 2, phase_two, 0)
+    tails = []
+    for k, plane in enumerate((1, length - 2)):
+        tails.append(pltpu.make_async_copy(w.at[:, plane], w_out.at[:, k], out_sems.at[2, k]))
+    for k, cell in enumerate((0, planes - 1)):
+        tails.append(pltpu.make_async_copy(uv.at[:, cell], uv_end.at[:, k], out_sems.at[2, 2 + k]))
+    for k, cell in enumerate((1, planes - 2)):
+        tails.append(pltpu.make_async_copy(uv.at[:, cell], uv_next.at[:, k], out_sems.at[2, 4 + k]))
+    for copy in tails:
+        copy.start()
+
+    def phase_three(cell, carry):
+        last_rhs_pair(held_2, 2 * cell, uv, cell)
+        return carry
+
+    lax.fori_loop(2, planes - 2, phase_three, 0)
+    for start in range(2, planes - 2, 2):
+        cells = range(start, min(start + 2, planes - 2))
+        entries = [(k, cell) for cell in cells for k in range(6)]
+        values = transform([uv_halves(uv, k, cell) for k, cell in entries], z_table, y_table)
+        for (k, cell), value in zip(entries, values):
+            out[pl.ds(k * planes + cell, blocks, group), :] = value
+    for start in range(1, planes - 1, 4):
+        cells = range(start, min(start + 4, planes - 1))
+        entries = [(c, cell) for cell in cells for c in range(3)]
+        values = transform([held_halves(held_2, c, 2 * cell) for c, cell in entries], z_table, y_table)
+        for (c, cell), value in zip(entries, values):
+            g[pl.ds(c * planes + cell, blocks, g_group), :] = value
+
+    def finish_one(plane, carry):
+        s1_copy(plane).wait()
+        return carry
+
+    def finish_two(plane, carry):
+        s2_copy(plane).wait()
+        return carry
+
+    lax.fori_loop(1, length - 1, finish_one, 0)
+    lax.fori_loop(2, length - 2, finish_two, 0)
+    for copy in tails:
+        copy.wait()
+
+
+def start_all(copies):
+    for copy in copies:
+        copy.start()
+    for copy in copies:
+        copy.wait()
+
+
+def end_one_kernel(
+    is_first, source, low, high, uv_in, low_out, high_out, w_out, uv, held, sems
+):
+    length, size = source.shape[1], source.shape[2]
+    rows_all = pl.ds(pad, size)
+    sources = [low, source.at[:, 0], source.at[:, 1]]
+    sources += [source.at[:, length - 2], source.at[:, length - 1], high]
+    start_all([
+        pltpu.make_async_copy(ref, held.at[:, slot, rows_all, :], sems.at[slot])
+        for slot, ref in enumerate(sources)
+    ])
+    uv[...] = uv_in[...]
+    for k, (slot, ref) in enumerate(((1, low_out), (4, high_out))):
+        wrap_rows(held, slot, 9)
+
+        def put_s1(c, row, value):
+            ref[c, row : row + rows_at_once, :] = value
+
+        def put_w(c, row, value):
+            w_out[c, k, row : row + rows_at_once, :] = value
+
+        sweep_one_plane(is_first, held, slot, put_s1, put_w, uv, k)
+
+
+def end_two_kernel(
+    g_group, swept, low, low_end, high_end, high, w_end, w_next, uv_in, g_in, z_table, y_table,
+    low_out, high_out, next_out, uv, g, held, held_2, sems
+):
+    count, size = swept.shape[1], swept.shape[2]
+    rows_all = pl.ds(pad, size)
+    planes = (count + 2) // 2
+    sources = [low, low_end, swept.at[:, 0], swept.at[:, 1]]
+    sources += [swept.at[:, count - 2], swept.at[:, count - 1], high_end, high]
+    start_all([
+        pltpu.make_async_copy(ref, held.at[:, slot, rows_all, :], sems.at[slot])
+        for slot, ref in enumerate(sources)
+    ])
+    uv[...] = uv_in[...]
+    g[...] = g_in[...]
+    places = ((1, 0, w_end, 0), (2, 0, w_next, 0), (5, 1, w_next, 1), (6, 1, w_end, 1))
+    for index, (slot, cell, w, k) in enumerate(places):
+        wrap_rows(held, slot, 3)
+
+        def get_w(c, row):
+            return w[c, k, row : row + rows_at_once, :]
+
+        def put_s2(c, row, value):
+            rows = slice(row, row + rows_at_once)
+            if slot == 1:
+                low_out[c, rows, :] = value
+            elif slot == 6:
+                high_out[c, rows, :] = value
+            else:
+                next_out[c, k, rows, :] = value
+            held_2[c, index, pad + row : pad + row + rows_at_once, :] = value
+
+        sweep_two_plane(held, slot, get_w, put_s2, uv, cell)
+    blocks = g.shape[0] // g_group
+    entries = [(c, k) for k in range(2) for c in range(3)]
+    values = transform([held_halves(held_2, c, 2 * k) for c, k in entries], z_table, y_table)
+    for (c, k), value in zip(entries, values):
+        g[pl.ds(c * planes + k * (planes - 1), blocks, g_group), :] = value
+
+
+def end_three_kernel(
+    group, g_group, swept, low, low_end, nexts, high_end, high, uv_end, uv_next, f, g,
+    z_table, y_table, pack, out, held, uv, sems, out_sems
+):
+    count, size = swept.shape[1], swept.shape[2]
+    rows_all = pl.ds(pad, size)
+    planes = (count + 4) // 2
+    sources = [low, low_end, nexts.at[:, 0], swept.at[:, 0], swept.at[:, 1], swept.at[:, 2]]
+    sources += [swept.at[:, count - 3], swept.at[:, count - 2], swept.at[:, count - 1]]
+    sources += [nexts.at[:, 1], high_end, high]
+    start_all([
+        pltpu.make_async_copy(ref, held.at[:, slot, rows_all, :], sems.at[slot])
+        for slot, ref in enumerate(sources)
+    ])
+    packing = [
+        pltpu.make_async_copy(held.at[:, slot, rows_all, :], pack.at[:, k], out_sems.at[k])
+        for k, slot in enumerate((0, 1, 2, 9, 10, 11))
+    ]
+    for k in range(2):
+        uv[:, 3 * k] = uv_end[:, k]
+        uv[:, 1 + k] = uv_next[:, k]
+    out[...] = f[...]
+    for slot in (1, 2, 3, 4, 7, 8, 9, 10):
+        wrap_rows(held, slot, 3)
+    for copy in packing:
+        copy.start()
+    for index, slot in enumerate((1, 3, 7, 9)):
+        last_rhs_pair(held, slot, uv, index)
+    blocks = out.shape[0] // group
+    cells = (0, 1, planes - 2, planes - 1)
+    for half in range(2):
+        entries = [(k, index) for index in (2 * half, 2 * half + 1) for k in range(6)]
+        values = transform([uv_halves(uv, k, index) for k, index in entries], z_table, y_table)
+        for (k, index), value in zip(entries, values):
+            out[pl.ds(k * planes + cells[index], blocks, group), :] = value
+    for block in range(blocks):
+        out[block * group : block * group + 3 * planes, :] += g[
+            block * g_group : block * g_group + 3 * planes, :
+        ]
+    for copy in packing:
+        copy.wait()
+
+
+def corrected_kernel(node, group, layouts, counts, *refs):
+    if len(layouts) > 1:
+        is_first, refs = refs[0], refs[1:]
     spectra, z_table, y_table = refs[:3]
-    fields = [refs[3 + 3 * k : 6 + 3 * k] for k in range(len(nodes))]
+    fields = refs[3 : 3 + counts]
     new_velocity, new_rhs, held, coarse, result, sems, out_sems, rhs_sems = refs[-8:]
-    length = fields[0][0].shape[1]
-    size = fields[0][0].shape[2]
+    length, size = held.shape[1] - 2, held.shape[2] - 2 * pad
     planes = length // 2
     rows_all = pl.ds(pad, size)
-    inner_copies, edge_copies = [], []
-    for k, (source, low, high) in enumerate(fields):
-        place = held.at[3 * k : 3 * k + 3]
-        edge_copies.append(
-            pltpu.make_async_copy(low, place.at[:, 0, rows_all, :], sems.at[k, length])
+
+    def arriving(layout, slot):
+        number, index = layout[slot]
+        ref = fields[number]
+        ref = ref.at[0:3, index] if index is not None else ref.at[0:3]
+        return pltpu.make_async_copy(ref, held.at[:, slot, rows_all, :], sems.at[slot])
+
+    def launch(layout):
+        for slot in range(length + 2):
+            arriving(layout, slot).start()
+
+    if len(layouts) > 1:
+
+        @pl.when(is_first[0] > 0)
+        def _():
+            launch(layouts[0])
+
+        @pl.when(is_first[0] <= 0)
+        def _():
+            launch(layouts[1])
+    else:
+        launch(layouts[0])
+    blocks = spectra.shape[0] // group
+    for c in range(3):
+        base = c * (planes + 2)
+        parts = [spectra[pl.ds(base + e, blocks, group), :] for e in range(planes + 2)]
+        in_z = right_dot(jnp.concatenate(parts, axis=0), z_table[...])
+        for e in range(planes + 2):
+            mine = in_z[e * blocks : (e + 1) * blocks]
+            stacked = jnp.concatenate([mine[:, :size], mine[:, size:]], axis=0)
+            coarse[c, e] = left_dot(y_table[...], stacked)
+    for slot in range(length + 2):
+        arriving(layouts[0], slot).wait()
+
+    def out_copy(plane):
+        return pltpu.make_async_copy(
+            held.at[:, plane + 1, rows_all, :], new_velocity.at[node, :, plane], out_sems.at[plane]
         )
-        edge_copies.append(
-            pltpu.make_async_copy(high, place.at[:, length + 1, rows_all, :], sems.at[k, length + 1])
+
+    def rhs_copy(plane):
+        return pltpu.make_async_copy(
+            result.at[:, plane], new_rhs.at[node, :, plane], rhs_sems.at[plane]
         )
-        for plane in range(length):
-            inner_copies.append(
-                pltpu.make_async_copy(
-                    source.at[:, plane], place.at[:, plane + 1, rows_all, :], sems.at[k, plane]
-                )
-            )
-    for copy in edge_copies + inner_copies:
-        copy.start()
-    blocks = spectra.shape[0] // group
-    for k in range(len(nodes)):
-        for c in range(3):
-            base = k * (group // len(nodes)) + c * (planes + 2)
-            parts = [spectra[pl.ds(base + e, blocks, group), :] for e in range(planes + 2)]
-            in_z = right_dot(jnp.concatenate(parts, axis=0), z_table[...])
-            for e in range(planes + 2):
-                mine = in_z[e * blocks : (e + 1) * blocks]
-                stacked = jnp.concatenate([mine[:, :size], mine[:, size:]], axis=0)
-                coarse[3 * k + c, e] = left_dot(y_table[...], stacked)
-    for copy in edge_copies + inner_copies:
-        copy.wait()
-
-    def out_copy(k, plane):
-        return pltpu.make_async_copy(
-            held.at[3 * k : 3 * k + 3, plane + 1, rows_all, :],
-            new_velocity.at[nodes[k], :, plane],
-            out_sems.at[k, plane],
-        )
-
-    def rhs_copy(k, plane):
-        return pltpu.make_async_copy(
-            result.at[3 * k : 3 * k + 3, plane],
-            new_rhs.at[nodes[k], :, plane],
-            rhs_sems.at[k, plane],
-        )
 
     def correct(plane, cell, odd):
-        for field in range(count):
+        for field in range(3):
             for row in chunks(size):
                 rows = slice(row, row + rows_at_once)
                 held_rows = slice(pad + row, pad + row + rows_at_once)
                 value = coarse[field, cell, rows, :]
                 if odd:
                     value = 0.5 * (value + coarse[field, cell + 1, rows, :])
-                held[field, plane, held_rows, :] = held[field, plane, held_rows, :] + value
-        wrap_rows(held, plane, count)
+                held[field, plane, held_rows, :] += value
+        wrap_rows(held, plane, 3)
 
     correct(0, 0, True)
     correct(1, 1, False)
-    for k in range(len(nodes)):
-        out_copy(k, 0).start()
+    out_copy(0).start()
 
     def body(q, carry):
         correct(2 * q + 2, q + 1, True)
         correct(2 * q + 3, q + 2, False)
-        for k in range(len(nodes)):
-            out_copy(k, 2 * q + 1).start()
-
-            @pl.when(2 * q + 2 < length)
-            def _():
-                out_copy(k, 2 * q + 2).start()
+        out_copy(2 * q + 1).start()
+
+        @pl.when(2 * q + 2 < length)
+        def _():
+            out_copy(2 * q + 2).start()
 
         for part in range(2):
             plane = 2 * q + part
-            for k in range(len(nodes)):
-                for row in chunks(size):
-                    _, fresh = rhs_rows(held, 3 * k, plane + 1, pad + row)
-                    for c in range(3):
-                        result[3 * k + c, plane, row : row + rows_at_once, :] = fresh[c].astype(bf16)
-                rhs_copy(k, plane).start()
+            for row in chunks(size):
+                _, fresh = rhs_rows(held, 0, plane + 1, pad + row)
+                for c in range(3):
+                    result[c, plane, row : row + rows_at_once, :] = fresh[c].astype(bf16)
+            rhs_copy(plane).start()
         return carry
 
     lax.fori_loop(0, planes, body, 0)
 
     def finish(plane, carry):
-        for k in range(len(nodes)):
-            out_copy(k, plane).wait()
-            rhs_copy(k, plane).wait()
+        out_copy(plane).wait()
+        rhs_copy(plane).wait()
         return carry
 
     lax.fori_loop(0, length, finish, 0)
 
 
 anywhere = pl.BlockSpec(memory_space=pl.ANY)
+scalar = pl.BlockSpec(memory_space=pltpu.SMEM)
+vmem = pl.BlockSpec(memory_space=pltpu.VMEM)
 
 
 def whole(shape):
@@ -447,38 +742,210 @@
     return lax.ppermute(value, "tm", [(i, i + 1) for i in range(count - 1)])
 
 
-def corrected(nodes, spectra, tables, fields, outs):
-    length, size_y, size_z = fields[0][0].shape[1:]
-    count = 3 * len(nodes)
+def corrected(node, spectra, tables, fields, layouts, outs, is_first=None):
+    length = len(layouts[0]) - 2
+    size_y, size_z = fields[0].shape[-2:]
     planes = length // 2
     group = spectra.shape[1]
     operands = [spectra.reshape(-1, lanes), *tables]
-    for field in fields:
-        operands.extend(field)
-    specs = [whole(o.shape) for o in operands[:3]] + [anywhere] * (len(operands) - 3)
+    specs = [whole(o.shape) for o in operands]
+    if is_first is not None:
+        operands, specs = [is_first, *operands], [scalar, *specs]
+    operands, specs = [*operands, *fields], specs + [anywhere] * len(fields)
     shape = (3, 3, length, size_y, size_z)
     aliases = {}
     if outs is not None:
         aliases = {len(operands): 0, len(operands) + 1: 1}
-        operands.extend(outs)
-        specs += [anywhere] * 2
+        operands, specs = [*operands, *outs], specs + [anywhere] * 2
     return pl.pallas_call(
-        functools.partial(corrected_kernel, nodes, group),
+        functools.partial(corrected_kernel, node, group, layouts, len(fields)),
         out_shape=(struct(shape), struct(shape, bf16)),
         in_specs=specs,
         out_specs=(anywhere, anywhere),
         input_output_aliases=aliases,
         scratch_shapes=[
-            held_planes(count, length, size_y, size_z),
-            pltpu.VMEM((count, planes + 2, size_y, size_z), f32),
-            pltpu.VMEM((count, length, size_y, size_z), bf16),
-            pltpu.SemaphoreType.DMA((len(nodes), length + 2)),
-            pltpu.SemaphoreType.DMA((len(nodes), length)),
-            pltpu.SemaphoreType.DMA((len(nodes), length)),
+            held_planes(3, length, size_y, size_z),
+            pltpu.VMEM((3, planes + 2, size_y, size_z), f32),
+            pltpu.VMEM((3, length, size_y, size_z), bf16),
+            pltpu.SemaphoreType.DMA((length + 2,)),
+            pltpu.SemaphoreType.DMA((length,)),
+            pltpu.SemaphoreType.DMA((length,)),
         ],
         compiler_params=params,
-        name="corrected",
+        name=f"corrected_{node}",
     )(*operands)
+
+
+def sweep_whole(fields, is_first, z_table, y_table, blocks):
+    length, size_y, size_z = fields.shape[1:]
+    planes = length // 2
+    low, high = neighbours(fields[:, 0], fields[:, length - 1])
+    fine = (3, length, size_y, size_z)
+    halved = (3, planes, size_y, size_z)
+    two = (3, 2, size_y, size_z)
+    one = (3, 1, size_y, size_z)
+    in_sems = pltpu.SemaphoreType.DMA((length + 2,))
+    swept_1, w, u, v = pl.pallas_call(
+        sweep_one_kernel,
+        grid=(planes,),
+        out_shape=(struct(fine), struct(fine), struct(halved), struct(halved)),
+        in_specs=[scalar, anywhere, anywhere, anywhere],
+        out_specs=(slab(two), slab(two), slab(one), slab(one)),
+        scratch_shapes=[held_planes(9, length, size_y, size_z), in_sems],
+        compiler_params=params,
+        name="sweep_one",
+    )(is_first, fields, low, high)
+    low_1, high_1 = neighbours(swept_1[:, 0], swept_1[:, length - 1])
+
+    g_group = round_up(3 * planes, 8)
+    swept_2, u, v, g = pl.pallas_call(
+        functools.partial(sweep_two_kernel, g_group),
+        grid=(planes,),
+        out_shape=(struct(fine), struct(halved), struct(halved), struct((blocks * g_group, lanes))),
+        in_specs=[anywhere, anywhere, anywhere, slab(two), slab(one), slab(one)]
+        + [whole(z_table.shape), whole(y_table.shape)],
+        out_specs=(slab(two), slab(one), slab(one), whole((blocks * g_group, lanes))),
+        scratch_shapes=[
+            held_planes(3, length, size_y, size_z),
+            pltpu.VMEM((3, size_y, size_z), f32),
+            in_sems,
+        ],
+        compiler_params=params,
+        name="sweep_two",
+    )(swept_1, low_1, high_1, w, u, v, z_table, y_table)
+    low_2, high_2 = neighbours(swept_2[:, 0], swept_2[:, length - 1])
+    g = later_interval(g)
+
+    group = round_up(6 * planes, 8)
+    sources = pl.pallas_call(
+        functools.partial(source_kernel, group, g_group),
+        grid=(planes,),
+        out_shape=struct((blocks * group, lanes)),
+        in_specs=[anywhere, anywhere, anywhere, slab(one), slab(one), whole(g.shape)]
+        + [whole(z_table.shape), whole(y_table.shape)],
+        out_specs=whole((blocks * group, lanes)),
+        scratch_shapes=[
+            held_planes(3, length, size_y, size_z),
+            pltpu.VMEM((6, size_y, size_z), f32),
+            in_sems,
+        ],
+        compiler_params=params,
+        name="sources",
+    )(swept_2, low_2, high_2, u, v, g, z_table, y_table)
+    layout = tuple([(0, None)] + [(1, p) for p in range(length)] + [(2, None)])
+    carried = [later_interval(value) for value in (low_2, swept_2, high_2)]
+    later = tuple((3 + number, index) for number, index in layout)
+    return (
+        sources,
+        ((low_1, swept_1, high_1), (layout,)),
+        ((low_2, swept_2, high_2), (layout,)),
+        ((low, fields, high, *carried), (layout, later)),
+    )
+
+
+def sweep_split(fields, is_first, z_table, y_table, blocks):
+    length, size_y, size_z = fields.shape[1:]
+    planes = length // 2
+    plane, g_group, group = (size_y, size_z), round_up(3 * planes, 8), round_up(6 * planes, 8)
+
+    def held(count, slots):
+        return pltpu.VMEM((count, slots, size_y + 2 * pad, size_z), f32)
+
+    def sems(*shape):
+        return pltpu.SemaphoreType.DMA(shape)
+
+    low, high = pl.pallas_call(
+        edges_kernel,
+        out_shape=(struct((9, *plane)),) * 2,
+        in_specs=[anywhere],
+        out_specs=(anywhere,) * 2,
+        scratch_shapes=[sems(2)],
+        name="edges",
+    )(fields)
+    low, high = neighbours(low, high)
+    swept_1, swept_2, w_next, uv_end, uv_next, f, g = pl.pallas_call(
+        functools.partial(interior_kernel, group, g_group),
+        out_shape=(
+            struct((3, length - 2, *plane)),
+            struct((3, length - 4, *plane)),
+            struct((3, 2, *plane)),
+            struct((6, 2, *plane)),
+            struct((6, 2, *plane)),
+            struct((blocks * group, lanes)),
+            struct((blocks * g_group, lanes)),
+        ),
+        in_specs=[scalar, anywhere, vmem, vmem],
+        out_specs=(anywhere,) * 5 + (vmem,) * 2,
+        scratch_shapes=[
+            held(9, length),
+            held(3, length),
+            held(3, length),
+            pltpu.VMEM((3, length, *plane), f32),
+            pltpu.VMEM((6, planes, *plane), f32),
+            sems(length),
+            sems(3, max(length, 6)),
+        ],
+        compiler_params=params,
+        cost_estimate=pl.CostEstimate(flops=4 * 10**9, bytes_accessed=6 * 10**7, transcendentals=0),
+        name="interior",
+    )(is_first, fields, z_table, y_table)
+    low_end_1, high_end_1, w_end, uv_end = pl.pallas_call(
+        end_one_kernel,
+        out_shape=(
+            struct((3, *plane)),
+            struct((3, *plane)),
+            struct((3, 2, *plane)),
+            struct((6, 2, *plane)),
+        ),
+        in_specs=[scalar, anywhere, anywhere, anywhere, vmem],
+        out_specs=(vmem,) * 4,
+        scratch_shapes=[held(9, 6), sems(6)],
+        compiler_params=params,
+        name="end_one",
+    )(is_first, fields, low, high, uv_end)
+    low_1, high_1 = neighbours(low_end_1, high_end_1)
+    low_end_2, high_end_2, next_2, uv_end, g = pl.pallas_call(
+        functools.partial(end_two_kernel, g_group),
+        out_shape=(
+            struct((3, *plane)),
+            struct((3, *plane)),
+            struct((3, 2, *plane)),
+            struct((6, 2, *plane)),
+            struct((blocks * g_group, lanes)),
+        ),
+        in_specs=[anywhere] * 5 + [vmem] * 6,
+        out_specs=(vmem,) * 5,
+        scratch_shapes=[held(3, 8), held(3, 4), sems(8)],
+        compiler_params=params,
+        name="end_two",
+    )(swept_1, low_1, low_end_1, high_end_1, high_1, w_end, w_next, uv_end, g, z_table, y_table)
+    low_2, high_2 = neighbours(low_end_2, high_end_2)
+    pack, sources = pl.pallas_call(
+        functools.partial(end_three_kernel, group, g_group),
+        out_shape=(struct((3, 6, *plane)), struct((blocks * group, lanes))),
+        in_specs=[anywhere] * 6 + [vmem] * 6,
+        out_specs=(anywhere, vmem),
+        scratch_shapes=[held(3, 12), pltpu.VMEM((6, 4, *plane), f32), sems(12), sems(6)],
+        compiler_params=params,
+        name="end_three",
+    )(
+        swept_2, low_2, low_end_2, next_2, high_end_2, high_2, uv_end, uv_next, f,
+        later_interval(g), z_table, y_table
+    )
+    layout_1 = [(0, None), (1, None)] + [(2, p) for p in range(length - 2)] + [(3, None), (4, None)]
+    layout_2 = [(0, None), (1, None), (2, 0)] + [(3, p) for p in range(length - 4)]
+    layout_2 += [(2, 1), (4, None), (5, None)]
+    layout_0 = [(0, None)] + [(1, p) for p in range(length)] + [(2, None)]
+    later = [(3, 0), (3, 1), (3, 2)] + [(4, p) for p in range(length - 4)] + [(3, 3), (3, 4), (3, 5)]
+    return (
+        sources,
+        ((low_1, low_end_1, swept_1, high_end_1, high_1), (tuple(layout_1),)),
+        ((low_2, low_end_2, next_2, swept_2, high_end_2, high_2), (tuple(layout_2),)),
+        (
+            (low, fields, high, later_interval(pack), later_interval(swept_2)),
+            (tuple(layout_0), tuple(later)),
+        ),
+    )
 
 
 def per_device(velocity):
@@ -513,62 +980,10 @@
     total = jnp.asarray(wave_squares(coarse_x), f32)[:, None] + mine
     rates = 1.0 / (1.0 + half_step * coarse_viscosity * (4.0 / (2.0 * 2.0)) * total)
 
-    low, high = neighbours(fields[:, 0], fields[:, length - 1])
-    fine = (3, length, size_y, size_z)
-    halved = (3, planes, size_y, size_z)
-    two = (3, 2, size_y, size_z)
-    one = (3, 1, size_y, size_z)
-    in_sems = pltpu.SemaphoreType.DMA((length + 2,))
-    swept_1, w, u, v = pl.pallas_call(
-        sweep_one_kernel,
-        grid=(planes,),
-        out_shape=(struct(fine), struct(fine), struct(halved), struct(halved)),
-        in_specs=[pl.BlockSpec(memory_space=pltpu.SMEM), anywhere, anywhere, anywhere],
-        out_specs=(slab(two), slab(two), slab(one), slab(one)),
-        scratch_shapes=[held_planes(9, length, size_y, size_z), in_sems],
-        compiler_params=params,
-        name="sweep_one",
-    )(tm_first.astype(f32).reshape(1), fields, low, high)
-    low_1, high_1 = neighbours(swept_1[:, 0], swept_1[:, length - 1])
-
-    g_group = round_up(3 * planes, 8)
-    swept_2, u, v, g = pl.pallas_call(
-        functools.partial(sweep_two_kernel, g_group),
-        grid=(planes,),
-        out_shape=(struct(fine), struct(halved), struct(halved), struct((blocks * g_group, lanes))),
-        in_specs=[anywhere, anywhere, anywhere, slab(two), slab(one), slab(one)]
-        + [whole(z_table.shape), whole(y_table.shape)],
-        out_specs=(slab(two), slab(one), slab(one), whole((blocks * g_group, lanes))),
-        scratch_shapes=[
-            held_planes(3, length, size_y, size_z),
-            pltpu.VMEM((3, size_y, size_z), f32),
-            in_sems,
-        ],
-        compiler_params=params,
-        name="sweep_two",
-    )(swept_1, low_1, high_1, w, u, v, z_table, y_table)
-    low_2, high_2 = neighbours(swept_2[:, 0], swept_2[:, length - 1])
-    g = later_interval(g)
-
+    is_first = tm_first.astype(f32).reshape(1)
+    sweep = sweep_split if length >= 10 else sweep_whole
+    sources, one, two, zero = sweep(fields, is_first, z_table, y_table, blocks)
     group = round_up(6 * planes, 8)
-    sources = pl.pallas_call(
-        functools.partial(source_kernel, group, g_group),
-        grid=(planes,),
-        out_shape=struct((blocks * group, lanes)),
-        in_specs=[anywhere, anywhere, anywhere, slab(one), slab(one), whole(g.shape)]
-        + [whole(z_table.shape), whole(y_table.shape)],
-        out_specs=whole((blocks * group, lanes)),
-        scratch_shapes=[
-            held_planes(3, length, size_y, size_z),
-            pltpu.VMEM((6, size_y, size_z), f32),
-            in_sems,
-        ],
-        compiler_params=params,
-        name="sources",
-    )(swept_2, low_2, high_2, u, v, g, z_table, y_table)
-    carried = later_interval(swept_2)
-    carried_low = later_interval(low_2)
-    carried_high = later_interval(high_2)
 
     both = ("space", "tm")
 
@@ -587,36 +1002,20 @@
             value = value.reshape(blocks, per_block, rows, columns).swapaxes(1, 2)
         return value.reshape(blocks, rows, lanes)
 
-    back = 2 * round_up(3 * (planes + 2), 8)
-    solved = pl.pallas_call(
+    back = round_up(3 * (planes + 2), 8)
+    columned = to_columns(sources, group)
+    solved_1, solved_2 = pl.pallas_call(
         functools.partial(solve_kernel, peers, intervals, planes, group, back),
-        out_shape=struct((devices * back, lanes)),
+        out_shape=(struct((devices * back, lanes)),) * 2,
         compiler_params=params,
         name="solve",
-    )(to_columns(sources, group), rates, x_forward, x_backward)
-    spectra = to_planes(solved, back)
-    carried_spectra = later_interval(spectra[:, back // 2 :])
-
-    outs = corrected(
-        (1, 2),
-        spectra,
-        (z_back_table, y_back_table),
-        ((swept_1, low_1, high_1), (swept_2, low_2, high_2)),
-        None,
-    )
-    new_velocity, new_rhs = corrected(
-        (0,),
-        carried_spectra,
-        (z_back_table, y_back_table),
-        (
-            (
-                jnp.where(tm_first, fields[:3], carried),
-                jnp.where(tm_first, low[:3], carried_low),
-                jnp.where(tm_first, high[:3], carried_high),
-            ),
-        ),
-        outs,
-    )
+    )(columned, rates, x_forward, x_backward)
+    spectra_2 = to_planes(solved_2, back)
+    spectra_1 = to_planes(solved_1, back)
+    tables = (z_back_table, y_back_table)
+    outs = corrected(2, spectra_2, tables, *two, None)
+    outs = corrected(1, spectra_1, tables, *one, outs)
+    new_velocity, new_rhs = corrected(0, later_interval(spectra_2), tables, *zero, outs, is_first)
     return (new_velocity[None], new_rhs[None])
 
 

time: 185 us -> 192 us (1.038)
  Pallas kernels: 53.3 us -> 86.7 us
  waiting for transfers between devices: 80.8 us -> 50.7 us
  local copies, waits for them, and re-layouts: 8.5 us -> 14.1 us
  other arithmetic: 5.44 us -> 0.08 us
  starting transfers between devices: 35.4 us -> 38.5 us
    pallas_call x5 -> x8, Pallas kernels: 50.9 us -> 85.2 us  [the longest x1 36.9 us: sweep_split(): pl.pallas_call(edges_kernel, out_shape=(struct((9, *plane)),) * 2, in_spe...]
    ppermute x5 -> x4, waiting for transfers between devices: 24.4 us -> 0.01 us  [later_interval(): return lax.ppermute(value, 'tm', [(i, i + 1) for i in range(count - 1)])]
    ppermute x3, waiting for transfers between devices: 30.3 us -> 9.83 us  [neighbours(): lax.ppermute(low_plane, 'space', down)]
    all_to_all x1 -> x2, waiting for transfers between devices: 0.01 us -> 12.9 us  [to_planes(): value = lax.all_to_all(value, both, split_axis=0, concat_axis=0, tiled=True)]
    unnamed x17 -> x52, local copies, waits for them, and re-layouts: 5.58 us -> 13.4 us
    select_n x3 -> x0, other arithmetic: 5.36 us -> none  [the longest x1 5.31 us: per_device(): jnp.where(tm_first, fields[:3], carried)]
    ppermute x5 -> x4, starting transfers between devices: 18.5 us -> 15.1 us  [later_interval(): return lax.ppermute(value, 'tm', [(i, i + 1) for i in range(count - 1)])]
    all_to_all x1 -> x2, starting transfers between devices: 4.09 us -> 7.41 us  [to_planes(): value = lax.all_to_all(value, both, split_axis=0, concat_axis=0, tiled=True)]
  transfers between devices with their start and end apart: 13 -> 13, of which waited for: 8 -> 9; matrix products, arithmetic and copies ran while one was open for 4% -> 0% of each run, Pallas kernels for 8% -> 15%
where the time goes in v2:
time: 192 us; the launch traced here: 191 us
  Pallas kernels  86.7 us (45%)
  waiting for transfers between devices  50.7 us (26%)
  starting transfers between devices  38.5 us (20%)
  local copies, waits for them, and re-layouts  14.1 us (7%)
    pallas_call x1, Pallas kernels, sweep_split(): pl.pallas_call(edges_kernel, out_shape=(struct((9, *plane)),) * 2, in_spe...  36.9 us
    pallas_call x3, Pallas kernels, corrected(): pl.pallas_call(functools.partial(corrected_kernel, node, group, layouts,...  19.2 us
    pallas_call x1, Pallas kernels, sweep_split(): pl.pallas_call(functools.partial(interior_kernel, group, g_group), out_sh...  16.1 us
    all_to_all x1, waiting for transfers between devices, to_columns(): value = lax.all_to_all(value, both, split_axis=0, concat_axis=0, tiled=True)  15.9 us
    ppermute x4, starting transfers between devices, later_interval(): return lax.ppermute(value, 'tm', [(i, i + 1) for i in range(count - 1)])  15.1 us
    unnamed x52, local copies, waits for them, and re-layouts  13.4 us
    all_to_all x2, waiting for transfers between devices, to_planes(): value = lax.all_to_all(value, both, split_axis=0, concat_axis=0, tiled=True)  12.9 us
    ppermute x3, waiting for transfers between devices, neighbours(): lax.ppermute(high_plane, 'space', up)  12 us
  transfers between devices with their start and end apart: 13, of which 9 were waited for; matrix products, arithmetic and copies ran while one was open for 0% of the time, Pallas kernels for 15%

profile of v2, /device:TPU:1, one launch (start us, length us, event | category | flops | bytes accessed | tf_op | source)
XLA Modules:
  0.0 191.1 jit_solution(5078979215982156018)
XLA Ops:
  0.7 36.9 %edges.1 = (f32[9,128,128]{2,1,0:T(8,128)}, f32[9,128,128]{2,1,0:T(8,128)}) custom-call(f32[9,16,128,128]{3,2,1,0:T(8,128)} %bitcast.19), custom_call_target="tpu_custom_call" | custom-call | tf_op jit(solution)/shard_map/edges/pallas_call | solution.py:857
  37.5 2.1 %collective-permute-start = (f32[9,128,128]{2,1,0:T(8,128)}, f32[9,128,128]{2,1,0:T(8,128)S(1)}, u32[]{:S(2)}, u32[]{:S(2)}) collective-permute-start(f32[9,128,128]{2,1,0:T(8,128)} %get-tuple-element.32), channel_id=1, source_target_pairs={{0,4},{4,8},{8,12},{12,16},{16,20},{20,24},{24,28},{28,0},{1,5},{5... | collective-permute-start | bytes 1769480 | tf_op jit(solution)/shard_map/ppermute | solution.py:737
  39.6 3.1 %collective-permute-start.1 = (f32[9,128,128]{2,1,0:T(8,128)}, f32[9,128,128]{2,1,0:T(8,128)S(1)}, u32[]{:S(2)}, u32[]{:S(2)}) collective-permute-start(f32[9,128,128]{2,1,0:T(8,128)} %get-tuple-element.33), channel_id=1, source_target_pairs={{4,0},{8,4},{12,8},{16,12},{20,16},{24,20},{28,24},{0,28},{5,1},{9... | collective-permute-start | bytes 1769480 | tf_op jit(solution)/shard_map/ppermute | solution.py:737
  42.7 16.1 %interior.1 = (f32[3,14,128,128]{3,2,1,0:T(8,128)}, f32[3,12,128,128]{3,2,1,0:T(8,128)}, f32[3,2,128,128]{3,2,1,0:T(8,128)S(1)}, f32[6,2,128,128]{3,2,1,0:T(8,12...) custom-call(f32[1]{0:T(128)} %bitcast.is_first.refs_0_, ...), custom_call_target="tpu_custom_call" | custom-call | flops 4000000000 | bytes 60000000 | tf_op jit(solution)/shard_map/interior/pallas_call | solution.py:866
  59.8 4.8 %collective-permute-done.low.refs_4_ = f32[9,128,128]{2,1,0:T(8,128)S(1)} collective-permute-done((f32[9,128,128]{2,1,0:T(8,128)}, f32[9,128,128]{2,1,0:T(8,128)S(1)}, u32[]{:S(2)}, u32[]{:S(2)}) %collective-permute-start) | collective-permute-done | bytes 589856 | tf_op jit(solution)/shard_map/ppermute | solution.py:737
  64.6 1.8 collective-permute-done.1.high.refs_6_
  66.4 2.6 %end_one.1 = (f32[3,128,128]{2,1,0:T(8,128)S(1)}, f32[3,128,128]{2,1,0:T(8,128)S(1)}, f32[3,2,128,128]{3,2,1,0:T(8,128)S(1)}, f32[6,2,128,128]{3,2,1,0:T(8,128)S(1)}) custom-call(f32[1]{0:T(128)} %bitcast.is_first.refs_0_, f32[9,16,128,128]{3,2,1,0:T(8,128)} %bitcast.21, f32[9,128,128]{2,1,0:T(8,128)S(1)} %collective-permute-done.low.refs_4_, ...), custom_call_target="tpu_custom_call" | custom-call | tf_op jit(solution)/shard_map/end_one/pallas_call | solution.py:892
  70.2 3.8 %collective-permute-start.3 = (f32[3,128,128]{2,1,0:T(8,128)S(1)}, f32[3,128,128]{2,1,0:T(8,128)S(1)}, u32[]{:S(2)}, u32[]{:S(2)}) collective-permute-start(f32[3,128,128]{2,1,0:T(8,128)S(1)} %get-tuple-element.36.low_end.refs_4_), channel_id=1, source_target_pairs={{4,0},{8,4},{12,8},{16,12},{20,16},{24,20},{28,24},{0,28},{5,1},{9... | collective-permute-start | bytes 589832 | tf_op jit(solution)/shard_map/ppermute | solution.py:737
  74.1 3.2 %collective-permute-done.2.low.refs_3_ = f32[3,128,128]{2,1,0:T(8,128)S(1)} collective-permute-done((f32[3,128,128]{2,1,0:T(8,128)S(1)}, f32[3,128,128]{2,1,0:T(8,128)S(1)}, u32[]{:S(2)}, u32[]{:S(2)}) %collective-permute-start.2) | collective-permute-done | bytes 196640 | tf_op jit(solution)/shard_map/ppermute | solution.py:737
  77.2 5.1 %collective-permute-done.3.high.refs_7_ = f32[3,128,128]{2,1,0:T(8,128)S(1)} collective-permute-done((f32[3,128,128]{2,1,0:T(8,128)S(1)}, f32[3,128,128]{2,1,0:T(8,128)S(1)}, u32[]{:S(2)}, u32[]{:S(2)}) %collective-permute-start.3) | collective-permute-done | bytes 196640 | tf_op jit(solution)/shard_map/ppermute | solution.py:737
  82.3 4.4 %end_two.1 = (f32[3,128,128]{2,1,0:T(8,128)S(1)}, f32[3,128,128]{2,1,0:T(8,128)S(1)}, f32[3,2,128,128]{3,2,1,0:T(8,128)S(1)}, f32[6,2,128,128]{3,2,1,0:T(8,128)}, f32[768,128]{1,0:T(8,128)S(1)}) custom-call(f32[3,14,128,128]{3,2,1,0:T(8,128)} %get-tuple-element.31.swept.refs_5_, f32[3,128,128]{2,1,0:T(8,128)S(1)} %collective-permute-done.2.low.refs_3_, ...), custom_call_target="tpu_custom_call" | custom-call | tf_op jit(solution)/shard_map/end_two/pallas_call | solution.py:907
  86.8 4.3 %collective-permute-start.6 = (f32[768,128]{1,0:T(8,128)S(1)}, f32[768,128]{1,0:T(8,128)S(1)}, u32[]{:S(2)}, u32[]{:S(2)}) collective-permute-start(f32[768,128]{1,0:T(8,128)S(1)} %get-tuple-element.47), channel_id=1, source_target_pairs={{0,1},{1,2},{2,3},{4,5},{5,6},{6,7},{8,9},{9,10},{10,11},{12,13},{... | collective-permute-start | bytes 1179656 | tf_op jit(solution)/shard_map/ppermute | solution.py:742
  91.2 4.1 %collective-permute-start.5 = (f32[3,128,128]{2,1,0:T(8,128)S(1)}, f32[3,128,128]{2,1,0:T(8,128)S(1)}, u32[]{:S(2)}, u32[]{:S(2)}) collective-permute-start(f32[3,128,128]{2,1,0:T(8,128)S(1)} %get-tuple-element.42.low_end.refs_4_), channel_id=1, source_target_pairs={{4,0},{8,4},{12,8},{16,12},{20,16},{24,20},{28,24},{0,28},{5,1},{9... | collective-permute-start | bytes 589832 | tf_op jit(solution)/shard_map/ppermute | solution.py:737
  95.3 4.0 %collective-permute-done.4.low.refs_3_ = f32[3,128,128]{2,1,0:T(8,128)S(1)} collective-permute-done((f32[3,128,128]{2,1,0:T(8,128)S(1)}, f32[3,128,128]{2,1,0:T(8,128)S(1)}, u32[]{:S(2)}, u32[]{:S(2)}) %collective-permute-start.4) | collective-permute-done | bytes 196640 | tf_op jit(solution)/shard_map/ppermute | solution.py:737
  99.4 2.9 %collective-permute-done.5.high.refs_8_ = f32[3,128,128]{2,1,0:T(8,128)S(1)} collective-permute-done((f32[3,128,128]{2,1,0:T(8,128)S(1)}, f32[3,128,128]{2,1,0:T(8,128)S(1)}, u32[]{:S(2)}, u32[]{:S(2)}) %collective-permute-start.5) | collective-permute-done | bytes 196640 | tf_op jit(solution)/shard_map/ppermute | solution.py:737
  102.3 1.2 copy-done.16
  103.5 5.9 %end_three.1 = (f32[3,6,128,128]{3,2,1,0:T(8,128)}, f32[1536,128]{1,0:T(8,128)S(1)}) custom-call(f32[3,12,128,128]{3,2,1,0:T(8,128)} %get-tuple-element.30.swept.refs_6_, f32[3,128,128]{2,1,0:T(8,128)S(1)} %collective-permute-done.4.low.refs_3_, f32[3,128,128]{2,1,0:T(8,128)S(1)} %get-tuple-element.42.low_end.refs_4_, ...), custom_call_target="tpu_custom_call" | custom-call | tf_op jit(solution)/shard_map/end_three/pallas_call | solution.py:923
  110.4 2.4 %all-to-all-start = ((f32[32,48,128]{2,1,0:T(8,128)}), f32[32,48,128]{2,1,0:T(8,128)S(1)}, u32[]{:S(2)}, u32[]{:S(2)}) async-start(f32[32,48,128]{2,1,0:T(8,128)} %bitcast.16), calls=%async_computation | async-start | bytes 1572864 | tf_op jit(solution)/shard_map/all_to_all | solution.py:994
  112.7 3.5 %collective-permute-start.9 = (f32[3,12,128,128]{3,2,1,0:T(8,128)}, f32[3,12,128,128]{3,2,1,0:T(8,128)}, u32[]{:S(2)}, u32[]{:S(2)}) collective-permute-start(f32[3,12,128,128]{3,2,1,0:T(8,128)} %get-tuple-element.30.swept.refs_6_), channel_id=1, source_target_pairs={{0,1},{1,2},{2,3},{4,5},{5,6},{6,7},{8,9},{9,10},{10,11},{12,13},{... | collective-permute-start | bytes 7077896 | tf_op jit(solution)/shard_map/ppermute | solution.py:742
  117.1 15.9 %all-to-all-done = f32[32,48,128]{2,1,0:T(8,128)S(1)} async-done(((f32[32,48,128]{2,1,0:T(8,128)}), f32[32,48,128]{2,1,0:T(8,128)S(1)}, u32[]{:S(2)}, u32[]{:S(2)}) %all-to-all-start) | async-done | bytes 786464 | tf_op jit(solution)/shard_map/all_to_all | solution.py:994
  134.6 1.4 solve.1
  137.6 4.0 %all-to-all-start.1 = ((f32[32,32,128]{2,1,0:T(8,128)}), f32[32,32,128]{2,1,0:T(8,128)S(1)}, u32[]{:S(2)}, u32[]{:S(2)}) async-start(f32[32,32,128]{2,1,0:T(8,128)} %bitcast.18), calls=%async_computation.1 | async-start | bytes 1048576 | tf_op jit(solution)/shard_map/all_to_all | solution.py:1000
  141.6 3.5 %collective-permute-start.8 = (f32[3,6,128,128]{3,2,1,0:T(8,128)}, f32[3,6,128,128]{3,2,1,0:T(8,128)}, u32[]{:S(2)}, u32[]{:S(2)}) collective-permute-start(f32[3,6,128,128]{3,2,1,0:T(8,128)} %get-tuple-element.50), channel_id=1, source_target_pairs={{0,1},{1,2},{2,3},{4,5},{5,6},{6,7},{8,9},{9,10},{10,11},{12,13},{... | collective-permute-start | bytes 3538952 | tf_op jit(solution)/shard_map/ppermute | solution.py:742
  145.1 11.6 %all-to-all-done.1 = f32[32,32,128]{2,1,0:T(8,128)S(1)} async-done(((f32[32,32,128]{2,1,0:T(8,128)}), f32[32,32,128]{2,1,0:T(8,128)S(1)}, u32[]{:S(2)}, u32[]{:S(2)}) %all-to-all-start.1) | async-done | bytes 524320 | tf_op jit(solution)/shard_map/all_to_all | solution.py:1000
  156.8 3.4 %all-to-all-start.2 = ((f32[32,32,128]{2,1,0:T(8,128)}), f32[32,32,128]{2,1,0:T(8,128)S(1)}, u32[]{:S(2)}, u32[]{:S(2)}) async-start(f32[32,32,128]{2,1,0:T(8,128)} %bitcast.17), calls=%async_computation.2 | async-start | bytes 1048576 | tf_op jit(solution)/shard_map/all_to_all | solution.py:1000
  160.2 3.7 %collective-permute-start.7 = (f32[32,32,128]{2,1,0:T(8,128)S(1)}, f32[32,32,128]{2,1,0:T(8,128)}, u32[]{:S(2)}, u32[]{:S(2)}) collective-permute-start(f32[32,32,128]{2,1,0:T(8,128)S(1)} %all-to-all-done.1), channel_id=1, source_target_pairs={{0,1},{1,2},{2,3},{4,5},{5,6},{6,7},{8,9},{9,10},{10,11},{12,13},{... | collective-permute-start | bytes 1572872 | tf_op jit(solution)/shard_map/ppermute | solution.py:742
  164.9 0.9 copy-done.8
  168.5 5.6 %corrected_2.1 = (f32[3,3,16,128,128]{4,3,2,1,0:T(8,128)}, bf16[3,3,16,128,128]{4,3,2,1,0:T(8,128)(2,1)}) custom-call(f32[1024,128]{1,0:T(8,128)S(1)} %bitcast.14, bf16[384,256]{1,0:T(8,128)(2,1)S(1)} %copy-done, bf16[128,192]{1,0:T(8,128)(2,1)S(1)} %copy-done.19, f32[3,128,128]{2,1,0:T(8,128)S(1)} %copy-done.11, f32[3,128,128]{2,1,0:T(8,128)S(1)} %copy-done.6, ...), custom_call_target="tpu_custom_call" | custom-call | tf_op jit(solution)/shard_map/corrected_2/pallas_call | solution.py:760
  174.2 1.3 all-to-all-done.2
  175.4 0.9 copy-done.2
  177.3 5.6 %corrected_1.1 = (f32[3,3,16,128,128]{4,3,2,1,0:T(8,128)}, bf16[3,3,16,128,128]{4,3,2,1,0:T(8,128)(2,1)}) custom-call(f32[1024,128]{1,0:T(8,128)S(1)} %bitcast.15, bf16[384,256]{1,0:T(8,128)(2,1)S(1)} %copy-done, bf16[128,192]{1,0:T(8,128)(2,1)S(1)} %copy-done.19, f32[3,128,128]{2,1,0:T(8,128)S(1)} %copy-done.2, ...), custom_call_target="tpu_custom_call", output_to_operand_aliasing={{0}: (8, {}), {1}: (9, {})} | custom-call | tf_op jit(solution)/shard_map/corrected_1/pallas_call | solution.py:760
  182.9 8.0 %corrected_0.1 = (f32[3,3,16,128,128]{4,3,2,1,0:T(8,128)}, bf16[3,3,16,128,128]{4,3,2,1,0:T(8,128)(2,1)}) custom-call(f32[1]{0:T(128)} %bitcast.is_first.refs_0_, f32[1024,128]{1,0:T(8,128)} %bitcast.6.refs_1_, bf16[384,256]{1,0:T(8,128)(2,1)S(1)} %copy-done, bf16[128,192]{1,0:T(8,128)(2,1)S(1)} %copy-done.19, ...), custom_call_target="tpu_custom_call", output_to_operand_aliasing={{0}: (9, {}), {1}: (10, {})} | custom-call | tf_op jit(solution)/shard_map/corrected_0/pallas_call | solution.py:760
  (57 shorter events, 11.5 us)
Async XLA Ops:
  0.6 42.1 %copy-start.9 = (bf16[768,128]{1,0:T(8,128)(2,1)S(1)}, bf16[768,128]{1,0:T(8,128)(2,1)}, u32[]{:S(2)}) copy-start(bf16[768,128]{1,0:T(8,128)(2,1)} %constant.37.clone.z_table) | copy-start | bytes 589828
  0.6 42.1 %copy-start.22 = (bf16[64,192]{1,0:T(8,128)(2,1)S(1)}, bf16[64,192]{1,0:T(8,128)(2,1)}, u32[]{:S(2)}) copy-start(bf16[64,192]{1,0:T(8,128)(2,1)} %constant.38.clone.y_table) | copy-start | bytes 73732
  37.5 27.1 %collective-permute-start = (f32[9,128,128]{2,1,0:T(8,128)}, f32[9,128,128]{2,1,0:T(8,128)S(1)}, u32[]{:S(2)}, u32[]{:S(2)}) collective-permute-start(f32[9,128,128]{2,1,0:T(8,128)} %get-tuple-element.32), channel_id=1, source_target_pairs={{0,4},{4,8},{8,12},{12,16},{16,20},{20,24},{24,28},{28,0},{1,5},{5... | collective-permute-start | bytes 1769480 | tf_op jit(solution)/shard_map/ppermute | solution.py:737
  39.6 26.7 %collective-permute-start.1 = (f32[9,128,128]{2,1,0:T(8,128)}, f32[9,128,128]{2,1,0:T(8,128)S(1)}, u32[]{:S(2)}, u32[]{:S(2)}) collective-permute-start(f32[9,128,128]{2,1,0:T(8,128)} %get-tuple-element.33), channel_id=1, source_target_pairs={{4,0},{8,4},{12,8},{16,12},{20,16},{24,20},{28,24},{0,28},{5,1},{9... | collective-permute-start | bytes 1769480 | tf_op jit(solution)/shard_map/ppermute | solution.py:737
  58.9 0.9 copy-start.15
  59.8 9.2 %copy-start.14 = (f32[6,2,128,128]{3,2,1,0:T(8,128)}, f32[6,2,128,128]{3,2,1,0:T(8,128)S(1)}, u32[]{:S(2)}) copy-start(f32[6,2,128,128]{3,2,1,0:T(8,128)S(1)} %get-tuple-element.45.uv_next) | copy-start | bytes 2359300
  69.9 7.3 %collective-permute-start.2 = (f32[3,128,128]{2,1,0:T(8,128)S(1)}, f32[3,128,128]{2,1,0:T(8,128)S(1)}, u32[]{:S(2)}, u32[]{:S(2)}) collective-permute-start(f32[3,128,128]{2,1,0:T(8,128)S(1)} %get-tuple-element.35.high_end.refs_6_), channel_id=1, source_target_pairs={{0,4},{4,8},{8,12},{12,16},{16,20},{20,24},{24,28},{28,0},{1,5},{5... | collective-permute-start | bytes 589832 | tf_op jit(solution)/shard_map/ppermute | solution.py:737
  70.2 12.1 %collective-permute-start.3 = (f32[3,128,128]{2,1,0:T(8,128)S(1)}, f32[3,128,128]{2,1,0:T(8,128)S(1)}, u32[]{:S(2)}, u32[]{:S(2)}) collective-permute-start(f32[3,128,128]{2,1,0:T(8,128)S(1)} %get-tuple-element.36.low_end.refs_4_), channel_id=1, source_target_pairs={{4,0},{8,4},{12,8},{16,12},{20,16},{24,20},{28,24},{0,28},{5,1},{9... | collective-permute-start | bytes 589832 | tf_op jit(solution)/shard_map/ppermute | solution.py:737
  77.2 25.1 %copy-start.1 = (f32[3,128,128]{2,1,0:T(8,128)}, f32[3,128,128]{2,1,0:T(8,128)S(1)}, u32[]{:S(2)}) copy-start(f32[3,128,128]{2,1,0:T(8,128)S(1)} %collective-permute-done.2.low.refs_3_) | copy-start | bytes 589828
  82.3 20.0 %copy-start.3 = (f32[3,128,128]{2,1,0:T(8,128)}, f32[3,128,128]{2,1,0:T(8,128)S(1)}, u32[]{:S(2)}) copy-start(f32[3,128,128]{2,1,0:T(8,128)S(1)} %collective-permute-done.3.high.refs_7_) | copy-start | bytes 589828
  86.8 50.8 %copy-start.5 = (f32[3,128,128]{2,1,0:T(8,128)}, f32[3,128,128]{2,1,0:T(8,128)S(1)}, u32[]{:S(2)}) copy-start(f32[3,128,128]{2,1,0:T(8,128)S(1)} %get-tuple-element.42.low_end.refs_4_) | copy-start | bytes 589828
  86.8 50.8 %copy-start.7 = (f32[3,128,128]{2,1,0:T(8,128)}, f32[3,128,128]{2,1,0:T(8,128)S(1)}, u32[]{:S(2)}) copy-start(f32[3,128,128]{2,1,0:T(8,128)S(1)} %get-tuple-element.41.high_end.refs_7_) | copy-start | bytes 589828
  86.8 30.2 %copy-start.25 = (f32[64]{0:T(128)S(1)}, f32[64]{0:T(128)}, u32[]{:S(2)}) copy-start(f32[64]{0:T(128)} %constant.36.clone) | copy-start | bytes 772
  86.8 15.5 %collective-permute-start.6 = (f32[768,128]{1,0:T(8,128)S(1)}, f32[768,128]{1,0:T(8,128)S(1)}, u32[]{:S(2)}, u32[]{:S(2)}) collective-permute-start(f32[768,128]{1,0:T(8,128)S(1)} %get-tuple-element.47), channel_id=1, source_target_pairs={{0,1},{1,2},{2,3},{4,5},{5,6},{6,7},{8,9},{9,10},{10,11},{12,13},{... | collective-permute-start | bytes 1179656 | tf_op jit(solution)/shard_map/ppermute | solution.py:742
  91.1 8.3 %collective-permute-start.4 = (f32[3,128,128]{2,1,0:T(8,128)S(1)}, f32[3,128,128]{2,1,0:T(8,128)S(1)}, u32[]{:S(2)}, u32[]{:S(2)}) collective-permute-start(f32[3,128,128]{2,1,0:T(8,128)S(1)} %get-tuple-element.41.high_end.refs_7_), channel_id=1, source_target_pairs={{0,4},{4,8},{8,12},{12,16},{16,20},{20,24},{24,28},{28,0},{1,5},{5... | collective-permute-start | bytes 589832 | tf_op jit(solution)/shard_map/ppermute | solution.py:737
  91.2 11.1 %collective-permute-start.5 = (f32[3,128,128]{2,1,0:T(8,128)S(1)}, f32[3,128,128]{2,1,0:T(8,128)S(1)}, u32[]{:S(2)}, u32[]{:S(2)}) collective-permute-start(f32[3,128,128]{2,1,0:T(8,128)S(1)} %get-tuple-element.42.low_end.refs_4_), channel_id=1, source_target_pairs={{4,0},{8,4},{12,8},{16,12},{20,16},{24,20},{28,24},{0,28},{5,1},{9... | collective-permute-start | bytes 589832 | tf_op jit(solution)/shard_map/ppermute | solution.py:737
  99.4 10.1 %copy-start.10 = (f32[3,128,128]{2,1,0:T(8,128)}, f32[3,128,128]{2,1,0:T(8,128)S(1)}, u32[]{:S(2)}) copy-start(f32[3,128,128]{2,1,0:T(8,128)S(1)} %collective-permute-done.4.low.refs_3_) | copy-start | bytes 589828
  102.3 8.0 %copy-start.12 = (f32[3,128,128]{2,1,0:T(8,128)}, f32[3,128,128]{2,1,0:T(8,128)S(1)}, u32[]{:S(2)}) copy-start(f32[3,128,128]{2,1,0:T(8,128)S(1)} %collective-permute-done.5.high.refs_8_) | copy-start | bytes 589828
  102.3 1.2 copy-start.16
  103.5 60.4 %copy-start = (bf16[384,256]{1,0:T(8,128)(2,1)S(1)}, bf16[384,256]{1,0:T(8,128)(2,1)}, u32[]{:S(2)}) copy-start(bf16[384,256]{1,0:T(8,128)(2,1)} %constant.41.clone.refs_1_.refs_2_) | copy-start | bytes 589828
  110.4 22.7 %all-to-all-start = ((f32[32,48,128]{2,1,0:T(8,128)}), f32[32,48,128]{2,1,0:T(8,128)S(1)}, u32[]{:S(2)}, u32[]{:S(2)}) async-start(f32[32,48,128]{2,1,0:T(8,128)} %bitcast.16), calls=%async_computation | async-start | bytes 1572864 | tf_op jit(solution)/shard_map/all_to_all | solution.py:994
  112.7 70.1 %collective-permute-start.9 = (f32[3,12,128,128]{3,2,1,0:T(8,128)}, f32[3,12,128,128]{3,2,1,0:T(8,128)}, u32[]{:S(2)}, u32[]{:S(2)}) collective-permute-start(f32[3,12,128,128]{3,2,1,0:T(8,128)} %get-tuple-element.30.swept.refs_6_), channel_id=1, source_target_pairs={{0,1},{1,2},{2,3},{4,5},{5,6},{6,7},{8,9},{9,10},{10,11},{12,13},{... | collective-permute-start | bytes 7077896 | tf_op jit(solution)/shard_map/ppermute | solution.py:742
  137.6 19.2 %all-to-all-start.1 = ((f32[32,32,128]{2,1,0:T(8,128)}), f32[32,32,128]{2,1,0:T(8,128)S(1)}, u32[]{:S(2)}, u32[]{:S(2)}) async-start(f32[32,32,128]{2,1,0:T(8,128)} %bitcast.18), calls=%async_computation.1 | async-start | bytes 1048576 | tf_op jit(solution)/shard_map/all_to_all | solution.py:1000
  141.6 41.3 %collective-permute-start.8 = (f32[3,6,128,128]{3,2,1,0:T(8,128)}, f32[3,6,128,128]{3,2,1,0:T(8,128)}, u32[]{:S(2)}, u32[]{:S(2)}) collective-permute-start(f32[3,6,128,128]{3,2,1,0:T(8,128)} %get-tuple-element.50), channel_id=1, source_target_pairs={{0,1},{1,2},{2,3},{4,5},{5,6},{6,7},{8,9},{9,10},{10,11},{12,13},{... | collective-permute-start | bytes 3538952 | tf_op jit(solution)/shard_map/ppermute | solution.py:742
  156.8 18.6 %all-to-all-start.2 = ((f32[32,32,128]{2,1,0:T(8,128)}), f32[32,32,128]{2,1,0:T(8,128)S(1)}, u32[]{:S(2)}, u32[]{:S(2)}) async-start(f32[32,32,128]{2,1,0:T(8,128)} %bitcast.17), calls=%async_computation.2 | async-start | bytes 1048576 | tf_op jit(solution)/shard_map/all_to_all | solution.py:1000
  160.2 22.7 %collective-permute-start.7 = (f32[32,32,128]{2,1,0:T(8,128)S(1)}, f32[32,32,128]{2,1,0:T(8,128)}, u32[]{:S(2)}, u32[]{:S(2)}) collective-permute-start(f32[32,32,128]{2,1,0:T(8,128)S(1)} %all-to-all-done.1), channel_id=1, source_target_pairs={{0,1},{1,2},{2,3},{4,5},{5,6},{6,7},{8,9},{9,10},{10,11},{12,13},{... | collective-permute-start | bytes 1572872 | tf_op jit(solution)/shard_map/ppermute | solution.py:742
  164.0 0.9 copy-start.6
  164.9 0.9 copy-start.8
  165.8 0.9 copy-start.11
  166.8 0.9 copy-start.13
  175.4 0.9 copy-start.2
  176.4 0.9 copy-start.4
  (7 other events, 5.7 us)

commit v3 on v2

--- a/solution.py
+++ b/solution.py
@@ -20,7 +20,16 @@
 lanes = 128
 pad = 8
 rows_at_once = 32
-params = pltpu.CompilerParams(vmem_limit_bytes=50 * 1024 * 1024)
+
+
+def params(kibibytes):
+    return pltpu.CompilerParams(vmem_limit_bytes=kibibytes * 1024)
+
+
+def params_but(kibibytes):
+    return params(64 * 1024 - kibibytes)
+
+
 f32 = jnp.float32
 bf16 = jnp.bfloat16
 
@@ -91,6 +100,13 @@
     return jnp.dot(
         jnp.concatenate([high, high, low], axis=1), table, preferred_element_type=f32
     )
+
+
+def start_all(copies):
+    for copy in copies:
+        copy.start()
+    for copy in copies:
+        copy.wait()
 
 
 def wrap_rows(ref, plane, count):
@@ -287,8 +303,15 @@
 
 
 def solve_kernel(
-    peers, intervals, planes, group, back, values, inverse, forward, backward, out_1, out_2
+    peers, intervals, planes, group, back, values, inverse_in, table_in,
+    sent_1, sent_2, inverse, table, out_1, out_2, sems, out_sems
 ):
+    start_all([
+        pltpu.make_async_copy(table_in, table, sems.at[0]),
+        pltpu.make_async_copy(inverse_in, inverse, sems.at[1]),
+    ])
+    sending = []
+    rows_x = peers * planes
     start = [None] * 3
     for interval in range(intervals):
         loaded = []
@@ -300,7 +323,7 @@
                 for p in range(planes)
             ]
             loaded.append(jnp.concatenate(parts, axis=0))
-        spectra = left_dot(forward[...], jnp.concatenate(loaded, axis=1))
+        spectra = left_dot(table[:rows_x, :], jnp.concatenate(loaded, axis=1))
         rates = inverse[...]
         wanted = []
         for field in range(6):
@@ -310,7 +333,7 @@
                 value = value + start[c]
             start[c] = value * rates
             wanted.append(start[c])
-        physical = left_dot(backward[...], jnp.concatenate(wanted, axis=1))
+        physical = left_dot(table[rows_x:, :], jnp.concatenate(wanted, axis=1))
         for field in range(6):
             out = (out_1, out_2)[field // 3]
             base = (field % 3) * (planes + 2)
@@ -318,18 +341,22 @@
                 out[pl.ds(interval * back + base + e, peers, intervals * back), :] = physical[
                     e * peers : (e + 1) * peers, field * lanes : (field + 1) * lanes
                 ]
+        for peer in range(peers):
+            rows = pl.ds((peer * intervals + interval) * back, back)
+            for k, (out, sent) in enumerate(((out_1, sent_1), (out_2, sent_2))):
+                sem = out_sems.at[k, peer * intervals + interval]
+                sending.append(pltpu.make_async_copy(out.at[rows], sent.at[rows], sem))
+                sending[-1].start()
+    for copy in sending:
+        copy.wait()
 
 
 def edges_kernel(source, low, high, sems):
     length = source.shape[1]
-    copies = [
+    start_all([
         pltpu.make_async_copy(source.at[:, 0], low, sems.at[0]),
         pltpu.make_async_copy(source.at[:, length - 1], high, sems.at[1]),
-    ]
-    for copy in copies:
-        copy.start()
-    for copy in copies:
-        copy.wait()
+    ])
 
 
 def sweep_one_plane(is_first, held, slot, put_s1, put_w, uv, cell):
@@ -394,7 +421,7 @@
 
 def interior_kernel(
     group, g_group, is_first, source, z_table, y_table,
-    s1_out, s2_out, w_out, uv_end, uv_next, out, g,
+    near, s1_out, s2_out, w_out, uv_end, uv_next, out, g,
     held, held_1, held_2, w, uv, sems, out_sems
 ):
     length, size = source.shape[1], source.shape[2]
@@ -458,6 +485,10 @@
 
     lax.fori_loop(2, length - 2, phase_two, 0)
     tails = []
+    for k, plane in enumerate((0, 1, length - 2, length - 1)):
+        tails.append(
+            pltpu.make_async_copy(held.at[:, plane, rows_all, :], near.at[:, k], out_sems.at[2, 6 + k])
+        )
     for k, plane in enumerate((1, length - 2)):
         tails.append(pltpu.make_async_copy(w.at[:, plane], w_out.at[:, k], out_sems.at[2, k]))
     for k, cell in enumerate((0, planes - 1)):
@@ -499,24 +530,22 @@
         copy.wait()
 
 
-def start_all(copies):
-    for copy in copies:
-        copy.start()
-    for copy in copies:
-        copy.wait()
-
-
 def end_one_kernel(
-    is_first, source, low, high, uv_in, low_out, high_out, w_out, uv, held, sems
+    is_first, near, low, high, uv_in, pack, low_out, high_out, w_out, uv, held, sems, out_sems
 ):
-    length, size = source.shape[1], source.shape[2]
+    size = near.shape[2]
     rows_all = pl.ds(pad, size)
-    sources = [low, source.at[:, 0], source.at[:, 1]]
-    sources += [source.at[:, length - 2], source.at[:, length - 1], high]
+    sources = [low, *[near.at[:, k] for k in range(4)], high]
     start_all([
         pltpu.make_async_copy(ref, held.at[:, slot, rows_all, :], sems.at[slot])
         for slot, ref in enumerate(sources)
     ])
+    packing = [
+        pltpu.make_async_copy(held.at[0:3, slot, rows_all, :], pack.at[:, k], out_sems.at[k])
+        for k, slot in enumerate((0, 5))
+    ]
+    for copy in packing:
+        copy.start()
     uv[...] = uv_in[...]
     for k, (slot, ref) in enumerate(((1, low_out), (4, high_out))):
         wrap_rows(held, slot, 9)
@@ -528,23 +557,29 @@
             w_out[c, k, row : row + rows_at_once, :] = value
 
         sweep_one_plane(is_first, held, slot, put_s1, put_w, uv, k)
+    for copy in packing:
+        copy.wait()
 
 
 def end_two_kernel(
-    g_group, swept, low, low_end, high_end, high, w_end, w_next, uv_in, g_in, z_table, y_table,
-    low_out, high_out, next_out, uv, g, held, held_2, sems
+    g_group, swept, low, low_end, high_end, high, w_end, w_next, uv_in, z_table, y_table,
+    pack, low_out, high_out, next_out, uv, g, held, held_2, sems, out_sems
 ):
     count, size = swept.shape[1], swept.shape[2]
     rows_all = pl.ds(pad, size)
-    planes = (count + 2) // 2
     sources = [low, low_end, swept.at[:, 0], swept.at[:, 1]]
     sources += [swept.at[:, count - 2], swept.at[:, count - 1], high_end, high]
     start_all([
         pltpu.make_async_copy(ref, held.at[:, slot, rows_all, :], sems.at[slot])
         for slot, ref in enumerate(sources)
     ])
+    packing = [
+        pltpu.make_async_copy(held.at[:, slot, rows_all, :], pack.at[:, k], out_sems.at[k])
+        for k, slot in enumerate((0, 1, 6, 7))
+    ]
+    for copy in packing:
+        copy.start()
     uv[...] = uv_in[...]
-    g[...] = g_in[...]
     places = ((1, 0, w_end, 0), (2, 0, w_next, 0), (5, 1, w_next, 1), (6, 1, w_end, 1))
     for index, (slot, cell, w, k) in enumerate(places):
         wrap_rows(held, slot, 3)
@@ -567,12 +602,14 @@
     entries = [(c, k) for k in range(2) for c in range(3)]
     values = transform([held_halves(held_2, c, 2 * k) for c, k in entries], z_table, y_table)
     for (c, k), value in zip(entries, values):
-        g[pl.ds(c * planes + k * (planes - 1), blocks, g_group), :] = value
+        g[pl.ds(2 * c + k, blocks, g_group), :] = value
+    for copy in packing:
+        copy.wait()
 
 
 def end_three_kernel(
-    group, g_group, swept, low, low_end, nexts, high_end, high, uv_end, uv_next, f, g,
-    z_table, y_table, pack, out, held, uv, sems, out_sems
+    group, g_group, end_group, swept, low, low_end, nexts, high_end, high, uv_end, uv_next, f, g, g_end,
+    z_table, y_table, pack, sent, out, held, uv, sems, out_sems
 ):
     count, size = swept.shape[1], swept.shape[2]
     rows_all = pl.ds(pad, size)
@@ -604,33 +641,43 @@
         entries = [(k, index) for index in (2 * half, 2 * half + 1) for k in range(6)]
         values = transform([uv_halves(uv, k, index) for k, index in entries], z_table, y_table)
         for (k, index), value in zip(entries, values):
+            if k < 3:
+                if index % 3 == 0:
+                    value = value + g_end[pl.ds(2 * k + index // 3, blocks, end_group), :]
+                else:
+                    value = value + g[pl.ds(k * planes + cells[index], blocks, g_group), :]
             out[pl.ds(k * planes + cells[index], blocks, group), :] = value
-    for block in range(blocks):
-        out[block * group : block * group + 3 * planes, :] += g[
-            block * g_group : block * g_group + 3 * planes, :
-        ]
+    for k in range(3):
+        for cell in range(2, planes - 2):
+            out[pl.ds(k * planes + cell, blocks, group), :] += g[
+                pl.ds(k * planes + cell, blocks, g_group), :
+            ]
+    start_all([pltpu.make_async_copy(out, sent, out_sems.at[6])])
     for copy in packing:
         copy.wait()
 
 
-def corrected_kernel(node, group, layouts, counts, *refs):
+def stage_kernel(layouts, counts, *refs):
     if len(layouts) > 1:
         is_first, refs = refs[0], refs[1:]
-    spectra, z_table, y_table = refs[:3]
-    fields = refs[3 : 3 + counts]
-    new_velocity, new_rhs, held, coarse, result, sems, out_sems, rhs_sems = refs[-8:]
-    length, size = held.shape[1] - 2, held.shape[2] - 2 * pad
-    planes = length // 2
-    rows_all = pl.ds(pad, size)
+    fields, sems = refs[:counts], refs[-1]
+    extras = (len(refs) - counts - 2) // 2
+    staged = refs[counts + extras]
+    rest = [
+        pltpu.make_async_copy(refs[counts + k], refs[counts + extras + 1 + k], sems.at[k])
+        for k in range(extras)
+    ]
+    for copy in rest:
+        copy.start()
 
     def arriving(layout, slot):
         number, index = layout[slot]
         ref = fields[number]
         ref = ref.at[0:3, index] if index is not None else ref.at[0:3]
-        return pltpu.make_async_copy(ref, held.at[:, slot, rows_all, :], sems.at[slot])
+        return pltpu.make_async_copy(ref, staged.at[:, slot], sems.at[extras + slot])
 
     def launch(layout):
-        for slot in range(length + 2):
+        for slot in range(len(layout)):
             arriving(layout, slot).start()
 
     if len(layouts) > 1:
@@ -644,17 +691,28 @@
             launch(layouts[1])
     else:
         launch(layouts[0])
+    for slot in range(len(layouts[0])):
+        arriving(layouts[0], slot).wait()
+    for copy in rest:
+        copy.wait()
+
+
+def corrected_kernel(node, group, spectra, table, staged, *refs):
+    new_velocity, new_rhs, held, coarse, result, out_sems, rhs_sems = refs[-7:]
+    length, size = staged.shape[1] - 2, staged.shape[2]
+    planes = length // 2
+    rows_all = pl.ds(pad, size)
+    z_rows = 3 * lanes
+    y_rows, y_columns = size, 3 * size // 2
     blocks = spectra.shape[0] // group
     for c in range(3):
         base = c * (planes + 2)
         parts = [spectra[pl.ds(base + e, blocks, group), :] for e in range(planes + 2)]
-        in_z = right_dot(jnp.concatenate(parts, axis=0), z_table[...])
+        in_z = right_dot(jnp.concatenate(parts, axis=0), table[:z_rows, :])
         for e in range(planes + 2):
             mine = in_z[e * blocks : (e + 1) * blocks]
             stacked = jnp.concatenate([mine[:, :size], mine[:, size:]], axis=0)
-            coarse[c, e] = left_dot(y_table[...], stacked)
-    for slot in range(length + 2):
-        arriving(layouts[0], slot).wait()
+            coarse[c, e] = left_dot(table[z_rows : z_rows + y_rows, :y_columns], stacked)
 
     def out_copy(plane):
         return pltpu.make_async_copy(
@@ -674,7 +732,7 @@
                 value = coarse[field, cell, rows, :]
                 if odd:
                     value = 0.5 * (value + coarse[field, cell + 1, rows, :])
-                held[field, plane, held_rows, :] += value
+                held[field, plane, held_rows, :] = staged[field, plane, rows, :] + value
         wrap_rows(held, plane, 3)
 
     correct(0, 0, True)
@@ -712,6 +770,7 @@
 anywhere = pl.BlockSpec(memory_space=pl.ANY)
 scalar = pl.BlockSpec(memory_space=pltpu.SMEM)
 vmem = pl.BlockSpec(memory_space=pltpu.VMEM)
+hbm = pl.BlockSpec(memory_space=pltpu.HBM)
 
 
 def whole(shape):
@@ -742,36 +801,48 @@
     return lax.ppermute(value, "tm", [(i, i + 1) for i in range(count - 1)])
 
 
-def corrected(node, spectra, tables, fields, layouts, outs, is_first=None):
-    length = len(layouts[0]) - 2
+def stage(fields, layouts, is_first, extras=()):
     size_y, size_z = fields[0].shape[-2:]
+    slots = len(layouts[0])
+    operands, specs = [*fields, *extras], [anywhere] * (len(fields) + len(extras))
+    if len(layouts) > 1:
+        operands, specs = [is_first, *operands], [scalar, *specs]
+    return pl.pallas_call(
+        functools.partial(stage_kernel, layouts, len(fields)),
+        out_shape=(struct((3, slots, size_y, size_z)), *[struct(e.shape, e.dtype) for e in extras]),
+        in_specs=specs,
+        out_specs=(vmem,) * (1 + len(extras)),
+        scratch_shapes=[pltpu.SemaphoreType.DMA((slots + len(extras),))],
+        compiler_params=params(8192 if len(layouts) == 1 else 57344),
+        name="stage",
+    )(*operands)
+
+
+def corrected(node, spectra, table, staged, outs):
+    length = staged.shape[1] - 2
+    size_y, size_z = staged.shape[-2:]
     planes = length // 2
     group = spectra.shape[1]
-    operands = [spectra.reshape(-1, lanes), *tables]
-    specs = [whole(o.shape) for o in operands]
-    if is_first is not None:
-        operands, specs = [is_first, *operands], [scalar, *specs]
-    operands, specs = [*operands, *fields], specs + [anywhere] * len(fields)
+    operands, specs = [spectra.reshape(-1, lanes), table, staged], [vmem] * 3
     shape = (3, 3, length, size_y, size_z)
     aliases = {}
     if outs is not None:
-        aliases = {len(operands): 0, len(operands) + 1: 1}
-        operands, specs = [*operands, *outs], specs + [anywhere] * 2
+        aliases = {3: 0, 4: 1}
+        operands, specs = [*operands, *outs], specs + [hbm] * 2
     return pl.pallas_call(
-        functools.partial(corrected_kernel, node, group, layouts, len(fields)),
+        functools.partial(corrected_kernel, node, group),
         out_shape=(struct(shape), struct(shape, bf16)),
         in_specs=specs,
-        out_specs=(anywhere, anywhere),
+        out_specs=(hbm, hbm),
         input_output_aliases=aliases,
         scratch_shapes=[
             held_planes(3, length, size_y, size_z),
             pltpu.VMEM((3, planes + 2, size_y, size_z), f32),
             pltpu.VMEM((3, length, size_y, size_z), bf16),
-            pltpu.SemaphoreType.DMA((length + 2,)),
             pltpu.SemaphoreType.DMA((length,)),
             pltpu.SemaphoreType.DMA((length,)),
         ],
-        compiler_params=params,
+        compiler_params=params(16384),
         name=f"corrected_{node}",
     )(*operands)
 
@@ -792,7 +863,7 @@
         in_specs=[scalar, anywhere, anywhere, anywhere],
         out_specs=(slab(two), slab(two), slab(one), slab(one)),
         scratch_shapes=[held_planes(9, length, size_y, size_z), in_sems],
-        compiler_params=params,
+        compiler_params=params(40960),
         name="sweep_one",
     )(is_first, fields, low, high)
     low_1, high_1 = neighbours(swept_1[:, 0], swept_1[:, length - 1])
@@ -810,7 +881,7 @@
             pltpu.VMEM((3, size_y, size_z), f32),
             in_sems,
         ],
-        compiler_params=params,
+        compiler_params=params(40960),
         name="sweep_two",
     )(swept_1, low_1, high_1, w, u, v, z_table, y_table)
     low_2, high_2 = neighbours(swept_2[:, 0], swept_2[:, length - 1])
@@ -829,7 +900,7 @@
             pltpu.VMEM((6, size_y, size_z), f32),
             in_sems,
         ],
-        compiler_params=params,
+        compiler_params=params(40960),
         name="sources",
     )(swept_2, low_2, high_2, u, v, g, z_table, y_table)
     layout = tuple([(0, None)] + [(1, p) for p in range(length)] + [(2, None)])
@@ -857,15 +928,17 @@
     low, high = pl.pallas_call(
         edges_kernel,
         out_shape=(struct((9, *plane)),) * 2,
-        in_specs=[anywhere],
-        out_specs=(anywhere,) * 2,
+        in_specs=[hbm],
+        out_specs=(vmem,) * 2,
         scratch_shapes=[sems(2)],
+        compiler_params=params_but(300),
         name="edges",
     )(fields)
     low, high = neighbours(low, high)
-    swept_1, swept_2, w_next, uv_end, uv_next, f, g = pl.pallas_call(
+    near, swept_1, swept_2, w_next, uv_end, uv_next, f, g = pl.pallas_call(
         functools.partial(interior_kernel, group, g_group),
         out_shape=(
+            struct((9, 4, *plane)),
             struct((3, length - 2, *plane)),
             struct((3, length - 4, *plane)),
             struct((3, 2, *plane)),
@@ -874,8 +947,8 @@
             struct((blocks * group, lanes)),
             struct((blocks * g_group, lanes)),
         ),
-        in_specs=[scalar, anywhere, vmem, vmem],
-        out_specs=(anywhere,) * 5 + (vmem,) * 2,
+        in_specs=[scalar, hbm, vmem, vmem],
+        out_specs=(hbm,) * 6 + (vmem,) * 2,
         scratch_shapes=[
             held(9, length),
             held(3, length),
@@ -883,67 +956,77 @@
             pltpu.VMEM((3, length, *plane), f32),
             pltpu.VMEM((6, planes, *plane), f32),
             sems(length),
-            sems(3, max(length, 6)),
+            sems(3, max(length, 10)),
         ],
-        compiler_params=params,
+        compiler_params=params(40960),
         cost_estimate=pl.CostEstimate(flops=4 * 10**9, bytes_accessed=6 * 10**7, transcendentals=0),
         name="interior",
     )(is_first, fields, z_table, y_table)
-    low_end_1, high_end_1, w_end, uv_end = pl.pallas_call(
+    g_moved = later_interval(g)
+    pack_0, low_end_1, high_end_1, w_end, uv_end = pl.pallas_call(
         end_one_kernel,
         out_shape=(
+            struct((3, 2, *plane)),
             struct((3, *plane)),
             struct((3, *plane)),
             struct((3, 2, *plane)),
             struct((6, 2, *plane)),
         ),
         in_specs=[scalar, anywhere, anywhere, anywhere, vmem],
-        out_specs=(vmem,) * 4,
-        scratch_shapes=[held(9, 6), sems(6)],
-        compiler_params=params,
+        out_specs=(hbm,) + (vmem,) * 4,
+        scratch_shapes=[held(9, 6), sems(6), sems(2)],
+        compiler_params=params(16384),
         name="end_one",
-    )(is_first, fields, low, high, uv_end)
+    )(is_first, near, low, high, uv_end)
     low_1, high_1 = neighbours(low_end_1, high_end_1)
-    low_end_2, high_end_2, next_2, uv_end, g = pl.pallas_call(
-        functools.partial(end_two_kernel, g_group),
+    end_group = 8
+    pack_1, low_end_2, high_end_2, next_2, uv_end, g_end = pl.pallas_call(
+        functools.partial(end_two_kernel, end_group),
         out_shape=(
+            struct((3, 4, *plane)),
             struct((3, *plane)),
             struct((3, *plane)),
             struct((3, 2, *plane)),
             struct((6, 2, *plane)),
-            struct((blocks * g_group, lanes)),
+            struct((blocks * end_group, lanes)),
         ),
-        in_specs=[anywhere] * 5 + [vmem] * 6,
-        out_specs=(vmem,) * 5,
-        scratch_shapes=[held(3, 8), held(3, 4), sems(8)],
-        compiler_params=params,
+        in_specs=[hbm] + [anywhere] * 4 + [vmem] * 5,
+        out_specs=(hbm,) + (vmem,) * 5,
+        scratch_shapes=[held(3, 8), held(3, 4), sems(8), sems(4)],
+        compiler_params=params(16384),
         name="end_two",
-    )(swept_1, low_1, low_end_1, high_end_1, high_1, w_end, w_next, uv_end, g, z_table, y_table)
+    )(swept_1, low_1, low_end_1, high_end_1, high_1, w_end, w_next, uv_end, z_table, y_table)
     low_2, high_2 = neighbours(low_end_2, high_end_2)
     pack, sources = pl.pallas_call(
-        functools.partial(end_three_kernel, group, g_group),
+        functools.partial(end_three_kernel, group, g_group, end_group),
         out_shape=(struct((3, 6, *plane)), struct((blocks * group, lanes))),
-        in_specs=[anywhere] * 6 + [vmem] * 6,
-        out_specs=(anywhere, vmem),
-        scratch_shapes=[held(3, 12), pltpu.VMEM((6, 4, *plane), f32), sems(12), sems(6)],
-        compiler_params=params,
+        in_specs=[hbm] + [anywhere] * 5 + [vmem] * 7,
+        out_specs=(hbm, hbm),
+        scratch_shapes=[
+            pltpu.VMEM((blocks * group, lanes), f32),
+            held(3, 12),
+            pltpu.VMEM((6, 4, *plane), f32),
+            sems(12),
+            sems(7),
+        ],
+        compiler_params=params(16384),
         name="end_three",
     )(
         swept_2, low_2, low_end_2, next_2, high_end_2, high_2, uv_end, uv_next, f,
-        later_interval(g), z_table, y_table
+        g_moved, later_interval(g_end), z_table, y_table
     )
-    layout_1 = [(0, None), (1, None)] + [(2, p) for p in range(length - 2)] + [(3, None), (4, None)]
-    layout_2 = [(0, None), (1, None), (2, 0)] + [(3, p) for p in range(length - 4)]
-    layout_2 += [(2, 1), (4, None), (5, None)]
-    layout_0 = [(0, None)] + [(1, p) for p in range(length)] + [(2, None)]
-    later = [(3, 0), (3, 1), (3, 2)] + [(4, p) for p in range(length - 4)] + [(3, 3), (3, 4), (3, 5)]
+    inner_1 = [(1, p) for p in range(length - 2)]
+    inner_2 = [(1, p) for p in range(length - 4)]
+    layout_1 = [(0, 0), (0, 1)] + inner_1 + [(0, 2), (0, 3)]
+    layout_2 = [(0, 0), (0, 1), (0, 2)] + inner_2 + [(0, 3), (0, 4), (0, 5)]
+    layout_0 = [(2, 0)] + [(3, p) for p in range(length)] + [(2, 1)]
     return (
         sources,
-        ((low_1, low_end_1, swept_1, high_end_1, high_1), (tuple(layout_1),)),
-        ((low_2, low_end_2, next_2, swept_2, high_end_2, high_2), (tuple(layout_2),)),
+        ((pack_1, swept_1), (tuple(layout_1),)),
+        ((pack, swept_2), (tuple(layout_2),)),
         (
-            (low, fields, high, later_interval(pack), later_interval(swept_2)),
-            (tuple(layout_0), tuple(later)),
+            (later_interval(pack), later_interval(swept_2), pack_0, fields),
+            (tuple(layout_0), tuple(layout_2)),
         ),
     )
 
@@ -982,6 +1065,7 @@
 
     is_first = tm_first.astype(f32).reshape(1)
     sweep = sweep_split if length >= 10 else sweep_whole
+    carried_at = 1 if length >= 10 else 4
     sources, one, two, zero = sweep(fields, is_first, z_table, y_table, blocks)
     group = round_up(6 * planes, 8)
 
@@ -1003,19 +1087,40 @@
         return value.reshape(blocks, rows, lanes)
 
     back = round_up(3 * (planes + 2), 8)
+    x_table = np.concatenate([x_forward, x_backward], axis=0)
+    y_back_table = np.pad(y_back_table, ((0, 0), (0, z_back_table.shape[1] - y_back_table.shape[1])))
+    table = np.concatenate([z_back_table, y_back_table], axis=0)
     columned = to_columns(sources, group)
+    columned, moved = lax.optimization_barrier((columned, zero[0][carried_at]))
+    carried_fields = zero[0][:carried_at] + (moved,) + zero[0][carried_at + 1 :]
     solved_1, solved_2 = pl.pallas_call(
         functools.partial(solve_kernel, peers, intervals, planes, group, back),
         out_shape=(struct((devices * back, lanes)),) * 2,
-        compiler_params=params,
+        in_specs=[vmem, hbm, hbm],
+        out_specs=(hbm, hbm),
+        scratch_shapes=[
+            pltpu.VMEM(rates.shape, f32),
+            pltpu.VMEM(x_table.shape, bf16),
+            pltpu.VMEM((devices * back, lanes), f32),
+            pltpu.VMEM((devices * back, lanes), f32),
+            pltpu.SemaphoreType.DMA((2,)),
+            pltpu.SemaphoreType.DMA((2, devices)),
+        ],
+        compiler_params=params_but(790),
         name="solve",
-    )(columned, rates, x_forward, x_backward)
+    )(columned, rates, x_table)
+    fields_1, fields_2, solved_2, solved_1 = lax.optimization_barrier(
+        (one[0], two[0], solved_2, solved_1)
+    )
     spectra_2 = to_planes(solved_2, back)
+    staged_2, table = stage(fields_2, two[1], None, (jnp.asarray(table),))
+    (staged_1,) = stage(fields_1, one[1], None)
+    solved_1, staged_2, staged_1 = lax.optimization_barrier((solved_1, staged_2, staged_1))
     spectra_1 = to_planes(solved_1, back)
-    tables = (z_back_table, y_back_table)
-    outs = corrected(2, spectra_2, tables, *two, None)
-    outs = corrected(1, spectra_1, tables, *one, outs)
-    new_velocity, new_rhs = corrected(0, later_interval(spectra_2), tables, *zero, outs, is_first)
+    (staged_0,) = stage(carried_fields, zero[1], is_first)
+    outs = corrected(2, spectra_2, table, staged_2, None)
+    outs = corrected(0, later_interval(spectra_2), table, staged_0, outs)
+    new_velocity, new_rhs = corrected(1, spectra_1, table, staged_1, outs)
     return (new_velocity[None], new_rhs[None])
 
 

time: 192 us -> 147 us (0.77)
  Pallas kernels: 86.7 us -> 59.6 us
  waiting for transfers between devices: 50.7 us -> 28.3 us
  starting transfers between devices: 38.5 us -> 46.7 us
  local copies, waits for them, and re-layouts: 14.1 us -> 10 us
    pallas_call x1, Pallas kernels: 36.9 us -> 2.33 us  [sweep_split(): pl.pallas_call(edges_kernel, out_shape=(struct((9, *plane)),) * 2, in_spe...]
    ppermute x3, waiting for transfers between devices: 12 us -> 0.01 us  [neighbours(): lax.ppermute(high_plane, 'space', up)]
    all_to_all x2, waiting for transfers between devices: 12.9 us -> 2.54 us  [to_planes(): value = lax.all_to_all(value, both, split_axis=0, concat_axis=0, tiled=True)]
    ppermute x4 -> x5, starting transfers between devices: 15.1 us -> 21.4 us  [later_interval(): return lax.ppermute(value, 'tm', [(i, i + 1) for i in range(count - 1)])]
    ppermute x3, waiting for transfers between devices: 9.83 us -> 4.17 us  [neighbours(): lax.ppermute(low_plane, 'space', down)]
    unnamed x52 -> x38, local copies, waits for them, and re-layouts: 13.4 us -> 9.31 us
    pallas_call x1, Pallas kernels: 1.42 us -> 4.75 us  [per_device(): pl.pallas_call(functools.partial(solve_kernel, peers, intervals, planes,...]
    all_to_all x1, waiting for transfers between devices: 15.9 us -> 18.9 us  [to_columns(): value = lax.all_to_all(value, both, split_axis=0, concat_axis=0, tiled=True)]
  transfers between devices with their start and end apart: 13 -> 14, of which waited for: 9 -> 7; matrix products, arithmetic and copies ran while one was open for 0% -> 1% of each run, Pallas kernels for 15% -> 32%
where the time goes in v3:
time: 147 us; the launch traced here: 146 us
  Pallas kernels  59.6 us (41%)
  starting transfers between devices  46.7 us (32%)
  waiting for transfers between devices  28.3 us (19%)
  local copies, waits for them, and re-layouts  10 us (7%)
    ppermute x5, starting transfers between devices, later_interval(): return lax.ppermute(value, 'tm', [(i, i + 1) for i in range(count - 1)])  21.4 us
    all_to_all x1, waiting for transfers between devices, to_columns(): value = lax.all_to_all(value, both, split_axis=0, concat_axis=0, tiled=True)  18.9 us
    pallas_call x1, Pallas kernels, sweep_split(): pl.pallas_call(functools.partial(interior_kernel, group, g_group), out_sh...  18.6 us
    pallas_call x3, Pallas kernels, corrected(): pl.pallas_call(functools.partial(corrected_kernel, node, group), out_shap...  16.9 us
    ppermute x3, starting transfers between devices, neighbours(): lax.ppermute(low_plane, 'space', down)  11.2 us
    unnamed x38, local copies, waits for them, and re-layouts  9.31 us
    pallas_call x3, Pallas kernels, stage(): pl.pallas_call(functools.partial(stage_kernel, layouts, len(fields)), out...  7.56 us
    all_to_all x2, starting transfers between devices, to_planes(): value = lax.all_to_all(value, both, split_axis=0, concat_axis=0, tiled=True)  7.53 us
  transfers between devices with their start and end apart: 14, of which 7 were waited for; matrix products, arithmetic and copies ran while one was open for 1% of the time, Pallas kernels for 32%

profile of v3, /device:TPU:1, one launch (start us, length us, event | category | flops | bytes accessed | tf_op | source)
XLA Modules:
  0.0 146.5 jit_solution(1891395611935240220)
XLA Ops:
  0.7 2.3 %edges.1 = (f32[9,128,128]{2,1,0:T(8,128)}, f32[9,128,128]{2,1,0:T(8,128)}) custom-call(f32[9,16,128,128]{3,2,1,0:T(8,128)} %bitcast.14), custom_call_target="tpu_custom_call" | custom-call | tf_op jit(solution)/shard_map/edges/pallas_call | solution.py:928
  3.0 2.1 %collective-permute-start = (f32[9,128,128]{2,1,0:T(8,128)}, f32[9,128,128]{2,1,0:T(8,128)S(1)}, u32[]{:S(2)}, u32[]{:S(2)}) collective-permute-start(f32[9,128,128]{2,1,0:T(8,128)} %get-tuple-element.48), channel_id=1, source_target_pairs={{0,4},{4,8},{8,12},{12,16},{16,20},{20,24},{24,28},{28,0},{1,5},{5... | collective-permute-start | bytes 1769480 | tf_op jit(solution)/shard_map/ppermute | solution.py:796
  5.1 3.1 %collective-permute-start.1 = (f32[9,128,128]{2,1,0:T(8,128)}, f32[9,128,128]{2,1,0:T(8,128)}, u32[]{:S(2)}, u32[]{:S(2)}) collective-permute-start(f32[9,128,128]{2,1,0:T(8,128)} %get-tuple-element.49), channel_id=1, source_target_pairs={{4,0},{8,4},{12,8},{16,12},{20,16},{24,20},{28,24},{0,28},{5,1},{9... | collective-permute-start | bytes 1769480 | tf_op jit(solution)/shard_map/ppermute | solution.py:796
  8.2 18.6 %interior.1 = (f32[9,4,128,128]{3,2,1,0:T(8,128)S(1)}, f32[3,14,128,128]{3,2,1,0:T(8,128)S(1)}, f32[3,12,128,128]{3,2,1,0:T(8,128)S(1)}, f32[3,2,128,128]{3,2,1,...) custom-call(f32[1]{0:T(128)} %bitcast.is_first.refs_0_, ...), custom_call_target="tpu_custom_call" | custom-call | flops 4000000000 | bytes 60000000 | tf_op jit(solution)/shard_map/interior/pallas_call | solution.py:938
  26.8 4.1 %collective-permute-start.8 = (f32[3,12,128,128]{3,2,1,0:T(8,128)S(1)}, f32[3,12,128,128]{3,2,1,0:T(8,128)}, u32[]{:S(2)}, u32[]{:S(2)}) collective-permute-start(f32[3,12,128,128]{3,2,1,0:T(8,128)S(1)} %get-tuple-element.73.swept.refs_1_), channel_id=1, source_target_pairs={{0,1},{1,2},{2,3},{4,5},{5,6},{6,7},{8,9},{9,10},{10,11},{12,13},{... | collective-permute-start | bytes 7077896 | tf_op jit(solution)/shard_map/ppermute | solution.py:801
  32.0 2.5 %end_one.1 = (f32[3,2,128,128]{3,2,1,0:T(8,128)S(1)}, f32[3,128,128]{2,1,0:T(8,128)S(1)}, f32[3,128,128]{2,1,0:T(8,128)S(1)}, f32[3,2,128,128]{3,2,1,0:T(8,128)S(1)}, f32[6,2,128,128]{3,2,1,0:T(8,128)S(1)}) custom-call(f32[1]{0:T(128)} %bitcast.is_first.refs_0_, f32[9,4,128,128]{3,2,1,0:T(8,128)S(1)} %get-tuple-element.47.near, ...), custom_call_target="tpu_custom_call" | custom-call | tf_op jit(solution)/shard_map/end_one/pallas_call | solution.py:966
  35.4 3.9 %collective-permute-start.3 = (f32[3,128,128]{2,1,0:T(8,128)S(1)}, f32[3,128,128]{2,1,0:T(8,128)S(1)}, u32[]{:S(2)}, u32[]{:S(2)}) collective-permute-start(f32[3,128,128]{2,1,0:T(8,128)S(1)} %get-tuple-element.52.low_end), channel_id=1, source_target_pairs={{4,0},{8,4},{12,8},{16,12},{20,16},{24,20},{28,24},{0,28},{5,1},{9... | collective-permute-start | bytes 589832 | tf_op jit(solution)/shard_map/ppermute | solution.py:796
  39.3 5.4 %collective-permute-start.6 = (f32[768,128]{1,0:T(8,128)S(1)}, f32[768,128]{1,0:T(8,128)S(1)}, u32[]{:S(2)}, u32[]{:S(2)}) collective-permute-start(f32[768,128]{1,0:T(8,128)S(1)} %get-tuple-element.64), channel_id=1, source_target_pairs={{0,1},{1,2},{2,3},{4,5},{5,6},{6,7},{8,9},{9,10},{10,11},{12,13},{... | collective-permute-start | bytes 1179656 | tf_op jit(solution)/shard_map/ppermute | solution.py:801
  44.8 2.8 %collective-permute-done.3.high = f32[3,128,128]{2,1,0:T(8,128)S(1)} collective-permute-done((f32[3,128,128]{2,1,0:T(8,128)S(1)}, f32[3,128,128]{2,1,0:T(8,128)S(1)}, u32[]{:S(2)}, u32[]{:S(2)}) %collective-permute-start.3) | collective-permute-done | bytes 196640 | tf_op jit(solution)/shard_map/ppermute | solution.py:796
  47.6 2.3 %end_two.1 = (f32[3,4,128,128]{3,2,1,0:T(8,128)S(1)}, f32[3,128,128]{2,1,0:T(8,128)S(1)}, f32[3,128,128]{2,1,0:T(8,128)S(1)}, f32[3,2,128,128]{3,2,1,0:T(8,128)S...) custom-call(f32[3,14,128,128]{3,2,1,0:T(8,128)S(1)} %get-tuple-element.76.swept.refs_1_, ...), custom_call_target="tpu_custom_call" | custom-call | tf_op jit(solution)/shard_map/end_two/pallas_call | solution.py:983
  50.8 4.2 %collective-permute-start.5 = (f32[3,128,128]{2,1,0:T(8,128)S(1)}, f32[3,128,128]{2,1,0:T(8,128)S(1)}, u32[]{:S(2)}, u32[]{:S(2)}) collective-permute-start(f32[3,128,128]{2,1,0:T(8,128)S(1)} %get-tuple-element.59.low_end), channel_id=1, source_target_pairs={{4,0},{8,4},{12,8},{16,12},{20,16},{24,20},{28,24},{0,28},{5,1},{9... | collective-permute-start | bytes 589832 | tf_op jit(solution)/shard_map/ppermute | solution.py:796
  55.0 4.7 %collective-permute-start.7 = (f32[256,128]{1,0:T(8,128)S(1)}, f32[256,128]{1,0:T(8,128)S(1)}, u32[]{:S(2)}, u32[]{:S(2)}) collective-permute-start(f32[256,128]{1,0:T(8,128)S(1)} %get-tuple-element.65), channel_id=1, source_target_pairs={{0,1},{1,2},{2,3},{4,5},{5,6},{6,7},{8,9},{9,10},{10,11},{12,13},{... | collective-permute-start | bytes 393224 | tf_op jit(solution)/shard_map/ppermute | solution.py:801
  59.6 1.2 collective-permute-done.6.g
  60.9 1.4 collective-permute-done.7.g_end
  62.5 4.8 %end_three.1 = (f32[3,6,128,128]{3,2,1,0:T(8,128)S(1)}, f32[1536,128]{1,0:T(8,128)}) custom-call(f32[3,12,128,128]{3,2,1,0:T(8,128)S(1)} %get-tuple-element.73.swept.refs_1_, f32[3,128,128]{2,1,0:T(8,128)S(1)} %collective-permute-done.4.low, f32[3,128,128]{2,1,0:T(8,128)S(1)} %get-tuple-element.59.low_end, f32[3,2,128,128]{3,2,1,0:T(8,128)S(1)} %get-tuple-element.60.nexts, ...), custom_call_target="tpu_custom_call" | custom-call | tf_op jit(solution)/shard_map/end_three/pallas_call | solution.py:1000
  68.4 4.2 %all-to-all-start = ((f32[32,48,128]{2,1,0:T(8,128)}), f32[32,48,128]{2,1,0:T(8,128)}, u32[]{:S(2)}, u32[]{:S(2)}) async-start(f32[32,48,128]{2,1,0:T(8,128)} %bitcast.2), calls=%async_computation | async-start | bytes 1572864 | tf_op jit(solution)/shard_map/all_to_all | solution.py:1078
  74.0 18.9 %all-to-all-done = f32[32,48,128]{2,1,0:T(8,128)} async-done(((f32[32,48,128]{2,1,0:T(8,128)}), f32[32,48,128]{2,1,0:T(8,128)}, u32[]{:S(2)}, u32[]{:S(2)}) %all-to-all-start) | async-done | bytes 786464 | tf_op jit(solution)/shard_map/all_to_all | solution.py:1078
  92.9 4.7 %solve.1 = (f32[1024,128]{1,0:T(8,128)}, f32[1024,128]{1,0:T(8,128)}) custom-call(f32[1536,128]{1,0:T(8,128)} %bitcast.3.values, f32[64,128]{1,0:T(8,128)} %add_divide_fusion.inverse_in, bf16[144,192]{1,0:T(8,128)(2,1)} %constant.35.clone.table_in), custom_call_target="tpu_custom_call" | custom-call | tf_op jit(solution)/shard_map/solve/pallas_call | solution.py:1096
  97.7 4.1 %all-to-all-start.2 = ((f32[32,32,128]{2,1,0:T(8,128)}), f32[32,32,128]{2,1,0:T(8,128)}, u32[]{:S(2)}, u32[]{:S(2)}) async-start(f32[32,32,128]{2,1,0:T(8,128)} %bitcast.20), calls=%async_computation.2 | async-start | bytes 1048576 | tf_op jit(solution)/shard_map/all_to_all | solution.py:1084
  101.7 3.5 %collective-permute-start.10 = (f32[3,6,128,128]{3,2,1,0:T(8,128)}, f32[3,6,128,128]{3,2,1,0:T(8,128)}, u32[]{:S(2)}, u32[]{:S(2)}) collective-permute-start(f32[3,6,128,128]{3,2,1,0:T(8,128)} %copy-done.10), channel_id=1, source_target_pairs={{0,1},{1,2},{2,3},{4,5},{5,6},{6,7},{8,9},{9,10},{10,11},{12,13},{... | collective-permute-start | bytes 3538952 | tf_op jit(solution)/shard_map/ppermute | solution.py:801
  105.3 1.8 %copy-done.2 = f32[3,14,128,128]{3,2,1,0:T(8,128)S(1)} copy-done((f32[3,14,128,128]{3,2,1,0:T(8,128)S(1)}, f32[3,14,128,128]{3,2,1,0:T(8,128)}, u32[]{:S(2)}) %copy-start.2) | copy-done | bytes 2752536
  107.1 1.1 copy-done.13
  108.2 1.7 %stage.4.staged = f32[3,18,128,128]{3,2,1,0:T(8,128)S(1)} custom-call(f32[3,4,128,128]{3,2,1,0:T(8,128)S(1)} %copy-done.13, f32[3,14,128,128]{3,2,1,0:T(8,128)S(1)} %copy-done.2), custom_call_target="tpu_custom_call" | custom-call | tf_op jit(solution)/shard_map/stage/pallas_call | solution.py:810
  110.2 1.7 %stage.3 = (f32[3,18,128,128]{3,2,1,0:T(8,128)S(1)}, bf16[512,256]{1,0:T(8,128)(2,1)S(1)}) custom-call(f32[3,6,128,128]{3,2,1,0:T(8,128)S(1)} %copy-done.11, f32[3,12,128,128]{3,2,1,0:T(8,128)S(1)} %copy-done.4, bf16[512,256]{1,0:T(8,128)(2,1)S(1)} %copy-done.16), custom_call_target="tpu_custom_call" | custom-call | tf_op jit(solution)/shard_map/stage/pallas_call | solution.py:810
  112.0 1.8 %copy-done.5 = f32[3,18,128,128]{3,2,1,0:T(8,128)} copy-done((f32[3,18,128,128]{3,2,1,0:T(8,128)}, f32[3,18,128,128]{3,2,1,0:T(8,128)S(1)}, u32[]{:S(2)}) %copy-start.5) | copy-done | bytes 3538968
  114.5 2.5 %all-to-all-done.2 = f32[32,32,128]{2,1,0:T(8,128)} async-done(((f32[32,32,128]{2,1,0:T(8,128)}), f32[32,32,128]{2,1,0:T(8,128)}, u32[]{:S(2)}, u32[]{:S(2)}) %all-to-all-start.2) | async-done | bytes 524320 | tf_op jit(solution)/shard_map/all_to_all | solution.py:1084
  117.0 3.5 %all-to-all-start.1 = ((f32[32,32,128]{2,1,0:T(8,128)}), f32[32,32,128]{2,1,0:T(8,128)}, u32[]{:S(2)}, u32[]{:S(2)}) async-start(f32[32,32,128]{2,1,0:T(8,128)} %bitcast.19), calls=%async_computation.1 | async-start | bytes 1048576 | tf_op jit(solution)/shard_map/all_to_all | solution.py:1084
  120.5 3.7 %collective-permute-start.9 = (f32[32,32,128]{2,1,0:T(8,128)}, f32[32,32,128]{2,1,0:T(8,128)S(1)}, u32[]{:S(2)}, u32[]{:S(2)}) collective-permute-start(f32[32,32,128]{2,1,0:T(8,128)} %all-to-all-done.2), channel_id=1, source_target_pairs={{0,1},{1,2},{2,3},{4,5},{5,6},{6,7},{8,9},{9,10},{10,11},{12,13},{... | collective-permute-start | bytes 1572872 | tf_op jit(solution)/shard_map/ppermute | solution.py:801
  124.2 4.1 %stage.5.staged = f32[3,18,128,128]{3,2,1,0:T(8,128)} custom-call(f32[1]{0:T(128)} %bitcast.is_first.refs_0_, f32[3,6,128,128]{3,2,1,0:T(8,128)} %collective-permute-done.10.refs_1_, f32[3,12,128,128]{3,2,1,0:T(8,128)} %collective-permute-done.8.refs_2_, f32[3,2,128,128]{3,2,1,0:T(8,128)} %copy-done.15, f32[9,16,128,128]{3,2,1,0:T(8,128)} %bitcast.16), custom_call_target="tpu_custom_call" | custom-call | tf_op jit(solution)/shard_map/stage/pallas_call | solution.py:810
  128.4 6.1 %corrected_2.1 = (f32[3,3,16,128,128]{4,3,2,1,0:T(8,128)}, bf16[3,3,16,128,128]{4,3,2,1,0:T(8,128)(2,1)}) custom-call(f32[1024,128]{1,0:T(8,128)} %bitcast.9.spectra, bf16[512,256]{1,0:T(8,128)(2,1)S(1)} %copy-done.8, f32[3,18,128,128]{3,2,1,0:T(8,128)S(1)} %copy-done.6), custom_call_target="tpu_custom_call" | custom-call | tf_op jit(solution)/shard_map/corrected_2/pallas_call | solution.py:832
  134.5 4.9 %corrected_0.1 = (f32[3,3,16,128,128]{4,3,2,1,0:T(8,128)}, bf16[3,3,16,128,128]{4,3,2,1,0:T(8,128)(2,1)}) custom-call(f32[1024,128]{1,0:T(8,128)S(1)} %bitcast.13, bf16[512,256]{1,0:T(8,128)(2,1)S(1)} %copy-done.8, f32[3,18,128,128]{3,2,1,0:T(8,128)S(1)} %copy-done, ...), custom_call_target="tpu_custom_call", output_to_operand_aliasing={{0}: (3, {}), {1}: (4, {})} | custom-call | tf_op jit(solution)/shard_map/corrected_0/pallas_call | solution.py:832
  140.4 5.9 %corrected_1.1 = (f32[3,3,16,128,128]{4,3,2,1,0:T(8,128)}, bf16[3,3,16,128,128]{4,3,2,1,0:T(8,128)(2,1)}) custom-call(f32[1024,128]{1,0:T(8,128)} %bitcast.6.spectra, bf16[512,256]{1,0:T(8,128)(2,1)S(1)} %copy-done.9, f32[3,18,128,128]{3,2,1,0:T(8,128)S(1)} %stage.4.staged, ...), custom_call_target="tpu_custom_call", output_to_operand_aliasing={{0}: (3, {}), {1}: (4, {})} | custom-call | tf_op jit(solution)/shard_map/corrected_1/pallas_call | solution.py:832
  (48 shorter events, 7.6 us)
Async XLA Ops:
  0.6 7.6 %copy-start.14 = (bf16[768,128]{1,0:T(8,128)(2,1)S(1)}, bf16[768,128]{1,0:T(8,128)(2,1)}, u32[]{:S(2)}) copy-start(bf16[768,128]{1,0:T(8,128)(2,1)} %constant.33.clone.z_table) | copy-start | bytes 589828
  0.6 7.6 %copy-start.17 = (bf16[64,192]{1,0:T(8,128)(2,1)S(1)}, bf16[64,192]{1,0:T(8,128)(2,1)}, u32[]{:S(2)}) copy-start(bf16[64,192]{1,0:T(8,128)(2,1)} %constant.34.clone.y_table) | copy-start | bytes 73732
  3.0 27.9 %collective-permute-start = (f32[9,128,128]{2,1,0:T(8,128)}, f32[9,128,128]{2,1,0:T(8,128)S(1)}, u32[]{:S(2)}, u32[]{:S(2)}) collective-permute-start(f32[9,128,128]{2,1,0:T(8,128)} %get-tuple-element.48), channel_id=1, source_target_pairs={{0,4},{4,8},{8,12},{12,16},{16,20},{20,24},{24,28},{28,0},{1,5},{5... | collective-permute-start | bytes 1769480 | tf_op jit(solution)/shard_map/ppermute | solution.py:796
  5.1 26.8 %collective-permute-start.1 = (f32[9,128,128]{2,1,0:T(8,128)}, f32[9,128,128]{2,1,0:T(8,128)}, u32[]{:S(2)}, u32[]{:S(2)}) collective-permute-start(f32[9,128,128]{2,1,0:T(8,128)} %get-tuple-element.49), channel_id=1, source_target_pairs={{4,0},{8,4},{12,8},{16,12},{20,16},{24,20},{28,24},{0,28},{5,1},{9... | collective-permute-start | bytes 1769480 | tf_op jit(solution)/shard_map/ppermute | solution.py:796
  26.8 23.1 %copy-start.1 = (f32[3,14,128,128]{3,2,1,0:T(8,128)}, f32[3,14,128,128]{3,2,1,0:T(8,128)S(1)}, u32[]{:S(2)}) copy-start(f32[3,14,128,128]{3,2,1,0:T(8,128)S(1)} %get-tuple-element.76.swept.refs_1_) | copy-start | bytes 8257540
  26.8 35.7 %copy-start.3 = (f32[3,12,128,128]{3,2,1,0:T(8,128)}, f32[3,12,128,128]{3,2,1,0:T(8,128)S(1)}, u32[]{:S(2)}) copy-start(f32[3,12,128,128]{3,2,1,0:T(8,128)S(1)} %get-tuple-element.73.swept.refs_1_) | copy-start | bytes 7077892
  26.8 47.2 %collective-permute-start.8 = (f32[3,12,128,128]{3,2,1,0:T(8,128)S(1)}, f32[3,12,128,128]{3,2,1,0:T(8,128)}, u32[]{:S(2)}, u32[]{:S(2)}) collective-permute-start(f32[3,12,128,128]{3,2,1,0:T(8,128)S(1)} %get-tuple-element.73.swept.refs_1_), channel_id=1, source_target_pairs={{0,1},{1,2},{2,3},{4,5},{5,6},{6,7},{8,9},{9,10},{10,11},{12,13},{... | collective-permute-start | bytes 7077896 | tf_op jit(solution)/shard_map/ppermute | solution.py:801
  34.4 0.8 copy-start.15
  35.2 9.6 %collective-permute-start.2 = (f32[3,128,128]{2,1,0:T(8,128)S(1)}, f32[3,128,128]{2,1,0:T(8,128)S(1)}, u32[]{:S(2)}, u32[]{:S(2)}) collective-permute-start(f32[3,128,128]{2,1,0:T(8,128)S(1)} %get-tuple-element.51.high_end), channel_id=1, source_target_pairs={{0,4},{4,8},{8,12},{12,16},{16,20},{20,24},{24,28},{28,0},{1,5},{5... | collective-permute-start | bytes 589832 | tf_op jit(solution)/shard_map/ppermute | solution.py:796
  35.4 12.2 %collective-permute-start.3 = (f32[3,128,128]{2,1,0:T(8,128)S(1)}, f32[3,128,128]{2,1,0:T(8,128)S(1)}, u32[]{:S(2)}, u32[]{:S(2)}) collective-permute-start(f32[3,128,128]{2,1,0:T(8,128)S(1)} %get-tuple-element.52.low_end), channel_id=1, source_target_pairs={{4,0},{8,4},{12,8},{16,12},{20,16},{24,20},{28,24},{0,28},{5,1},{9... | collective-permute-start | bytes 589832 | tf_op jit(solution)/shard_map/ppermute | solution.py:796
  39.3 21.5 %collective-permute-start.6 = (f32[768,128]{1,0:T(8,128)S(1)}, f32[768,128]{1,0:T(8,128)S(1)}, u32[]{:S(2)}, u32[]{:S(2)}) collective-permute-start(f32[768,128]{1,0:T(8,128)S(1)} %get-tuple-element.64), channel_id=1, source_target_pairs={{0,1},{1,2},{2,3},{4,5},{5,6},{6,7},{8,9},{9,10},{10,11},{12,13},{... | collective-permute-start | bytes 1179656 | tf_op jit(solution)/shard_map/ppermute | solution.py:801
  49.9 0.9 copy-start.12
  50.8 11.5 %collective-permute-start.4 = (f32[3,128,128]{2,1,0:T(8,128)S(1)}, f32[3,128,128]{2,1,0:T(8,128)S(1)}, u32[]{:S(2)}, u32[]{:S(2)}) collective-permute-start(f32[3,128,128]{2,1,0:T(8,128)S(1)} %get-tuple-element.58.high_end), channel_id=1, source_target_pairs={{0,4},{4,8},{8,12},{12,16},{16,20},{20,24},{24,28},{28,0},{1,5},{5... | collective-permute-start | bytes 589832 | tf_op jit(solution)/shard_map/ppermute | solution.py:796
  50.8 11.7 %collective-permute-start.5 = (f32[3,128,128]{2,1,0:T(8,128)S(1)}, f32[3,128,128]{2,1,0:T(8,128)S(1)}, u32[]{:S(2)}, u32[]{:S(2)}) collective-permute-start(f32[3,128,128]{2,1,0:T(8,128)S(1)} %get-tuple-element.59.low_end), channel_id=1, source_target_pairs={{4,0},{8,4},{12,8},{16,12},{20,16},{24,20},{28,24},{0,28},{5,1},{9... | collective-permute-start | bytes 589832 | tf_op jit(solution)/shard_map/ppermute | solution.py:796
  55.0 7.3 %collective-permute-start.7 = (f32[256,128]{1,0:T(8,128)S(1)}, f32[256,128]{1,0:T(8,128)S(1)}, u32[]{:S(2)}, u32[]{:S(2)}) collective-permute-start(f32[256,128]{1,0:T(8,128)S(1)} %get-tuple-element.65), channel_id=1, source_target_pairs={{0,1},{1,2},{2,3},{4,5},{5,6},{6,7},{8,9},{9,10},{10,11},{12,13},{... | collective-permute-start | bytes 393224 | tf_op jit(solution)/shard_map/ppermute | solution.py:801
  62.5 10.8 %copy-start.18 = (f32[64]{0:T(128)S(1)}, f32[64]{0:T(128)}, u32[]{:S(2)}) copy-start(f32[64]{0:T(128)} %constant.32.clone) | copy-start | bytes 772
  67.3 1.0 copy-start.10
  68.4 24.6 %all-to-all-start = ((f32[32,48,128]{2,1,0:T(8,128)}), f32[32,48,128]{2,1,0:T(8,128)}, u32[]{:S(2)}, u32[]{:S(2)}) async-start(f32[32,48,128]{2,1,0:T(8,128)} %bitcast.2), calls=%async_computation | async-start | bytes 1572864 | tf_op jit(solution)/shard_map/all_to_all | solution.py:1078
  97.7 19.3 %all-to-all-start.2 = ((f32[32,32,128]{2,1,0:T(8,128)}), f32[32,32,128]{2,1,0:T(8,128)}, u32[]{:S(2)}, u32[]{:S(2)}) async-start(f32[32,32,128]{2,1,0:T(8,128)} %bitcast.20), calls=%async_computation.2 | async-start | bytes 1048576 | tf_op jit(solution)/shard_map/all_to_all | solution.py:1084
  101.7 22.5 %collective-permute-start.10 = (f32[3,6,128,128]{3,2,1,0:T(8,128)}, f32[3,6,128,128]{3,2,1,0:T(8,128)}, u32[]{:S(2)}, u32[]{:S(2)}) collective-permute-start(f32[3,6,128,128]{3,2,1,0:T(8,128)} %copy-done.10), channel_id=1, source_target_pairs={{0,1},{1,2},{2,3},{4,5},{5,6},{6,7},{8,9},{9,10},{10,11},{12,13},{... | collective-permute-start | bytes 3538952 | tf_op jit(solution)/shard_map/ppermute | solution.py:801
  105.3 1.8 %copy-start.2 = (f32[3,14,128,128]{3,2,1,0:T(8,128)S(1)}, f32[3,14,128,128]{3,2,1,0:T(8,128)}, u32[]{:S(2)}) copy-start(f32[3,14,128,128]{3,2,1,0:T(8,128)} %copy-done.1) | copy-start | bytes 8257540
  107.1 1.1 copy-start.13
  108.2 1.7 %copy-start.4 = (f32[3,12,128,128]{3,2,1,0:T(8,128)S(1)}, f32[3,12,128,128]{3,2,1,0:T(8,128)}, u32[]{:S(2)}) copy-start(f32[3,12,128,128]{3,2,1,0:T(8,128)} %copy-done.3) | copy-start | bytes 7077892
  108.2 2.0 %copy-start.11 = (f32[3,6,128,128]{3,2,1,0:T(8,128)S(1)}, f32[3,6,128,128]{3,2,1,0:T(8,128)}, u32[]{:S(2)}) copy-start(f32[3,6,128,128]{3,2,1,0:T(8,128)} %copy-done.10) | copy-start | bytes 3538948
  108.2 2.0 %copy-start.16 = (bf16[512,256]{1,0:T(8,128)(2,1)S(1)}, bf16[512,256]{1,0:T(8,128)(2,1)}, u32[]{:S(2)}) copy-start(bf16[512,256]{1,0:T(8,128)(2,1)} %constant.36.clone.refs_2_) | copy-start | bytes 786436
  112.0 1.8 %copy-start.5 = (f32[3,18,128,128]{3,2,1,0:T(8,128)}, f32[3,18,128,128]{3,2,1,0:T(8,128)S(1)}, u32[]{:S(2)}) copy-start(f32[3,18,128,128]{3,2,1,0:T(8,128)S(1)} %get-tuple-element.83.staged) | copy-start | bytes 10616836
  117.0 22.4 %all-to-all-start.1 = ((f32[32,32,128]{2,1,0:T(8,128)}), f32[32,32,128]{2,1,0:T(8,128)}, u32[]{:S(2)}, u32[]{:S(2)}) async-start(f32[32,32,128]{2,1,0:T(8,128)} %bitcast.19), calls=%async_computation.1 | async-start | bytes 1048576 | tf_op jit(solution)/shard_map/all_to_all | solution.py:1084
  120.5 14.0 %collective-permute-start.9 = (f32[32,32,128]{2,1,0:T(8,128)}, f32[32,32,128]{2,1,0:T(8,128)S(1)}, u32[]{:S(2)}, u32[]{:S(2)}) collective-permute-start(f32[32,32,128]{2,1,0:T(8,128)} %all-to-all-done.2), channel_id=1, source_target_pairs={{0,1},{1,2},{2,3},{4,5},{5,6},{6,7},{8,9},{9,10},{10,11},{12,13},{... | collective-permute-start | bytes 1572872 | tf_op jit(solution)/shard_map/ppermute | solution.py:801
  124.2 4.2 %copy-start.6 = (f32[3,18,128,128]{3,2,1,0:T(8,128)S(1)}, f32[3,18,128,128]{3,2,1,0:T(8,128)}, u32[]{:S(2)}) copy-start(f32[3,18,128,128]{3,2,1,0:T(8,128)} %copy-done.5) | copy-start | bytes 10616836
  124.2 4.2 %copy-start.8 = (bf16[512,256]{1,0:T(8,128)(2,1)S(1)}, bf16[512,256]{1,0:T(8,128)(2,1)}, u32[]{:S(2)}) copy-start(bf16[512,256]{1,0:T(8,128)(2,1)} %copy-done.7) | copy-start | bytes 786436
  128.4 6.1 %copy-start = (f32[3,18,128,128]{3,2,1,0:T(8,128)S(1)}, f32[3,18,128,128]{3,2,1,0:T(8,128)}, u32[]{:S(2)}) copy-start(f32[3,18,128,128]{3,2,1,0:T(8,128)} %stage.5.staged) | copy-start | bytes 10616836
  139.4 1.0 copy-start.9
  (1 other events, 0.7 us)

commit v4 on v3

--- a/solution.py
+++ b/solution.py
@@ -407,6 +407,16 @@
             uv[3 + c, cell, rows, :] += second[2] * total
 
 
+def last_rhs_one(held, slot, uv, cell):
+    size = held.shape[2] - 2 * pad
+    for row in chunks(size):
+        rows = slice(row, row + rows_at_once)
+        _, fresh = rhs_rows(held, 0, slot, pad + row)
+        for c in range(3):
+            uv[c, cell, rows, :] += first[2] * fresh[c]
+            uv[3 + c, cell, rows, :] += second[2] * fresh[c]
+
+
 def uv_halves(uv, k, cell):
     half = uv.shape[2] // 2
     return uv[k, cell, pl.ds(0, half, 2), :] + uv[k, cell, pl.ds(1, half, 2), :]
@@ -531,7 +541,7 @@
 
 
 def end_one_kernel(
-    is_first, near, low, high, uv_in, pack, low_out, high_out, w_out, uv, held, sems, out_sems
+    is_first, near, low, high, uv_in, low_out, high_out, w_out, uv, held, sems
 ):
     size = near.shape[2]
     rows_all = pl.ds(pad, size)
@@ -540,12 +550,6 @@
         pltpu.make_async_copy(ref, held.at[:, slot, rows_all, :], sems.at[slot])
         for slot, ref in enumerate(sources)
     ])
-    packing = [
-        pltpu.make_async_copy(held.at[0:3, slot, rows_all, :], pack.at[:, k], out_sems.at[k])
-        for k, slot in enumerate((0, 5))
-    ]
-    for copy in packing:
-        copy.start()
     uv[...] = uv_in[...]
     for k, (slot, ref) in enumerate(((1, low_out), (4, high_out))):
         wrap_rows(held, slot, 9)
@@ -557,13 +561,11 @@
             w_out[c, k, row : row + rows_at_once, :] = value
 
         sweep_one_plane(is_first, held, slot, put_s1, put_w, uv, k)
-    for copy in packing:
-        copy.wait()
 
 
 def end_two_kernel(
     g_group, swept, low, low_end, high_end, high, w_end, w_next, uv_in, z_table, y_table,
-    pack, low_out, high_out, next_out, uv, g, held, held_2, sems, out_sems
+    low_out, high_out, next_out, uv, g, held, held_2, sems
 ):
     count, size = swept.shape[1], swept.shape[2]
     rows_all = pl.ds(pad, size)
@@ -573,12 +575,6 @@
         pltpu.make_async_copy(ref, held.at[:, slot, rows_all, :], sems.at[slot])
         for slot, ref in enumerate(sources)
     ])
-    packing = [
-        pltpu.make_async_copy(held.at[:, slot, rows_all, :], pack.at[:, k], out_sems.at[k])
-        for k, slot in enumerate((0, 1, 6, 7))
-    ]
-    for copy in packing:
-        copy.start()
     uv[...] = uv_in[...]
     places = ((1, 0, w_end, 0), (2, 0, w_next, 0), (5, 1, w_next, 1), (6, 1, w_end, 1))
     for index, (slot, cell, w, k) in enumerate(places):
@@ -603,52 +599,71 @@
     values = transform([held_halves(held_2, c, 2 * k) for c, k in entries], z_table, y_table)
     for (c, k), value in zip(entries, values):
         g[pl.ds(2 * c + k, blocks, g_group), :] = value
-    for copy in packing:
-        copy.wait()
+
+
+def middle_kernel(
+    group, swept, low_end, nexts, high_end, uv_in, uv_next, f, z_table, y_table,
+    uv, out, held, near, sems
+):
+    count, size = swept.shape[1], swept.shape[2]
+    planes = (count + 4) // 2
+    rows_all = pl.ds(pad, size)
+    sources = [low_end, nexts.at[:, 0], swept.at[:, 0], swept.at[:, 1], swept.at[:, 2]]
+    sources += [swept.at[:, count - 3], swept.at[:, count - 2], swept.at[:, count - 1]]
+    sources += [nexts.at[:, 1], high_end]
+    start_all([
+        pltpu.make_async_copy(ref, held.at[:, slot, rows_all, :], sems.at[slot])
+        for slot, ref in enumerate(sources)
+    ])
+    uv[...] = uv_in[...]
+    near[...] = uv_next[...]
+    out[...] = f[...]
+    for slot in (1, 2, 3, 6, 7, 8):
+        wrap_rows(held, slot, 3)
+    last_rhs_one(held, 1, uv, 0)
+    last_rhs_one(held, 8, uv, 1)
+    last_rhs_pair(held, 2, near, 0)
+    last_rhs_pair(held, 6, near, 1)
+    blocks = out.shape[0] // group
+    entries = [(k, index) for index in range(2) for k in range(6)]
+    values = transform([uv_halves(near, k, index) for k, index in entries], z_table, y_table)
+    for (k, index), value in zip(entries, values):
+        out[pl.ds(k * planes + (1, planes - 2)[index], blocks, group), :] = value
 
 
 def end_three_kernel(
-    group, g_group, end_group, swept, low, low_end, nexts, high_end, high, uv_end, uv_next, f, g, g_end,
+    group, g_group, end_group, low, low_end, nexts, high_end, high, uv_in, f, g, g_end,
     z_table, y_table, pack, sent, out, held, uv, sems, out_sems
 ):
-    count, size = swept.shape[1], swept.shape[2]
+    size = held.shape[2] - 2 * pad
     rows_all = pl.ds(pad, size)
-    planes = (count + 4) // 2
-    sources = [low, low_end, nexts.at[:, 0], swept.at[:, 0], swept.at[:, 1], swept.at[:, 2]]
-    sources += [swept.at[:, count - 3], swept.at[:, count - 2], swept.at[:, count - 1]]
-    sources += [nexts.at[:, 1], high_end, high]
+    blocks = out.shape[0] // group
+    planes = g.shape[0] // blocks // 3
+    sources = [low, low_end, nexts.at[:, 0], nexts.at[:, 1], high_end, high]
     start_all([
         pltpu.make_async_copy(ref, held.at[:, slot, rows_all, :], sems.at[slot])
         for slot, ref in enumerate(sources)
     ])
     packing = [
-        pltpu.make_async_copy(held.at[:, slot, rows_all, :], pack.at[:, k], out_sems.at[k])
-        for k, slot in enumerate((0, 1, 2, 9, 10, 11))
+        pltpu.make_async_copy(held.at[:, slot, rows_all, :], pack.at[:, slot], out_sems.at[slot])
+        for slot in range(6)
     ]
-    for k in range(2):
-        uv[:, 3 * k] = uv_end[:, k]
-        uv[:, 1 + k] = uv_next[:, k]
+    uv[...] = uv_in[...]
     out[...] = f[...]
-    for slot in (1, 2, 3, 4, 7, 8, 9, 10):
+    for slot in (1, 4):
         wrap_rows(held, slot, 3)
     for copy in packing:
         copy.start()
-    for index, slot in enumerate((1, 3, 7, 9)):
-        last_rhs_pair(held, slot, uv, index)
-    blocks = out.shape[0] // group
-    cells = (0, 1, planes - 2, planes - 1)
-    for half in range(2):
-        entries = [(k, index) for index in (2 * half, 2 * half + 1) for k in range(6)]
-        values = transform([uv_halves(uv, k, index) for k, index in entries], z_table, y_table)
-        for (k, index), value in zip(entries, values):
-            if k < 3:
-                if index % 3 == 0:
-                    value = value + g_end[pl.ds(2 * k + index // 3, blocks, end_group), :]
-                else:
-                    value = value + g[pl.ds(k * planes + cells[index], blocks, g_group), :]
-            out[pl.ds(k * planes + cells[index], blocks, group), :] = value
+    last_rhs_one(held, 1, uv, 0)
+    last_rhs_one(held, 4, uv, 1)
+    entries = [(k, index) for index in range(2) for k in range(6)]
+    values = transform([uv_halves(uv, k, index) for k, index in entries], z_table, y_table)
+    for (k, index), value in zip(entries, values):
+        if k < 3:
+            value = value + g_end[pl.ds(2 * k + index, blocks, end_group), :]
+        out[pl.ds(k * planes + index * (planes - 1), blocks, group), :] = value
     for k in range(3):
-        for cell in range(2, planes - 2):
+        for cell in range(1, planes - 1):
             out[pl.ds(k * planes + cell, blocks, group), :] += g[
                 pl.ds(k * planes + cell, blocks, g_group), :
             ]
@@ -657,48 +672,23 @@
         copy.wait()
 
 
-def stage_kernel(layouts, counts, *refs):
+def place(fields, layouts, is_first, staged, sems):
+    def launch(layout):
+        for slot, (number, index) in enumerate(layout):
+            ref = fields[number]
+            ref = ref.at[0:3, index] if index is not None else ref.at[0:3]
+            pltpu.make_async_copy(ref, staged.at[:, slot], sems.at[slot]).start()
+
     if len(layouts) > 1:
-        is_first, refs = refs[0], refs[1:]
-    fields, sems = refs[:counts], refs[-1]
-    extras = (len(refs) - counts - 2) // 2
-    staged = refs[counts + extras]
-    rest = [
-        pltpu.make_async_copy(refs[counts + k], refs[counts + extras + 1 + k], sems.at[k])
-        for k in range(extras)
-    ]
-    for copy in rest:
-        copy.start()
-
-    def arriving(layout, slot):
-        number, index = layout[slot]
-        ref = fields[number]
-        ref = ref.at[0:3, index] if index is not None else ref.at[0:3]
-        return pltpu.make_async_copy(ref, staged.at[:, slot], sems.at[extras + slot])
-
-    def launch(layout):
-        for slot in range(len(layout)):
-            arriving(layout, slot).start()
-
-    if len(layouts) > 1:
-
-        @pl.when(is_first[0] > 0)
-        def _():
-            launch(layouts[0])
-
-        @pl.when(is_first[0] <= 0)
-        def _():
-            launch(layouts[1])
+        pl.when(is_first[0] > 0)(functools.partial(launch, layouts[0]))
+        pl.when(is_first[0] <= 0)(functools.partial(launch, layouts[1]))
     else:
         launch(layouts[0])
-    for slot in range(len(layouts[0])):
-        arriving(layouts[0], slot).wait()
-    for copy in rest:
-        copy.wait()
-
-
-def corrected_kernel(node, group, spectra, table, staged, *refs):
-    new_velocity, new_rhs, held, coarse, result, out_sems, rhs_sems = refs[-7:]
+
+
+def corrected_kernel(node, group, layouts, count, is_first, spectra, table, *refs):
+    new_velocity, new_rhs, held, staged, coarse, result, sems, out_sems, rhs_sems = refs[-9:]
+    place(refs[:count], layouts, is_first, staged, sems)
     length, size = staged.shape[1] - 2, staged.shape[2]
     planes = length // 2
     rows_all = pl.ds(pad, size)
@@ -709,10 +699,16 @@
         base = c * (planes + 2)
         parts = [spectra[pl.ds(base + e, blocks, group), :] for e in range(planes + 2)]
         in_z = right_dot(jnp.concatenate(parts, axis=0), table[:z_rows, :])
-        for e in range(planes + 2):
-            mine = in_z[e * blocks : (e + 1) * blocks]
-            stacked = jnp.concatenate([mine[:, :size], mine[:, size:]], axis=0)
-            coarse[c, e] = left_dot(table[z_rows : z_rows + y_rows, :y_columns], stacked)
+        for e in range(0, planes + 2, 2):
+            stacked = []
+            for k in (e, min(e + 1, planes + 1)):
+                mine = in_z[k * blocks : (k + 1) * blocks]
+                stacked.append(jnp.concatenate([mine[:, :size], mine[:, size:]], axis=0))
+            both = left_dot(
+                table[z_rows : z_rows + y_rows, :y_columns], jnp.concatenate(stacked, axis=1)
+            )
+            for k in range(min(2, planes + 2 - e)):
+                coarse[c, e + k] = both[:, k * size : (k + 1) * size]
 
     def out_copy(plane):
         return pltpu.make_async_copy(
@@ -725,6 +721,7 @@
         )
 
     def correct(plane, cell, odd):
+        pltpu.make_async_copy(staged.at[:, plane], staged.at[:, plane], sems.at[plane]).wait()
         for field in range(3):
             for row in chunks(size):
                 rows = slice(row, row + rows_at_once)
@@ -801,48 +798,33 @@
     return lax.ppermute(value, "tm", [(i, i + 1) for i in range(count - 1)])
 
 
-def stage(fields, layouts, is_first, extras=()):
-    size_y, size_z = fields[0].shape[-2:]
-    slots = len(layouts[0])
-    operands, specs = [*fields, *extras], [anywhere] * (len(fields) + len(extras))
-    if len(layouts) > 1:
-        operands, specs = [is_first, *operands], [scalar, *specs]
-    return pl.pallas_call(
-        functools.partial(stage_kernel, layouts, len(fields)),
-        out_shape=(struct((3, slots, size_y, size_z)), *[struct(e.shape, e.dtype) for e in extras]),
-        in_specs=specs,
-        out_specs=(vmem,) * (1 + len(extras)),
-        scratch_shapes=[pltpu.SemaphoreType.DMA((slots + len(extras),))],
-        compiler_params=params(8192 if len(layouts) == 1 else 57344),
-        name="stage",
-    )(*operands)
-
-
-def corrected(node, spectra, table, staged, outs):
-    length = staged.shape[1] - 2
-    size_y, size_z = staged.shape[-2:]
-    planes = length // 2
-    group = spectra.shape[1]
-    operands, specs = [spectra.reshape(-1, lanes), table, staged], [vmem] * 3
+def corrected(node, spectra, table, placed, outs, is_first):
+    fields, layouts = placed
+    group, slots, (size_y, size_z) = spectra.shape[1], len(layouts[0]), fields[0].shape[-2:]
+    length, planes = slots - 2, slots // 2 - 1
+    operands = [is_first, spectra.reshape(-1, lanes), table, *fields]
+    specs = [scalar, vmem, vmem] + [anywhere] * len(fields)
     shape = (3, 3, length, size_y, size_z)
     aliases = {}
     if outs is not None:
-        aliases = {3: 0, 4: 1}
+        aliases = {len(operands): 0, len(operands) + 1: 1}
         operands, specs = [*operands, *outs], specs + [hbm] * 2
     return pl.pallas_call(
-        functools.partial(corrected_kernel, node, group),
+        functools.partial(corrected_kernel, node, group, layouts, len(fields)),
         out_shape=(struct(shape), struct(shape, bf16)),
         in_specs=specs,
         out_specs=(hbm, hbm),
         input_output_aliases=aliases,
         scratch_shapes=[
             held_planes(3, length, size_y, size_z),
+            pltpu.VMEM((3, slots, size_y, size_z), f32),
             pltpu.VMEM((3, planes + 2, size_y, size_z), f32),
             pltpu.VMEM((3, length, size_y, size_z), bf16),
+            pltpu.SemaphoreType.DMA((slots,)),
             pltpu.SemaphoreType.DMA((length,)),
             pltpu.SemaphoreType.DMA((length,)),
         ],
-        compiler_params=params(16384),
+        compiler_params=params_but(560),
         name=f"corrected_{node}",
     )(*operands)
 
@@ -905,12 +887,13 @@
     )(swept_2, low_2, high_2, u, v, g, z_table, y_table)
     layout = tuple([(0, None)] + [(1, p) for p in range(length)] + [(2, None)])
     carried = [later_interval(value) for value in (low_2, swept_2, high_2)]
-    later = tuple((3 + number, index) for number, index in layout)
+    own = tuple((3 + number, index) for number, index in layout)
     return (
         sources,
         ((low_1, swept_1, high_1), (layout,)),
         ((low_2, swept_2, high_2), (layout,)),
-        ((low, fields, high, *carried), (layout, later)),
+        tuple(carried),
+        ((low, fields, high), (own, layout)),
     )
 
 
@@ -963,27 +946,25 @@
         name="interior",
     )(is_first, fields, z_table, y_table)
     g_moved = later_interval(g)
-    pack_0, low_end_1, high_end_1, w_end, uv_end = pl.pallas_call(
+    low_end_1, high_end_1, w_end, uv_end = pl.pallas_call(
         end_one_kernel,
         out_shape=(
-            struct((3, 2, *plane)),
             struct((3, *plane)),
             struct((3, *plane)),
             struct((3, 2, *plane)),
             struct((6, 2, *plane)),
         ),
         in_specs=[scalar, anywhere, anywhere, anywhere, vmem],
-        out_specs=(hbm,) + (vmem,) * 4,
-        scratch_shapes=[held(9, 6), sems(6), sems(2)],
+        out_specs=(vmem,) * 4,
+        scratch_shapes=[held(9, 6), sems(6)],
         compiler_params=params(16384),
         name="end_one",
     )(is_first, near, low, high, uv_end)
     low_1, high_1 = neighbours(low_end_1, high_end_1)
     end_group = 8
-    pack_1, low_end_2, high_end_2, next_2, uv_end, g_end = pl.pallas_call(
+    low_end_2, high_end_2, next_2, uv_end, g_end = pl.pallas_call(
         functools.partial(end_two_kernel, end_group),
         out_shape=(
-            struct((3, 4, *plane)),
             struct((3, *plane)),
             struct((3, *plane)),
             struct((3, 2, *plane)),
@@ -991,43 +972,50 @@
             struct((blocks * end_group, lanes)),
         ),
         in_specs=[hbm] + [anywhere] * 4 + [vmem] * 5,
-        out_specs=(hbm,) + (vmem,) * 5,
-        scratch_shapes=[held(3, 8), held(3, 4), sems(8), sems(4)],
+        out_specs=(vmem,) * 5,
+        scratch_shapes=[held(3, 8), held(3, 4), sems(8)],
         compiler_params=params(16384),
         name="end_two",
     )(swept_1, low_1, low_end_1, high_end_1, high_1, w_end, w_next, uv_end, z_table, y_table)
     low_2, high_2 = neighbours(low_end_2, high_end_2)
+    uv_end, f = pl.pallas_call(
+        functools.partial(middle_kernel, group),
+        out_shape=(struct((6, 2, *plane)), struct((blocks * group, lanes))),
+        in_specs=[hbm] + [anywhere] * 3 + [vmem] * 5,
+        out_specs=(vmem,) * 2,
+        scratch_shapes=[held(3, 10), pltpu.VMEM((6, 2, *plane), f32), sems(10)],
+        compiler_params=params(16384),
+        name="middle",
+    )(swept_2, low_end_2, next_2, high_end_2, uv_end, uv_next, f, z_table, y_table)
     pack, sources = pl.pallas_call(
         functools.partial(end_three_kernel, group, g_group, end_group),
         out_shape=(struct((3, 6, *plane)), struct((blocks * group, lanes))),
-        in_specs=[hbm] + [anywhere] * 5 + [vmem] * 7,
+        in_specs=[anywhere] * 5 + [vmem] * 6,
         out_specs=(hbm, hbm),
         scratch_shapes=[
             pltpu.VMEM((blocks * group, lanes), f32),
-            held(3, 12),
-            pltpu.VMEM((6, 4, *plane), f32),
-            sems(12),
+            held(3, 6),
+            pltpu.VMEM((6, 2, *plane), f32),
+            sems(6),
             sems(7),
         ],
         compiler_params=params(16384),
         name="end_three",
     )(
-        swept_2, low_2, low_end_2, next_2, high_end_2, high_2, uv_end, uv_next, f,
+        low_2, low_end_2, next_2, high_end_2, high_2, uv_end, f,
         g_moved, later_interval(g_end), z_table, y_table
     )
-    inner_1 = [(1, p) for p in range(length - 2)]
+    inner_1 = [(2, p) for p in range(length - 2)]
     inner_2 = [(1, p) for p in range(length - 4)]
-    layout_1 = [(0, 0), (0, 1)] + inner_1 + [(0, 2), (0, 3)]
+    layout_1 = [(0, None), (1, None)] + inner_1 + [(3, None), (4, None)]
     layout_2 = [(0, 0), (0, 1), (0, 2)] + inner_2 + [(0, 3), (0, 4), (0, 5)]
-    layout_0 = [(2, 0)] + [(3, p) for p in range(length)] + [(2, 1)]
+    layout_0 = [(2, None)] + [(3, p) for p in range(length)] + [(4, None)]
     return (
         sources,
-        ((pack_1, swept_1), (tuple(layout_1),)),
+        ((low_1, low_end_1, swept_1, high_end_1, high_1), (tuple(layout_1),)),
         ((pack, swept_2), (tuple(layout_2),)),
-        (
-            (later_interval(pack), later_interval(swept_2), pack_0, fields),
-            (tuple(layout_0), tuple(layout_2)),
-        ),
+        (later_interval(pack), later_interval(swept_2)),
+        ((low, fields, high), (tuple(layout_0), tuple(layout_2))),
     )
 
 
@@ -1065,8 +1053,8 @@
 
     is_first = tm_first.astype(f32).reshape(1)
     sweep = sweep_split if length >= 10 else sweep_whole
-    carried_at = 1 if length >= 10 else 4
-    sources, one, two, zero = sweep(fields, is_first, z_table, y_table, blocks)
+    moved_at = 1
+    sources, one, two, carried, zero = sweep(fields, is_first, z_table, y_table, blocks)
     group = round_up(6 * planes, 8)
 
     both = ("space", "tm")
@@ -1091,8 +1079,9 @@
     y_back_table = np.pad(y_back_table, ((0, 0), (0, z_back_table.shape[1] - y_back_table.shape[1])))
     table = np.concatenate([z_back_table, y_back_table], axis=0)
     columned = to_columns(sources, group)
-    columned, moved = lax.optimization_barrier((columned, zero[0][carried_at]))
-    carried_fields = zero[0][:carried_at] + (moved,) + zero[0][carried_at + 1 :]
+    moved = carried[moved_at]
+    columned, moved = lax.optimization_barrier((columned, moved))
+    carried = (*carried[:moved_at], moved, *carried[moved_at + 1 :])
     solved_1, solved_2 = pl.pallas_call(
         functools.partial(solve_kernel, peers, intervals, planes, group, back),
         out_shape=(struct((devices * back, lanes)),) * 2,
@@ -1109,18 +1098,13 @@
         compiler_params=params_but(790),
         name="solve",
     )(columned, rates, x_table)
-    fields_1, fields_2, solved_2, solved_1 = lax.optimization_barrier(
-        (one[0], two[0], solved_2, solved_1)
-    )
     spectra_2 = to_planes(solved_2, back)
-    staged_2, table = stage(fields_2, two[1], None, (jnp.asarray(table),))
-    (staged_1,) = stage(fields_1, one[1], None)
-    solved_1, staged_2, staged_1 = lax.optimization_barrier((solved_1, staged_2, staged_1))
+    solved_1, *carried = lax.optimization_barrier((solved_1, *carried))
+    zero = ((*carried, *zero[0]), zero[1])
     spectra_1 = to_planes(solved_1, back)
-    (staged_0,) = stage(carried_fields, zero[1], is_first)
-    outs = corrected(2, spectra_2, table, staged_2, None)
-    outs = corrected(0, later_interval(spectra_2), table, staged_0, outs)
-    new_velocity, new_rhs = corrected(1, spectra_1, table, staged_1, outs)
+    outs = corrected(2, spectra_2, table, two, None, is_first)
+    outs = corrected(0, later_interval(spectra_2), table, zero, outs, is_first)
+    new_velocity, new_rhs = corrected(1, spectra_1, table, one, outs, is_first)
     return (new_velocity[None], new_rhs[None])
 
 

time: 147 us -> 145 us (0.986)
  waiting for transfers between devices: 28.3 us -> 40.6 us
  local copies, waits for them, and re-layouts: 10 us -> 2.43 us
  Pallas kernels: 59.6 us -> 52.4 us
    all_to_all x2, waiting for transfers between devices: 2.54 us -> 15.2 us  [to_planes(): value = lax.all_to_all(value, both, split_axis=0, concat_axis=0, tiled=True)]
    unnamed x38 -> x24, local copies, waits for them, and re-layouts: 9.31 us -> 1.73 us
    pallas_call x7 -> x5, Pallas kernels: 26.9 us -> 22.1 us  [the longest x3 18.5 us: corrected(): pl.pallas_call(functools.partial(corrected_kernel, node, group, layouts,...]
    ppermute x5, waiting for transfers between devices: 2.62 us -> 7.46 us  [later_interval(): return lax.ppermute(value, 'tm', [(i, i + 1) for i in range(count - 1)])]
    all_to_all x1, waiting for transfers between devices: 18.9 us -> 15.3 us  [to_columns(): value = lax.all_to_all(value, both, split_axis=0, concat_axis=0, tiled=True)]
    pallas_call x1, Pallas kernels: 4.78 us -> 2.88 us  [sweep_split(): pl.pallas_call(functools.partial(end_three_kernel, group, g_group, end_gr...]
    ppermute x3, waiting for transfers between devices: 4.17 us -> 2.63 us  [neighbours(): lax.ppermute(low_plane, 'space', down)]
  transfers between devices with their start and end apart: 14 -> 14, of which waited for: 7 -> 6; matrix products, arithmetic and copies ran while one was open for 1% -> 1% of each run, Pallas kernels for 32% -> 31%
where the time goes in v4:
time: 145 us; the launch traced here: 144 us
  Pallas kernels  52.4 us (36%)
  starting transfers between devices  46.6 us (32%)
  waiting for transfers between devices  40.6 us (28%)
  local copies, waits for them, and re-layouts  2.43 us (2%)
    ppermute x5, starting transfers between devices, later_interval(): return lax.ppermute(value, 'tm', [(i, i + 1) for i in range(count - 1)])  21 us
    pallas_call x1, Pallas kernels, sweep_split(): pl.pallas_call(functools.partial(interior_kernel, group, g_group), out_sh...  18.6 us
    pallas_call x3, Pallas kernels, corrected(): pl.pallas_call(functools.partial(corrected_kernel, node, group, layouts,...  18.5 us
    all_to_all x1, waiting for transfers between devices, to_columns(): value = lax.all_to_all(value, both, split_axis=0, concat_axis=0, tiled=True)  15.3 us
    all_to_all x2, waiting for transfers between devices, to_planes(): value = lax.all_to_all(value, both, split_axis=0, concat_axis=0, tiled=True)  15.2 us
    ppermute x3, starting transfers between devices, neighbours(): lax.ppermute(low_plane, 'space', down)  11.4 us
    all_to_all x2, starting transfers between devices, to_planes(): value = lax.all_to_all(value, both, split_axis=0, concat_axis=0, tiled=True)  7.63 us
    ppermute x5, waiting for transfers between devices, later_interval(): return lax.ppermute(value, 'tm', [(i, i + 1) for i in range(count - 1)])  7.46 us
  transfers between devices with their start and end apart: 14, of which 6 were waited for; matrix products, arithmetic and copies ran while one was open for 1% of the time, Pallas kernels for 31%

profile of v4, /device:TPU:1, one launch (start us, length us, event | category | flops | bytes accessed | tf_op | source)
XLA Modules:
  0.0 143.8 jit_solution(9452586334230912419)
XLA Ops:
  0.6 2.3 %edges.1 = (f32[9,128,128]{2,1,0:T(8,128)}, f32[9,128,128]{2,1,0:T(8,128)}) custom-call(f32[9,16,128,128]{3,2,1,0:T(8,128)} %bitcast.13), custom_call_target="tpu_custom_call" | custom-call | tf_op jit(solution)/shard_map/edges/pallas_call | solution.py:911
  2.9 2.1 %collective-permute-start = (f32[9,128,128]{2,1,0:T(8,128)}, f32[9,128,128]{2,1,0:T(8,128)S(1)}, u32[]{:S(2)}, u32[]{:S(2)}) collective-permute-start(f32[9,128,128]{2,1,0:T(8,128)} %get-tuple-element.40), channel_id=1, source_target_pairs={{0,4},{4,8},{8,12},{12,16},{16,20},{20,24},{24,28},{28,0},{1,5},{5... | collective-permute-start | bytes 1769480 | tf_op jit(solution)/shard_map/ppermute | solution.py:793
  5.0 3.1 %collective-permute-start.1 = (f32[9,128,128]{2,1,0:T(8,128)}, f32[9,128,128]{2,1,0:T(8,128)S(1)}, u32[]{:S(2)}, u32[]{:S(2)}) collective-permute-start(f32[9,128,128]{2,1,0:T(8,128)} %get-tuple-element.41), channel_id=1, source_target_pairs={{4,0},{8,4},{12,8},{16,12},{20,16},{24,20},{28,24},{0,28},{5,1},{9... | collective-permute-start | bytes 1769480 | tf_op jit(solution)/shard_map/ppermute | solution.py:793
  8.1 0.9 copy-done.4
  9.1 0.8 copy-done.9
  9.8 18.6 %interior.1 = (f32[9,4,128,128]{3,2,1,0:T(8,128)S(1)}, f32[3,14,128,128]{3,2,1,0:T(8,128)S(1)}, f32[3,12,128,128]{3,2,1,0:T(8,128)S(1)}, f32[3,2,128,128]{3,2,1,...) custom-call(f32[1]{0:T(128)} %bitcast.is_first, ...), custom_call_target="tpu_custom_call" | custom-call | flops 4000000000 | bytes 60000000 | tf_op jit(solution)/shard_map/interior/pallas_call | solution.py:921
  28.4 4.1 %collective-permute-start.8 = (f32[3,12,128,128]{3,2,1,0:T(8,128)S(1)}, f32[3,12,128,128]{3,2,1,0:T(8,128)}, u32[]{:S(2)}, u32[]{:S(2)}) collective-permute-start(f32[3,12,128,128]{3,2,1,0:T(8,128)S(1)} %get-tuple-element.51.swept.refs_1_), channel_id=1, source_target_pairs={{0,1},{1,2},{2,3},{4,5},{5,6},{6,7},{8,9},{9,10},{10,11},{12,13},{... | collective-permute-start | bytes 7077896 | tf_op jit(solution)/shard_map/ppermute | solution.py:798
  32.5 1.3 end_one.1
  33.9 4.1 %collective-permute-start.3 = (f32[3,128,128]{2,1,0:T(8,128)S(1)}, f32[3,128,128]{2,1,0:T(8,128)S(1)}, u32[]{:S(2)}, u32[]{:S(2)}) collective-permute-start(f32[3,128,128]{2,1,0:T(8,128)S(1)} %get-tuple-element.44.low_end.refs_1_), channel_id=1, source_target_pairs={{4,0},{8,4},{12,8},{16,12},{20,16},{24,20},{28,24},{0,28},{5,1},{9... | collective-permute-start | bytes 589832 | tf_op jit(solution)/shard_map/ppermute | solution.py:793
  38.1 4.7 %collective-permute-start.6 = (f32[768,128]{1,0:T(8,128)S(1)}, f32[768,128]{1,0:T(8,128)S(1)}, u32[]{:S(2)}, u32[]{:S(2)}) collective-permute-start(f32[768,128]{1,0:T(8,128)S(1)} %get-tuple-element.57), channel_id=1, source_target_pairs={{0,1},{1,2},{2,3},{4,5},{5,6},{6,7},{8,9},{9,10},{10,11},{12,13},{... | collective-permute-start | bytes 1179656 | tf_op jit(solution)/shard_map/ppermute | solution.py:798
  42.7 2.6 %collective-permute-done.3.high.refs_4_ = f32[3,128,128]{2,1,0:T(8,128)S(1)} collective-permute-done((f32[3,128,128]{2,1,0:T(8,128)S(1)}, f32[3,128,128]{2,1,0:T(8,128)S(1)}, u32[]{:S(2)}, u32[]{:S(2)}) %collective-permute-start.3) | collective-permute-done | bytes 196640 | tf_op jit(solution)/shard_map/ppermute | solution.py:793
  45.4 1.9 %end_two.1 = (f32[3,128,128]{2,1,0:T(8,128)S(1)}, f32[3,128,128]{2,1,0:T(8,128)S(1)}, f32[3,2,128,128]{3,2,1,0:T(8,128)S(1)}, f32[6,2,128,128]{3,2,1,0:T(8,128)S(1)}, f32[256,128]{1,0:T(8,128)S(1)}) custom-call(f32[3,14,128,128]{3,2,1,0:T(8,128)S(1)} %get-tuple-element.38.swept.refs_2_, f32[3,128,128]{2,1,0:T(8,128)S(1)} %collective-permute-done.2.low.refs_0_, ...), custom_call_target="tpu_custom_call" | custom-call | tf_op jit(solution)/shard_map/end_two/pallas_call | solution.py:965
  47.4 4.1 %collective-permute-start.5 = (f32[3,128,128]{2,1,0:T(8,128)S(1)}, f32[3,128,128]{2,1,0:T(8,128)S(1)}, u32[]{:S(2)}, u32[]{:S(2)}) collective-permute-start(f32[3,128,128]{2,1,0:T(8,128)S(1)} %get-tuple-element.49.low_end), channel_id=1, source_target_pairs={{4,0},{8,4},{12,8},{16,12},{20,16},{24,20},{28,24},{0,28},{5,1},{9... | collective-permute-start | bytes 589832 | tf_op jit(solution)/shard_map/ppermute | solution.py:793
  51.6 5.0 %collective-permute-start.7 = (f32[256,128]{1,0:T(8,128)S(1)}, f32[256,128]{1,0:T(8,128)S(1)}, u32[]{:S(2)}, u32[]{:S(2)}) collective-permute-start(f32[256,128]{1,0:T(8,128)S(1)} %get-tuple-element.58), channel_id=1, source_target_pairs={{0,1},{1,2},{2,3},{4,5},{5,6},{6,7},{8,9},{9,10},{10,11},{12,13},{... | collective-permute-start | bytes 393224 | tf_op jit(solution)/shard_map/ppermute | solution.py:798
  56.6 2.3 %middle.1 = (f32[6,2,128,128]{3,2,1,0:T(8,128)S(1)}, f32[1536,128]{1,0:T(8,128)S(1)}) custom-call(f32[3,12,128,128]{3,2,1,0:T(8,128)S(1)} %get-tuple-element.51.swept.refs_1_, f32[3,128,128]{2,1,0:T(8,128)S(1)} %get-tuple-element.49.low_end, f32[3,2,128,128]{3,2,1,0:T(8,128)S(1)} %get-tuple-element.50.nexts, f32[3,128,128]{2,1,0:T(8,128)S(1)} %get-tuple-element.48.high_end, ...), custom_call_target="tpu_custom_call" | custom-call | tf_op jit(solution)/shard_map/middle/pallas_call | solution.py:981
  58.9 3.5 %collective-permute-done.6.g = f32[768,128]{1,0:T(8,128)S(1)} collective-permute-done((f32[768,128]{1,0:T(8,128)S(1)}, f32[768,128]{1,0:T(8,128)S(1)}, u32[]{:S(2)}, u32[]{:S(2)}) %collective-permute-start.6) | collective-permute-done | bytes 393248 | tf_op jit(solution)/shard_map/ppermute | solution.py:798
  62.5 1.4 collective-permute-done.7.g_end
  63.9 2.9 %end_three.1 = (f32[3,6,128,128]{3,2,1,0:T(8,128)}, f32[1536,128]{1,0:T(8,128)}) custom-call(f32[3,128,128]{2,1,0:T(8,128)S(1)} %collective-permute-done.4.low, f32[3,128,128]{2,1,0:T(8,128)S(1)} %get-tuple-element.49.low_end, f32[3,2,128,128]{3,2,1,0:T(8,128)S(1)} %get-tuple-element.50.nexts, f32[3,128,128]{2,1,0:T(8,128)S(1)} %get-tuple-element.48.high_end, ...), custom_call_target="tpu_custom_call" | custom-call | tf_op jit(solution)/shard_map/end_three/pallas_call | solution.py:990
  66.7 4.3 %all-to-all-start = ((f32[32,48,128]{2,1,0:T(8,128)}), f32[32,48,128]{2,1,0:T(8,128)}, u32[]{:S(2)}, u32[]{:S(2)}) async-start(f32[32,48,128]{2,1,0:T(8,128)} %bitcast.2), calls=%async_computation | async-start | bytes 1572864 | tf_op jit(solution)/shard_map/all_to_all | solution.py:1066
  71.1 0.7 dynamic-slice_bitcast_fusion
  71.8 3.5 %collective-permute-start.9 = (f32[3,6,128,128]{3,2,1,0:T(8,128)}, f32[3,6,128,128]{3,2,1,0:T(8,128)}, u32[]{:S(2)}, u32[]{:S(2)}) collective-permute-start(f32[3,6,128,128]{3,2,1,0:T(8,128)} %get-tuple-element.62.refs_0_), channel_id=1, source_target_pairs={{0,1},{1,2},{2,3},{4,5},{5,6},{6,7},{8,9},{9,10},{10,11},{12,13},{... | collective-permute-start | bytes 3538952 | tf_op jit(solution)/shard_map/ppermute | solution.py:798
  75.3 0.7 add_divide_fusion.inverse_in
  76.0 15.3 %all-to-all-done = f32[32,48,128]{2,1,0:T(8,128)} async-done(((f32[32,48,128]{2,1,0:T(8,128)}), f32[32,48,128]{2,1,0:T(8,128)}, u32[]{:S(2)}, u32[]{:S(2)}) %all-to-all-start) | async-done | bytes 786464 | tf_op jit(solution)/shard_map/all_to_all | solution.py:1066
  91.3 4.7 %solve.1 = (f32[1024,128]{1,0:T(8,128)}, f32[1024,128]{1,0:T(8,128)}) custom-call(f32[1536,128]{1,0:T(8,128)} %bitcast.3.values, f32[64,128]{1,0:T(8,128)} %add_divide_fusion.inverse_in, bf16[144,192]{1,0:T(8,128)(2,1)} %constant.35.clone.table_in), custom_call_target="tpu_custom_call" | custom-call | tf_op jit(solution)/shard_map/solve/pallas_call | solution.py:1085
  96.0 4.2 %all-to-all-start.2 = ((f32[32,32,128]{2,1,0:T(8,128)}), f32[32,32,128]{2,1,0:T(8,128)}, u32[]{:S(2)}, u32[]{:S(2)}) async-start(f32[32,32,128]{2,1,0:T(8,128)} %bitcast.19), calls=%async_computation.2 | async-start | bytes 1048576 | tf_op jit(solution)/shard_map/all_to_all | solution.py:1072
  100.2 15.2 %all-to-all-done.2 = f32[32,32,128]{2,1,0:T(8,128)} async-done(((f32[32,32,128]{2,1,0:T(8,128)}), f32[32,32,128]{2,1,0:T(8,128)}, u32[]{:S(2)}, u32[]{:S(2)}) %all-to-all-start.2) | async-done | bytes 524320 | tf_op jit(solution)/shard_map/all_to_all | solution.py:1072
  115.4 3.5 %all-to-all-start.1 = ((f32[32,32,128]{2,1,0:T(8,128)}), f32[32,32,128]{2,1,0:T(8,128)}, u32[]{:S(2)}, u32[]{:S(2)}) async-start(f32[32,32,128]{2,1,0:T(8,128)} %bitcast.18), calls=%async_computation.1 | async-start | bytes 1048576 | tf_op jit(solution)/shard_map/all_to_all | solution.py:1072
  118.9 3.7 %collective-permute-start.10 = (f32[32,32,128]{2,1,0:T(8,128)}, f32[32,32,128]{2,1,0:T(8,128)}, u32[]{:S(2)}, u32[]{:S(2)}) collective-permute-start(f32[32,32,128]{2,1,0:T(8,128)} %all-to-all-done.2), channel_id=1, source_target_pairs={{0,1},{1,2},{2,3},{4,5},{5,6},{6,7},{8,9},{9,10},{10,11},{12,13},{... | collective-permute-start | bytes 1572872 | tf_op jit(solution)/shard_map/ppermute | solution.py:798
  122.6 6.1 %corrected_2.1 = (f32[3,3,16,128,128]{4,3,2,1,0:T(8,128)}, bf16[3,3,16,128,128]{4,3,2,1,0:T(8,128)(2,1)}) custom-call(f32[1]{0:T(128)} %bitcast.is_first, f32[1024,128]{1,0:T(8,128)} %bitcast.9.spectra, bf16[512,256]{1,0:T(8,128)(2,1)} %constant.36.clone.table, f32[3,6,128,128]{3,2,1,0:T(8,128)} %get-tuple-element.62.refs_0_, f32[3,12,128,128]{3,2,1,0:T(8,128)} %copy-done.1), custom_call_target="tpu_custom_call" | custom-call | tf_op jit(solution)/shard_map/corrected_2/pallas_call | solution.py:812
  128.8 2.5 %collective-permute-done.10 = f32[32,32,128]{2,1,0:T(8,128)} collective-permute-done((f32[32,32,128]{2,1,0:T(8,128)}, f32[32,32,128]{2,1,0:T(8,128)}, u32[]{:S(2)}, u32[]{:S(2)}) %collective-permute-start.10) | collective-permute-done | bytes 524320 | tf_op jit(solution)/shard_map/ppermute | solution.py:798
  131.3 6.2 %corrected_0.1 = (f32[3,3,16,128,128]{4,3,2,1,0:T(8,128)}, bf16[3,3,16,128,128]{4,3,2,1,0:T(8,128)(2,1)}) custom-call(f32[1]{0:T(128)} %bitcast.is_first, f32[1024,128]{1,0:T(8,128)} %bitcast.8.spectra, bf16[512,256]{1,0:T(8,128)(2,1)} %constant.36.clone.table, ...), custom_call_target="tpu_custom_call", output_to_operand_aliasing={{0}: (8, {}), {1}: (9, {})} | custom-call | tf_op jit(solution)/shard_map/corrected_0/pallas_call | solution.py:812
  137.5 6.1 %corrected_1.1 = (f32[3,3,16,128,128]{4,3,2,1,0:T(8,128)}, bf16[3,3,16,128,128]{4,3,2,1,0:T(8,128)(2,1)}) custom-call(f32[1]{0:T(128)} %bitcast.is_first, f32[1024,128]{1,0:T(8,128)} %bitcast.6.spectra, bf16[512,256]{1,0:T(8,128)(2,1)} %constant.36.clone.table, f32[3,128,128]{2,1,0:T(8,128)} %copy-done.7, ...), custom_call_target="tpu_custom_call", output_to_operand_aliasing={{0}: (8, {}), {1}: (9, {})} | custom-call | tf_op jit(solution)/shard_map/corrected_1/pallas_call | solution.py:812
  (32 shorter events, 0.2 us)
Async XLA Ops:
  2.9 29.6 %collective-permute-start = (f32[9,128,128]{2,1,0:T(8,128)}, f32[9,128,128]{2,1,0:T(8,128)S(1)}, u32[]{:S(2)}, u32[]{:S(2)}) collective-permute-start(f32[9,128,128]{2,1,0:T(8,128)} %get-tuple-element.40), channel_id=1, source_target_pairs={{0,4},{4,8},{8,12},{12,16},{16,20},{20,24},{24,28},{28,0},{1,5},{5... | collective-permute-start | bytes 1769480 | tf_op jit(solution)/shard_map/ppermute | solution.py:793
  5.0 27.5 %collective-permute-start.1 = (f32[9,128,128]{2,1,0:T(8,128)}, f32[9,128,128]{2,1,0:T(8,128)S(1)}, u32[]{:S(2)}, u32[]{:S(2)}) collective-permute-start(f32[9,128,128]{2,1,0:T(8,128)} %get-tuple-element.41), channel_id=1, source_target_pairs={{4,0},{8,4},{12,8},{16,12},{20,16},{24,20},{28,24},{0,28},{5,1},{9... | collective-permute-start | bytes 1769480 | tf_op jit(solution)/shard_map/ppermute | solution.py:793
  8.1 0.9 copy-start.4
  9.1 0.8 copy-start.9
  9.8 35.6 %copy-start.10 = (bf16[64,192]{1,0:T(8,128)(2,1)S(1)}, bf16[64,192]{1,0:T(8,128)(2,1)}, u32[]{:S(2)}) copy-start(bf16[64,192]{1,0:T(8,128)(2,1)} %constant.34.clone.y_table) | copy-start | bytes 73732
  28.4 18.9 %copy-start = (f32[3,14,128,128]{3,2,1,0:T(8,128)}, f32[3,14,128,128]{3,2,1,0:T(8,128)S(1)}, u32[]{:S(2)}) copy-start(f32[3,14,128,128]{3,2,1,0:T(8,128)S(1)} %get-tuple-element.38.swept.refs_2_) | copy-start | bytes 8257540
  28.4 28.2 %copy-start.1 = (f32[3,12,128,128]{3,2,1,0:T(8,128)}, f32[3,12,128,128]{3,2,1,0:T(8,128)S(1)}, u32[]{:S(2)}) copy-start(f32[3,12,128,128]{3,2,1,0:T(8,128)S(1)} %get-tuple-element.51.swept.refs_1_) | copy-start | bytes 7077892
  28.4 47.6 %collective-permute-start.8 = (f32[3,12,128,128]{3,2,1,0:T(8,128)S(1)}, f32[3,12,128,128]{3,2,1,0:T(8,128)}, u32[]{:S(2)}, u32[]{:S(2)}) collective-permute-start(f32[3,12,128,128]{3,2,1,0:T(8,128)S(1)} %get-tuple-element.51.swept.refs_1_), channel_id=1, source_target_pairs={{0,1},{1,2},{2,3},{4,5},{5,6},{6,7},{8,9},{9,10},{10,11},{12,13},{... | collective-permute-start | bytes 7077896 | tf_op jit(solution)/shard_map/ppermute | solution.py:798
  32.5 14.8 %copy-start.2 = (f32[9,128,128]{2,1,0:T(8,128)}, f32[9,128,128]{2,1,0:T(8,128)S(1)}, u32[]{:S(2)}) copy-start(f32[9,128,128]{2,1,0:T(8,128)S(1)} %collective-permute-done.low.refs_2_) | copy-start | bytes 1769476
  32.5 14.8 %copy-start.3 = (f32[9,128,128]{2,1,0:T(8,128)}, f32[9,128,128]{2,1,0:T(8,128)S(1)}, u32[]{:S(2)}) copy-start(f32[9,128,128]{2,1,0:T(8,128)S(1)} %collective-permute-done.1.high.refs_4_) | copy-start | bytes 1769476
  33.8 13.5 %copy-start.5 = (f32[3,128,128]{2,1,0:T(8,128)}, f32[3,128,128]{2,1,0:T(8,128)S(1)}, u32[]{:S(2)}) copy-start(f32[3,128,128]{2,1,0:T(8,128)S(1)} %get-tuple-element.44.low_end.refs_1_) | copy-start | bytes 589828
  33.8 13.6 %copy-start.6 = (f32[3,128,128]{2,1,0:T(8,128)}, f32[3,128,128]{2,1,0:T(8,128)S(1)}, u32[]{:S(2)}) copy-start(f32[3,128,128]{2,1,0:T(8,128)S(1)} %get-tuple-element.43.high_end.refs_3_) | copy-start | bytes 589828
  33.8 8.9 %collective-permute-start.2 = (f32[3,128,128]{2,1,0:T(8,128)S(1)}, f32[3,128,128]{2,1,0:T(8,128)S(1)}, u32[]{:S(2)}, u32[]{:S(2)}) collective-permute-start(f32[3,128,128]{2,1,0:T(8,128)S(1)} %get-tuple-element.43.high_end.refs_3_), channel_id=1, source_target_pairs={{0,4},{4,8},{8,12},{12,16},{16,20},{20,24},{24,28},{28,0},{1,5},{5... | collective-permute-start | bytes 589832 | tf_op jit(solution)/shard_map/ppermute | solution.py:793
  33.9 11.5 %collective-permute-start.3 = (f32[3,128,128]{2,1,0:T(8,128)S(1)}, f32[3,128,128]{2,1,0:T(8,128)S(1)}, u32[]{:S(2)}, u32[]{:S(2)}) collective-permute-start(f32[3,128,128]{2,1,0:T(8,128)S(1)} %get-tuple-element.44.low_end.refs_1_), channel_id=1, source_target_pairs={{4,0},{8,4},{12,8},{16,12},{20,16},{24,20},{28,24},{0,28},{5,1},{9... | collective-permute-start | bytes 589832 | tf_op jit(solution)/shard_map/ppermute | solution.py:793
  38.1 24.4 %collective-permute-start.6 = (f32[768,128]{1,0:T(8,128)S(1)}, f32[768,128]{1,0:T(8,128)S(1)}, u32[]{:S(2)}, u32[]{:S(2)}) collective-permute-start(f32[768,128]{1,0:T(8,128)S(1)} %get-tuple-element.57), channel_id=1, source_target_pairs={{0,1},{1,2},{2,3},{4,5},{5,6},{6,7},{8,9},{9,10},{10,11},{12,13},{... | collective-permute-start | bytes 1179656 | tf_op jit(solution)/shard_map/ppermute | solution.py:798
  42.7 16.2 %copy-start.7 = (f32[3,128,128]{2,1,0:T(8,128)}, f32[3,128,128]{2,1,0:T(8,128)S(1)}, u32[]{:S(2)}) copy-start(f32[3,128,128]{2,1,0:T(8,128)S(1)} %collective-permute-done.2.low.refs_0_) | copy-start | bytes 589828
  45.4 2.1 %copy-start.8 = (f32[3,128,128]{2,1,0:T(8,128)}, f32[3,128,128]{2,1,0:T(8,128)S(1)}, u32[]{:S(2)}) copy-start(f32[3,128,128]{2,1,0:T(8,128)S(1)} %collective-permute-done.3.high.refs_4_) | copy-start | bytes 589828
  47.4 16.5 %collective-permute-start.4 = (f32[3,128,128]{2,1,0:T(8,128)S(1)}, f32[3,128,128]{2,1,0:T(8,128)S(1)}, u32[]{:S(2)}, u32[]{:S(2)}) collective-permute-start(f32[3,128,128]{2,1,0:T(8,128)S(1)} %get-tuple-element.48.high_end), channel_id=1, source_target_pairs={{0,4},{4,8},{8,12},{12,16},{16,20},{20,24},{24,28},{28,0},{1,5},{5... | collective-permute-start | bytes 589832 | tf_op jit(solution)/shard_map/ppermute | solution.py:793
  47.4 16.4 %collective-permute-start.5 = (f32[3,128,128]{2,1,0:T(8,128)S(1)}, f32[3,128,128]{2,1,0:T(8,128)S(1)}, u32[]{:S(2)}, u32[]{:S(2)}) collective-permute-start(f32[3,128,128]{2,1,0:T(8,128)S(1)} %get-tuple-element.49.low_end), channel_id=1, source_target_pairs={{4,0},{8,4},{12,8},{16,12},{20,16},{24,20},{28,24},{0,28},{5,1},{9... | collective-permute-start | bytes 589832 | tf_op jit(solution)/shard_map/ppermute | solution.py:793
  51.6 12.3 %collective-permute-start.7 = (f32[256,128]{1,0:T(8,128)S(1)}, f32[256,128]{1,0:T(8,128)S(1)}, u32[]{:S(2)}, u32[]{:S(2)}) collective-permute-start(f32[256,128]{1,0:T(8,128)S(1)} %get-tuple-element.58), channel_id=1, source_target_pairs={{0,1},{1,2},{2,3},{4,5},{5,6},{6,7},{8,9},{9,10},{10,11},{12,13},{... | collective-permute-start | bytes 393224 | tf_op jit(solution)/shard_map/ppermute | solution.py:798
  56.6 18.7 %copy-start.11 = (f32[64]{0:T(128)S(1)}, f32[64]{0:T(128)}, u32[]{:S(2)}) copy-start(f32[64]{0:T(128)} %constant.32.clone) | copy-start | bytes 772
  66.7 24.5 %all-to-all-start = ((f32[32,48,128]{2,1,0:T(8,128)}), f32[32,48,128]{2,1,0:T(8,128)}, u32[]{:S(2)}, u32[]{:S(2)}) async-start(f32[32,48,128]{2,1,0:T(8,128)} %bitcast.2), calls=%async_computation | async-start | bytes 1572864 | tf_op jit(solution)/shard_map/all_to_all | solution.py:1066
  71.8 28.4 %collective-permute-start.9 = (f32[3,6,128,128]{3,2,1,0:T(8,128)}, f32[3,6,128,128]{3,2,1,0:T(8,128)}, u32[]{:S(2)}, u32[]{:S(2)}) collective-permute-start(f32[3,6,128,128]{3,2,1,0:T(8,128)} %get-tuple-element.62.refs_0_), channel_id=1, source_target_pairs={{0,1},{1,2},{2,3},{4,5},{5,6},{6,7},{8,9},{9,10},{10,11},{12,13},{... | collective-permute-start | bytes 3538952 | tf_op jit(solution)/shard_map/ppermute | solution.py:798
  96.0 19.4 %all-to-all-start.2 = ((f32[32,32,128]{2,1,0:T(8,128)}), f32[32,32,128]{2,1,0:T(8,128)}, u32[]{:S(2)}, u32[]{:S(2)}) async-start(f32[32,32,128]{2,1,0:T(8,128)} %bitcast.19), calls=%async_computation.2 | async-start | bytes 1048576 | tf_op jit(solution)/shard_map/all_to_all | solution.py:1072
  115.4 22.1 %all-to-all-start.1 = ((f32[32,32,128]{2,1,0:T(8,128)}), f32[32,32,128]{2,1,0:T(8,128)}, u32[]{:S(2)}, u32[]{:S(2)}) async-start(f32[32,32,128]{2,1,0:T(8,128)} %bitcast.18), calls=%async_computation.1 | async-start | bytes 1048576 | tf_op jit(solution)/shard_map/all_to_all | solution.py:1072
  118.9 12.4 %collective-permute-start.10 = (f32[32,32,128]{2,1,0:T(8,128)}, f32[32,32,128]{2,1,0:T(8,128)}, u32[]{:S(2)}, u32[]{:S(2)}) collective-permute-start(f32[32,32,128]{2,1,0:T(8,128)} %all-to-all-done.2), channel_id=1, source_target_pairs={{0,1},{1,2},{2,3},{4,5},{5,6},{6,7},{8,9},{9,10},{10,11},{12,13},{... | collective-permute-start | bytes 1572872 | tf_op jit(solution)/shard_map/ppermute | solution.py:798

commit v5 on v4

--- a/solution.py
+++ b/solution.py
@@ -431,7 +431,7 @@
 
 def interior_kernel(
     group, g_group, is_first, source, z_table, y_table,
-    near, s1_out, s2_out, w_out, uv_end, uv_next, out, g,
+    near, s1_out, s2_out, s2_side, w_out, uv_end, uv_next, out, g,
     held, held_1, held_2, w, uv, sems, out_sems
 ):
     length, size = source.shape[1], source.shape[2]
@@ -459,9 +459,13 @@
             held_1.at[:, plane, rows_all, :], s1_out.at[:, plane - 1], out_sems.at[0, plane]
         )
 
+    sides = (2, 3, length - 4, length - 3)
+
     def s2_copy(plane):
+        inner = plane not in sides
+        target = s2_out.at[:, plane - 4] if inner else s2_side.at[:, sides.index(plane)]
         return pltpu.make_async_copy(
-            held_2.at[:, plane, rows_all, :], s2_out.at[:, plane - 2], out_sems.at[1, plane]
+            held_2.at[:, plane, rows_all, :], target, out_sems.at[1, plane]
         )
 
     def phase_one(plane, carry):
@@ -490,10 +494,11 @@
 
         sweep_two_plane(held_1, plane, get_w, put_s2, uv, plane // 2)
         wrap_rows(held_2, plane, 3)
+        return carry
+
+    lax.fori_loop(2, length - 2, phase_two, 0)
+    for plane in range(2, length - 2):
         s2_copy(plane).start()
-        return carry
-
-    lax.fori_loop(2, length - 2, phase_two, 0)
     tails = []
     for k, plane in enumerate((0, 1, length - 2, length - 1)):
         tails.append(
@@ -530,12 +535,9 @@
         s1_copy(plane).wait()
         return carry
 
-    def finish_two(plane, carry):
+    lax.fori_loop(1, length - 1, finish_one, 0)
+    for plane in range(2, length - 2):
         s2_copy(plane).wait()
-        return carry
-
-    lax.fori_loop(1, length - 1, finish_one, 0)
-    lax.fori_loop(2, length - 2, finish_two, 0)
     for copy in tails:
         copy.wait()
 
@@ -602,15 +604,14 @@
 
 
 def middle_kernel(
-    group, swept, low_end, nexts, high_end, uv_in, uv_next, f, z_table, y_table,
+    group, swept, side, low_end, nexts, high_end, uv_in, uv_next, f, z_table, y_table,
     uv, out, held, near, sems
 ):
     count, size = swept.shape[1], swept.shape[2]
-    planes = (count + 4) // 2
+    planes = (count + 8) // 2
     rows_all = pl.ds(pad, size)
-    sources = [low_end, nexts.at[:, 0], swept.at[:, 0], swept.at[:, 1], swept.at[:, 2]]
-    sources += [swept.at[:, count - 3], swept.at[:, count - 2], swept.at[:, count - 1]]
-    sources += [nexts.at[:, 1], high_end]
+    sources = [low_end, nexts.at[:, 0], side.at[:, 0], side.at[:, 1], swept.at[:, 0]]
+    sources += [swept.at[:, count - 1], side.at[:, 2], side.at[:, 3], nexts.at[:, 1], high_end]
     start_all([
         pltpu.make_async_copy(ref, held.at[:, slot, rows_all, :], sems.at[slot])
         for slot, ref in enumerate(sources)
@@ -632,26 +633,32 @@
 
 
 def end_three_kernel(
-    group, g_group, end_group, low, low_end, nexts, high_end, high, uv_in, f, g, g_end,
-    z_table, y_table, pack, sent, out, held, uv, sems, out_sems
+    group, g_group, end_group, side, low, low_end, nexts, high_end, high, uv_in, f, g, g_end,
+    z_table, y_table, pack, sent, out, held, side_held, uv, sems, out_sems
 ):
     size = held.shape[2] - 2 * pad
     rows_all = pl.ds(pad, size)
     blocks = out.shape[0] // group
     planes = g.shape[0] // blocks // 3
     sources = [low, low_end, nexts.at[:, 0], nexts.at[:, 1], high_end, high]
+    side_in = pltpu.make_async_copy(side, side_held, sems.at[6])
+    side_in.start()
     start_all([
         pltpu.make_async_copy(ref, held.at[:, slot, rows_all, :], sems.at[slot])
         for slot, ref in enumerate(sources)
     ])
     packing = [
-        pltpu.make_async_copy(held.at[:, slot, rows_all, :], pack.at[:, slot], out_sems.at[slot])
+        pltpu.make_async_copy(
+            held.at[:, slot, rows_all, :], pack.at[:, (0, 1, 2, 7, 8, 9)[slot]], out_sems.at[slot]
+        )
         for slot in range(6)
     ]
+    packing.append(pltpu.make_async_copy(side_held, pack.at[:, 3:7], out_sems.at[7]))
     uv[...] = uv_in[...]
     out[...] = f[...]
     for slot in (1, 4):
         wrap_rows(held, slot, 3)
+    side_in.wait()
     for copy in packing:
         copy.start()
     last_rhs_one(held, 1, uv, 0)
@@ -918,12 +925,13 @@
         name="edges",
     )(fields)
     low, high = neighbours(low, high)
-    near, swept_1, swept_2, w_next, uv_end, uv_next, f, g = pl.pallas_call(
+    near, swept_1, swept_2, side_2, w_next, uv_end, uv_next, f, g = pl.pallas_call(
         functools.partial(interior_kernel, group, g_group),
         out_shape=(
             struct((9, 4, *plane)),
             struct((3, length - 2, *plane)),
-            struct((3, length - 4, *plane)),
+            struct((3, length - 8, *plane)),
+            struct((3, 4, *plane)),
             struct((3, 2, *plane)),
             struct((6, 2, *plane)),
             struct((6, 2, *plane)),
@@ -931,7 +939,7 @@
             struct((blocks * g_group, lanes)),
         ),
         in_specs=[scalar, hbm, vmem, vmem],
-        out_specs=(hbm,) * 6 + (vmem,) * 2,
+        out_specs=(hbm,) * 7 + (vmem,) * 2,
         scratch_shapes=[
             held(9, length),
             held(3, length),
@@ -981,34 +989,35 @@
     uv_end, f = pl.pallas_call(
         functools.partial(middle_kernel, group),
         out_shape=(struct((6, 2, *plane)), struct((blocks * group, lanes))),
-        in_specs=[hbm] + [anywhere] * 3 + [vmem] * 5,
+        in_specs=[hbm, hbm] + [anywhere] * 3 + [vmem] * 5,
         out_specs=(vmem,) * 2,
         scratch_shapes=[held(3, 10), pltpu.VMEM((6, 2, *plane), f32), sems(10)],
         compiler_params=params(16384),
         name="middle",
-    )(swept_2, low_end_2, next_2, high_end_2, uv_end, uv_next, f, z_table, y_table)
+    )(swept_2, side_2, low_end_2, next_2, high_end_2, uv_end, uv_next, f, z_table, y_table)
     pack, sources = pl.pallas_call(
         functools.partial(end_three_kernel, group, g_group, end_group),
-        out_shape=(struct((3, 6, *plane)), struct((blocks * group, lanes))),
-        in_specs=[anywhere] * 5 + [vmem] * 6,
+        out_shape=(struct((3, 10, *plane)), struct((blocks * group, lanes))),
+        in_specs=[hbm] + [anywhere] * 5 + [vmem] * 6,
         out_specs=(hbm, hbm),
         scratch_shapes=[
             pltpu.VMEM((blocks * group, lanes), f32),
             held(3, 6),
+            pltpu.VMEM((3, 4, *plane), f32),
             pltpu.VMEM((6, 2, *plane), f32),
-            sems(6),
             sems(7),
+            sems(8),
         ],
         compiler_params=params(16384),
         name="end_three",
     )(
-        low_2, low_end_2, next_2, high_end_2, high_2, uv_end, f,
+        side_2, low_2, low_end_2, next_2, high_end_2, high_2, uv_end, f,
         g_moved, later_interval(g_end), z_table, y_table
     )
     inner_1 = [(2, p) for p in range(length - 2)]
-    inner_2 = [(1, p) for p in range(length - 4)]
+    inner_2 = [(1, p) for p in range(length - 8)]
     layout_1 = [(0, None), (1, None)] + inner_1 + [(3, None), (4, None)]
-    layout_2 = [(0, 0), (0, 1), (0, 2)] + inner_2 + [(0, 3), (0, 4), (0, 5)]
+    layout_2 = [(0, p) for p in range(5)] + inner_2 + [(0, p) for p in range(5, 10)]
     layout_0 = [(2, None)] + [(3, p) for p in range(length)] + [(4, None)]
     return (
         sources,
@@ -1052,7 +1061,7 @@
     rates = 1.0 / (1.0 + half_step * coarse_viscosity * (4.0 / (2.0 * 2.0)) * total)
 
     is_first = tm_first.astype(f32).reshape(1)
-    sweep = sweep_split if length >= 10 else sweep_whole
+    sweep = sweep_split if length >= 12 else sweep_whole
     moved_at = 1
     sources, one, two, carried, zero = sweep(fields, is_first, z_table, y_table, blocks)
     group = round_up(6 * planes, 8)

time: 145 us -> 142 us (0.979)
  local copies, waits for them, and re-layouts: 2.43 us -> 0.75 us
  starting transfers between devices: 46.6 us -> 45.1 us
    ppermute x5, waiting for transfers between devices: 7.46 us -> 23.7 us  [later_interval(): return lax.ppermute(value, 'tm', [(i, i + 1) for i in range(count - 1)])]
    all_to_all x2, waiting for transfers between devices: 15.2 us -> 2.96 us  [to_planes(): value = lax.all_to_all(value, both, split_axis=0, concat_axis=0, tiled=True)]
    all_to_all x1, waiting for transfers between devices: 15.3 us -> 6.48 us  [to_columns(): value = lax.all_to_all(value, both, split_axis=0, concat_axis=0, tiled=True)]
    ppermute x3, waiting for transfers between devices: 0.01 us -> 3.36 us  [neighbours(): lax.ppermute(high_plane, 'space', up)]
    ppermute x3, waiting for transfers between devices: 2.63 us -> 4.61 us  [neighbours(): lax.ppermute(low_plane, 'space', down)]
    unnamed x24 -> x22, local copies, waits for them, and re-layouts: 1.73 us -> 0.05 us
    ppermute x5, starting transfers between devices: 21 us -> 19.3 us  [later_interval(): return lax.ppermute(value, 'tm', [(i, i + 1) for i in range(count - 1)])]
  transfers between devices with their start and end apart: 14 -> 14, of which waited for: 6 -> 8; matrix products, arithmetic and copies ran while one was open for 1% -> 1% of each run, Pallas kernels for 31% -> 30%
where the time goes in v5:
time: 142 us; the launch traced here: 141 us
  Pallas kernels  52.3 us (37%)
  starting transfers between devices  45.1 us (32%)
  waiting for transfers between devices  41.1 us (29%)
    ppermute x5, waiting for transfers between devices, later_interval(): return lax.ppermute(value, 'tm', [(i, i + 1) for i in range(count - 1)])  23.7 us
    ppermute x5, starting transfers between devices, later_interval(): return lax.ppermute(value, 'tm', [(i, i + 1) for i in range(count - 1)])  19.3 us
    pallas_call x3, Pallas kernels, corrected(): pl.pallas_call(functools.partial(corrected_kernel, node, group, layouts,...  18.5 us
    pallas_call x1, Pallas kernels, sweep_split(): pl.pallas_call(functools.partial(interior_kernel, group, g_group), out_sh...  18.5 us
    ppermute x3, starting transfers between devices, neighbours(): lax.ppermute(low_plane, 'space', down)  11.1 us
    all_to_all x2, starting transfers between devices, to_planes(): value = lax.all_to_all(value, both, split_axis=0, concat_axis=0, tiled=True)  7.53 us
    all_to_all x1, waiting for transfers between devices, to_columns(): value = lax.all_to_all(value, both, split_axis=0, concat_axis=0, tiled=True)  6.48 us
    pallas_call x1, Pallas kernels, per_device(): pl.pallas_call(functools.partial(solve_kernel, peers, intervals, planes,...  4.71 us
  transfers between devices with their start and end apart: 14, of which 8 were waited for; matrix products, arithmetic and copies ran while one was open for 1% of the time, Pallas kernels for 30%

profile of v5, /device:TPU:1, one launch (start us, length us, event | category | flops | bytes accessed | tf_op | source)
XLA Modules:
  0.0 141.0 jit_solution(12694490742014444214)
XLA Ops:
  0.7 2.3 %edges.1 = (f32[9,128,128]{2,1,0:T(8,128)}, f32[9,128,128]{2,1,0:T(8,128)}) custom-call(f32[9,16,128,128]{3,2,1,0:T(8,128)} %bitcast.13), custom_call_target="tpu_custom_call" | custom-call | tf_op jit(solution)/shard_map/edges/pallas_call | solution.py:918
  3.0 2.1 %collective-permute-start = (f32[9,128,128]{2,1,0:T(8,128)}, f32[9,128,128]{2,1,0:T(8,128)S(1)}, u32[]{:S(2)}, u32[]{:S(2)}) collective-permute-start(f32[9,128,128]{2,1,0:T(8,128)} %get-tuple-element.42), channel_id=1, source_target_pairs={{0,4},{4,8},{8,12},{12,16},{16,20},{20,24},{24,28},{28,0},{1,5},{5... | collective-permute-start | bytes 1769480 | tf_op jit(solution)/shard_map/ppermute | solution.py:800
  5.1 3.1 %collective-permute-start.1 = (f32[9,128,128]{2,1,0:T(8,128)}, f32[9,128,128]{2,1,0:T(8,128)S(1)}, u32[]{:S(2)}, u32[]{:S(2)}) collective-permute-start(f32[9,128,128]{2,1,0:T(8,128)} %get-tuple-element.43), channel_id=1, source_target_pairs={{4,0},{8,4},{12,8},{16,12},{20,16},{24,20},{28,24},{0,28},{5,1},{9... | collective-permute-start | bytes 1769480 | tf_op jit(solution)/shard_map/ppermute | solution.py:800
  8.2 18.5 %interior.1 = (f32[9,4,128,128]{3,2,1,0:T(8,128)S(1)}, f32[3,14,128,128]{3,2,1,0:T(8,128)S(1)}, f32[3,8,128,128]{3,2,1,0:T(8,128)S(1)}, f32[3,4,128,128]{3,2,1,0...) custom-call(f32[1]{0:T(128)} %bitcast.is_first, ...), custom_call_target="tpu_custom_call" | custom-call | flops 4000000000 | bytes 60000000 | tf_op jit(solution)/shard_map/interior/pallas_call | solution.py:928
  26.7 3.4 %collective-permute-done.low.refs_2_ = f32[9,128,128]{2,1,0:T(8,128)S(1)} collective-permute-done((f32[9,128,128]{2,1,0:T(8,128)}, f32[9,128,128]{2,1,0:T(8,128)S(1)}, u32[]{:S(2)}, u32[]{:S(2)}) %collective-permute-start) | collective-permute-done | bytes 589856 | tf_op jit(solution)/shard_map/ppermute | solution.py:800
  30.0 1.8 %collective-permute-done.1.high.refs_4_ = f32[9,128,128]{2,1,0:T(8,128)S(1)} collective-permute-done((f32[9,128,128]{2,1,0:T(8,128)}, f32[9,128,128]{2,1,0:T(8,128)S(1)}, u32[]{:S(2)}, u32[]{:S(2)}) %collective-permute-start.1) | collective-permute-done | bytes 589856 | tf_op jit(solution)/shard_map/ppermute | solution.py:800
  31.8 1.3 end_one.1
  33.5 3.8 %collective-permute-start.3 = (f32[3,128,128]{2,1,0:T(8,128)S(1)}, f32[3,128,128]{2,1,0:T(8,128)S(1)}, u32[]{:S(2)}, u32[]{:S(2)}) collective-permute-start(f32[3,128,128]{2,1,0:T(8,128)S(1)} %get-tuple-element.46.low_end.refs_1_), channel_id=1, source_target_pairs={{4,0},{8,4},{12,8},{16,12},{20,16},{24,20},{28,24},{0,28},{5,1},{9... | collective-permute-start | bytes 589832 | tf_op jit(solution)/shard_map/ppermute | solution.py:800
  37.4 5.4 %collective-permute-start.6 = (f32[768,128]{1,0:T(8,128)S(1)}, f32[768,128]{1,0:T(8,128)S(1)}, u32[]{:S(2)}, u32[]{:S(2)}) collective-permute-start(f32[768,128]{1,0:T(8,128)S(1)} %get-tuple-element.59), channel_id=1, source_target_pairs={{0,1},{1,2},{2,3},{4,5},{5,6},{6,7},{8,9},{9,10},{10,11},{12,13},{... | collective-permute-start | bytes 1179656 | tf_op jit(solution)/shard_map/ppermute | solution.py:805
  42.8 2.8 %collective-permute-done.3.high.refs_4_ = f32[3,128,128]{2,1,0:T(8,128)S(1)} collective-permute-done((f32[3,128,128]{2,1,0:T(8,128)S(1)}, f32[3,128,128]{2,1,0:T(8,128)S(1)}, u32[]{:S(2)}, u32[]{:S(2)}) %collective-permute-start.3) | collective-permute-done | bytes 196640 | tf_op jit(solution)/shard_map/ppermute | solution.py:800
  45.6 1.9 %end_two.1 = (f32[3,128,128]{2,1,0:T(8,128)S(1)}, f32[3,128,128]{2,1,0:T(8,128)S(1)}, f32[3,2,128,128]{3,2,1,0:T(8,128)S(1)}, f32[6,2,128,128]{3,2,1,0:T(8,128)S(1)}, f32[256,128]{1,0:T(8,128)S(1)}) custom-call(f32[3,14,128,128]{3,2,1,0:T(8,128)S(1)} %get-tuple-element.40.swept.refs_2_, f32[3,128,128]{2,1,0:T(8,128)S(1)} %collective-permute-done.2.low.refs_0_, ...), custom_call_target="tpu_custom_call" | custom-call | tf_op jit(solution)/shard_map/end_two/pallas_call | solution.py:973
  47.7 4.1 %collective-permute-start.5 = (f32[3,128,128]{2,1,0:T(8,128)S(1)}, f32[3,128,128]{2,1,0:T(8,128)S(1)}, u32[]{:S(2)}, u32[]{:S(2)}) collective-permute-start(f32[3,128,128]{2,1,0:T(8,128)S(1)} %get-tuple-element.51.low_end), channel_id=1, source_target_pairs={{4,0},{8,4},{12,8},{16,12},{20,16},{24,20},{28,24},{0,28},{5,1},{9... | collective-permute-start | bytes 589832 | tf_op jit(solution)/shard_map/ppermute | solution.py:800
  51.8 4.7 %collective-permute-start.7 = (f32[256,128]{1,0:T(8,128)S(1)}, f32[256,128]{1,0:T(8,128)S(1)}, u32[]{:S(2)}, u32[]{:S(2)}) collective-permute-start(f32[256,128]{1,0:T(8,128)S(1)} %get-tuple-element.60), channel_id=1, source_target_pairs={{0,1},{1,2},{2,3},{4,5},{5,6},{6,7},{8,9},{9,10},{10,11},{12,13},{... | collective-permute-start | bytes 393224 | tf_op jit(solution)/shard_map/ppermute | solution.py:805
  56.5 1.9 %collective-permute-start.8 = (f32[3,8,128,128]{3,2,1,0:T(8,128)S(1)}, f32[3,8,128,128]{3,2,1,0:T(8,128)}, u32[]{:S(2)}, u32[]{:S(2)}) collective-permute-start(f32[3,8,128,128]{3,2,1,0:T(8,128)S(1)} %get-tuple-element.53.swept.refs_1_), channel_id=1, source_target_pairs={{0,1},{1,2},{2,3},{4,5},{5,6},{6,7},{8,9},{9,10},{10,11},{12,13},{... | collective-permute-start | bytes 4718600 | tf_op jit(solution)/shard_map/ppermute | solution.py:805
  58.5 2.3 %middle.1 = (f32[6,2,128,128]{3,2,1,0:T(8,128)S(1)}, f32[1536,128]{1,0:T(8,128)S(1)}) custom-call(f32[3,8,128,128]{3,2,1,0:T(8,128)S(1)} %get-tuple-element.53.swept.refs_1_, f32[3,4,128,128]{3,2,1,0:T(8,128)S(1)} %get-tuple-element.39.side, f32[3,128,128]{2,1,0:T(8,128)S(1)} %get-tuple-element.51.low_end, f32[3,2,128,128]{3,2,1,0:T(8,128)S(1)} %get-tuple-element.52.nexts, ...), custom_call_target="tpu_custom_call" | custom-call | tf_op jit(solution)/shard_map/middle/pallas_call | solution.py:989
  60.9 2.8 %end_three.1 = (f32[3,10,128,128]{3,2,1,0:T(8,128)}, f32[1536,128]{1,0:T(8,128)}) custom-call(f32[3,4,128,128]{3,2,1,0:T(8,128)S(1)} %get-tuple-element.39.side, f32[3,128,128]{2,1,0:T(8,128)S(1)} %collective-permute-done.4.low, f32[3,128,128]{2,1,0:T(8,128)S(1)} %get-tuple-element.51.low_end, f32[3,2,128,128]{3,2,1,0:T(8,128)S(1)} %get-tuple-element.52.nexts, ...), custom_call_target="tpu_custom_call" | custom-call | tf_op jit(solution)/shard_map/end_three/pallas_call | solution.py:998
  63.7 4.6 %all-to-all-start = ((f32[32,48,128]{2,1,0:T(8,128)}), f32[32,48,128]{2,1,0:T(8,128)}, u32[]{:S(2)}, u32[]{:S(2)}) async-start(f32[32,48,128]{2,1,0:T(8,128)} %bitcast.2), calls=%async_computation | async-start | bytes 1572864 | tf_op jit(solution)/shard_map/all_to_all | solution.py:1075
  68.3 3.5 %collective-permute-start.9 = (f32[3,10,128,128]{3,2,1,0:T(8,128)}, f32[3,10,128,128]{3,2,1,0:T(8,128)}, u32[]{:S(2)}, u32[]{:S(2)}) collective-permute-start(f32[3,10,128,128]{3,2,1,0:T(8,128)} %get-tuple-element.64.refs_0_), channel_id=1, source_target_pairs={{0,1},{1,2},{2,3},{4,5},{5,6},{6,7},{8,9},{9,10},{10,11},{12,13},{... | collective-permute-start | bytes 5898248 | tf_op jit(solution)/shard_map/ppermute | solution.py:805
  71.8 0.7 dynamic-slice_bitcast_fusion
  72.5 0.7 add_divide_fusion.inverse_in
  73.2 8.9 %collective-permute-done.8.refs_1_ = f32[3,8,128,128]{3,2,1,0:T(8,128)} collective-permute-done((f32[3,8,128,128]{3,2,1,0:T(8,128)S(1)}, f32[3,8,128,128]{3,2,1,0:T(8,128)}, u32[]{:S(2)}, u32[]{:S(2)}) %collective-permute-start.8) | collective-permute-done | bytes 1572896 | tf_op jit(solution)/shard_map/ppermute | solution.py:805
  82.1 6.5 %all-to-all-done = f32[32,48,128]{2,1,0:T(8,128)} async-done(((f32[32,48,128]{2,1,0:T(8,128)}), f32[32,48,128]{2,1,0:T(8,128)}, u32[]{:S(2)}, u32[]{:S(2)}) %all-to-all-start) | async-done | bytes 786464 | tf_op jit(solution)/shard_map/all_to_all | solution.py:1075
  88.6 4.7 %solve.1 = (f32[1024,128]{1,0:T(8,128)}, f32[1024,128]{1,0:T(8,128)}) custom-call(f32[1536,128]{1,0:T(8,128)} %bitcast.3.values, f32[64,128]{1,0:T(8,128)} %add_divide_fusion.inverse_in, bf16[144,192]{1,0:T(8,128)(2,1)} %constant.35.clone.table_in), custom_call_target="tpu_custom_call" | custom-call | tf_op jit(solution)/shard_map/solve/pallas_call | solution.py:1094
  93.3 4.1 %all-to-all-start.2 = ((f32[32,32,128]{2,1,0:T(8,128)}), f32[32,32,128]{2,1,0:T(8,128)}, u32[]{:S(2)}, u32[]{:S(2)}) async-start(f32[32,32,128]{2,1,0:T(8,128)} %bitcast.19), calls=%async_computation.2 | async-start | bytes 1048576 | tf_op jit(solution)/shard_map/all_to_all | solution.py:1081
  97.4 12.3 %collective-permute-done.9.refs_0_ = f32[3,10,128,128]{3,2,1,0:T(8,128)} collective-permute-done((f32[3,10,128,128]{3,2,1,0:T(8,128)}, f32[3,10,128,128]{3,2,1,0:T(8,128)}, u32[]{:S(2)}, u32[]{:S(2)}) %collective-permute-start.9) | collective-permute-done | bytes 1966112 | tf_op jit(solution)/shard_map/ppermute | solution.py:805
  109.7 3.0 %all-to-all-done.2 = f32[32,32,128]{2,1,0:T(8,128)} async-done(((f32[32,32,128]{2,1,0:T(8,128)}), f32[32,32,128]{2,1,0:T(8,128)}, u32[]{:S(2)}, u32[]{:S(2)}) %all-to-all-start.2) | async-done | bytes 524320 | tf_op jit(solution)/shard_map/all_to_all | solution.py:1081
  112.6 3.5 %all-to-all-start.1 = ((f32[32,32,128]{2,1,0:T(8,128)}), f32[32,32,128]{2,1,0:T(8,128)}, u32[]{:S(2)}, u32[]{:S(2)}) async-start(f32[32,32,128]{2,1,0:T(8,128)} %bitcast.18), calls=%async_computation.1 | async-start | bytes 1048576 | tf_op jit(solution)/shard_map/all_to_all | solution.py:1081
  116.1 3.7 %collective-permute-start.10 = (f32[32,32,128]{2,1,0:T(8,128)}, f32[32,32,128]{2,1,0:T(8,128)}, u32[]{:S(2)}, u32[]{:S(2)}) collective-permute-start(f32[32,32,128]{2,1,0:T(8,128)} %all-to-all-done.2), channel_id=1, source_target_pairs={{0,1},{1,2},{2,3},{4,5},{5,6},{6,7},{8,9},{9,10},{10,11},{12,13},{... | collective-permute-start | bytes 1572872 | tf_op jit(solution)/shard_map/ppermute | solution.py:805
  119.9 6.1 %corrected_2.1 = (f32[3,3,16,128,128]{4,3,2,1,0:T(8,128)}, bf16[3,3,16,128,128]{4,3,2,1,0:T(8,128)(2,1)}) custom-call(f32[1]{0:T(128)} %bitcast.is_first, f32[1024,128]{1,0:T(8,128)} %bitcast.9.spectra, bf16[512,256]{1,0:T(8,128)(2,1)} %constant.36.clone.table, f32[3,10,128,128]{3,2,1,0:T(8,128)} %get-tuple-element.64.refs_0_, f32[3,8,128,128]{3,2,1,0:T(8,128)} %copy-done.1), custom_call_target="tpu_custom_call" | custom-call | tf_op jit(solution)/shard_map/corrected_2/pallas_call | solution.py:819
  126.0 2.5 %collective-permute-done.10 = f32[32,32,128]{2,1,0:T(8,128)} collective-permute-done((f32[32,32,128]{2,1,0:T(8,128)}, f32[32,32,128]{2,1,0:T(8,128)}, u32[]{:S(2)}, u32[]{:S(2)}) %collective-permute-start.10) | collective-permute-done | bytes 524320 | tf_op jit(solution)/shard_map/ppermute | solution.py:805
  128.5 6.2 %corrected_0.1 = (f32[3,3,16,128,128]{4,3,2,1,0:T(8,128)}, bf16[3,3,16,128,128]{4,3,2,1,0:T(8,128)(2,1)}) custom-call(f32[1]{0:T(128)} %bitcast.is_first, f32[1024,128]{1,0:T(8,128)} %bitcast.8.spectra, bf16[512,256]{1,0:T(8,128)(2,1)} %constant.36.clone.table, ...), custom_call_target="tpu_custom_call", output_to_operand_aliasing={{0}: (8, {}), {1}: (9, {})} | custom-call | tf_op jit(solution)/shard_map/corrected_0/pallas_call | solution.py:819
  134.7 6.1 %corrected_1.1 = (f32[3,3,16,128,128]{4,3,2,1,0:T(8,128)}, bf16[3,3,16,128,128]{4,3,2,1,0:T(8,128)(2,1)}) custom-call(f32[1]{0:T(128)} %bitcast.is_first, f32[1024,128]{1,0:T(8,128)} %bitcast.6.spectra, bf16[512,256]{1,0:T(8,128)(2,1)} %constant.36.clone.table, f32[3,128,128]{2,1,0:T(8,128)} %copy-done.7, ...), custom_call_target="tpu_custom_call", output_to_operand_aliasing={{0}: (8, {}), {1}: (9, {})} | custom-call | tf_op jit(solution)/shard_map/corrected_1/pallas_call | solution.py:819
  (30 shorter events, 0.5 us)
Async XLA Ops:
  0.6 7.6 %copy-start.4 = (bf16[768,128]{1,0:T(8,128)(2,1)S(1)}, bf16[768,128]{1,0:T(8,128)(2,1)}, u32[]{:S(2)}) copy-start(bf16[768,128]{1,0:T(8,128)(2,1)} %constant.33.clone.z_table) | copy-start | bytes 589828
  0.6 7.6 %copy-start.9 = (bf16[64,192]{1,0:T(8,128)(2,1)S(1)}, bf16[64,192]{1,0:T(8,128)(2,1)}, u32[]{:S(2)}) copy-start(bf16[64,192]{1,0:T(8,128)(2,1)} %constant.34.clone.y_table) | copy-start | bytes 73732
  3.0 27.1 %collective-permute-start = (f32[9,128,128]{2,1,0:T(8,128)}, f32[9,128,128]{2,1,0:T(8,128)S(1)}, u32[]{:S(2)}, u32[]{:S(2)}) collective-permute-start(f32[9,128,128]{2,1,0:T(8,128)} %get-tuple-element.42), channel_id=1, source_target_pairs={{0,4},{4,8},{8,12},{12,16},{16,20},{20,24},{24,28},{28,0},{1,5},{5... | collective-permute-start | bytes 1769480 | tf_op jit(solution)/shard_map/ppermute | solution.py:800
  5.1 26.7 %collective-permute-start.1 = (f32[9,128,128]{2,1,0:T(8,128)}, f32[9,128,128]{2,1,0:T(8,128)S(1)}, u32[]{:S(2)}, u32[]{:S(2)}) collective-permute-start(f32[9,128,128]{2,1,0:T(8,128)} %get-tuple-element.43), channel_id=1, source_target_pairs={{4,0},{8,4},{12,8},{16,12},{20,16},{24,20},{28,24},{0,28},{5,1},{9... | collective-permute-start | bytes 1769480 | tf_op jit(solution)/shard_map/ppermute | solution.py:800
  26.7 20.9 %copy-start = (f32[3,14,128,128]{3,2,1,0:T(8,128)}, f32[3,14,128,128]{3,2,1,0:T(8,128)S(1)}, u32[]{:S(2)}) copy-start(f32[3,14,128,128]{3,2,1,0:T(8,128)S(1)} %get-tuple-element.40.swept.refs_2_) | copy-start | bytes 8257540
  26.7 31.8 %copy-start.1 = (f32[3,8,128,128]{3,2,1,0:T(8,128)}, f32[3,8,128,128]{3,2,1,0:T(8,128)S(1)}, u32[]{:S(2)}) copy-start(f32[3,8,128,128]{3,2,1,0:T(8,128)S(1)} %get-tuple-element.53.swept.refs_1_) | copy-start | bytes 4718596
  30.0 17.5 %copy-start.2 = (f32[9,128,128]{2,1,0:T(8,128)}, f32[9,128,128]{2,1,0:T(8,128)S(1)}, u32[]{:S(2)}) copy-start(f32[9,128,128]{2,1,0:T(8,128)S(1)} %collective-permute-done.low.refs_2_) | copy-start | bytes 1769476
  31.8 15.8 %copy-start.3 = (f32[9,128,128]{2,1,0:T(8,128)}, f32[9,128,128]{2,1,0:T(8,128)S(1)}, u32[]{:S(2)}) copy-start(f32[9,128,128]{2,1,0:T(8,128)S(1)} %collective-permute-done.1.high.refs_4_) | copy-start | bytes 1769476
  33.1 23.4 %copy-start.5 = (f32[3,128,128]{2,1,0:T(8,128)}, f32[3,128,128]{2,1,0:T(8,128)S(1)}, u32[]{:S(2)}) copy-start(f32[3,128,128]{2,1,0:T(8,128)S(1)} %get-tuple-element.46.low_end.refs_1_) | copy-start | bytes 589828
  33.1 23.4 %copy-start.6 = (f32[3,128,128]{2,1,0:T(8,128)}, f32[3,128,128]{2,1,0:T(8,128)S(1)}, u32[]{:S(2)}) copy-start(f32[3,128,128]{2,1,0:T(8,128)S(1)} %get-tuple-element.45.high_end.refs_3_) | copy-start | bytes 589828
  33.1 9.6 %collective-permute-start.2 = (f32[3,128,128]{2,1,0:T(8,128)S(1)}, f32[3,128,128]{2,1,0:T(8,128)S(1)}, u32[]{:S(2)}, u32[]{:S(2)}) collective-permute-start(f32[3,128,128]{2,1,0:T(8,128)S(1)} %get-tuple-element.45.high_end.refs_3_), channel_id=1, source_target_pairs={{0,4},{4,8},{8,12},{12,16},{16,20},{20,24},{24,28},{28,0},{1,5},{5... | collective-permute-start | bytes 589832 | tf_op jit(solution)/shard_map/ppermute | solution.py:800
  33.5 12.1 %collective-permute-start.3 = (f32[3,128,128]{2,1,0:T(8,128)S(1)}, f32[3,128,128]{2,1,0:T(8,128)S(1)}, u32[]{:S(2)}, u32[]{:S(2)}) collective-permute-start(f32[3,128,128]{2,1,0:T(8,128)S(1)} %get-tuple-element.46.low_end.refs_1_), channel_id=1, source_target_pairs={{4,0},{8,4},{12,8},{16,12},{20,16},{24,20},{28,24},{0,28},{5,1},{9... | collective-permute-start | bytes 589832 | tf_op jit(solution)/shard_map/ppermute | solution.py:800
  37.4 23.5 %collective-permute-start.6 = (f32[768,128]{1,0:T(8,128)S(1)}, f32[768,128]{1,0:T(8,128)S(1)}, u32[]{:S(2)}, u32[]{:S(2)}) collective-permute-start(f32[768,128]{1,0:T(8,128)S(1)} %get-tuple-element.59), channel_id=1, source_target_pairs={{0,1},{1,2},{2,3},{4,5},{5,6},{6,7},{8,9},{9,10},{10,11},{12,13},{... | collective-permute-start | bytes 1179656 | tf_op jit(solution)/shard_map/ppermute | solution.py:805
  42.8 18.0 %copy-start.7 = (f32[3,128,128]{2,1,0:T(8,128)}, f32[3,128,128]{2,1,0:T(8,128)S(1)}, u32[]{:S(2)}) copy-start(f32[3,128,128]{2,1,0:T(8,128)S(1)} %collective-permute-done.2.low.refs_0_) | copy-start | bytes 589828
  45.6 12.8 %copy-start.8 = (f32[3,128,128]{2,1,0:T(8,128)}, f32[3,128,128]{2,1,0:T(8,128)S(1)}, u32[]{:S(2)}) copy-start(f32[3,128,128]{2,1,0:T(8,128)S(1)} %collective-permute-done.3.high.refs_4_) | copy-start | bytes 589828
  47.6 13.2 %collective-permute-start.4 = (f32[3,128,128]{2,1,0:T(8,128)S(1)}, f32[3,128,128]{2,1,0:T(8,128)S(1)}, u32[]{:S(2)}, u32[]{:S(2)}) collective-permute-start(f32[3,128,128]{2,1,0:T(8,128)S(1)} %get-tuple-element.50.high_end), channel_id=1, source_target_pairs={{0,4},{4,8},{8,12},{12,16},{16,20},{20,24},{24,28},{28,0},{1,5},{5... | collective-permute-start | bytes 589832 | tf_op jit(solution)/shard_map/ppermute | solution.py:800
  47.7 13.2 %collective-permute-start.5 = (f32[3,128,128]{2,1,0:T(8,128)S(1)}, f32[3,128,128]{2,1,0:T(8,128)S(1)}, u32[]{:S(2)}, u32[]{:S(2)}) collective-permute-start(f32[3,128,128]{2,1,0:T(8,128)S(1)} %get-tuple-element.51.low_end), channel_id=1, source_target_pairs={{4,0},{8,4},{12,8},{16,12},{20,16},{24,20},{28,24},{0,28},{5,1},{9... | collective-permute-start | bytes 589832 | tf_op jit(solution)/shard_map/ppermute | solution.py:800
  51.8 9.0 %collective-permute-start.7 = (f32[256,128]{1,0:T(8,128)S(1)}, f32[256,128]{1,0:T(8,128)S(1)}, u32[]{:S(2)}, u32[]{:S(2)}) collective-permute-start(f32[256,128]{1,0:T(8,128)S(1)} %get-tuple-element.60), channel_id=1, source_target_pairs={{0,1},{1,2},{2,3},{4,5},{5,6},{6,7},{8,9},{9,10},{10,11},{12,13},{... | collective-permute-start | bytes 393224 | tf_op jit(solution)/shard_map/ppermute | solution.py:805
  56.5 25.6 %collective-permute-start.8 = (f32[3,8,128,128]{3,2,1,0:T(8,128)S(1)}, f32[3,8,128,128]{3,2,1,0:T(8,128)}, u32[]{:S(2)}, u32[]{:S(2)}) collective-permute-start(f32[3,8,128,128]{3,2,1,0:T(8,128)S(1)} %get-tuple-element.53.swept.refs_1_), channel_id=1, source_target_pairs={{0,1},{1,2},{2,3},{4,5},{5,6},{6,7},{8,9},{9,10},{10,11},{12,13},{... | collective-permute-start | bytes 4718600 | tf_op jit(solution)/shard_map/ppermute | solution.py:805
  58.5 14.0 %copy-start.10 = (f32[64]{0:T(128)S(1)}, f32[64]{0:T(128)}, u32[]{:S(2)}) copy-start(f32[64]{0:T(128)} %constant.32.clone) | copy-start | bytes 772
  63.7 24.9 %all-to-all-start = ((f32[32,48,128]{2,1,0:T(8,128)}), f32[32,48,128]{2,1,0:T(8,128)}, u32[]{:S(2)}, u32[]{:S(2)}) async-start(f32[32,48,128]{2,1,0:T(8,128)} %bitcast.2), calls=%async_computation | async-start | bytes 1572864 | tf_op jit(solution)/shard_map/all_to_all | solution.py:1075
  68.3 41.4 %collective-permute-start.9 = (f32[3,10,128,128]{3,2,1,0:T(8,128)}, f32[3,10,128,128]{3,2,1,0:T(8,128)}, u32[]{:S(2)}, u32[]{:S(2)}) collective-permute-start(f32[3,10,128,128]{3,2,1,0:T(8,128)} %get-tuple-element.64.refs_0_), channel_id=1, source_target_pairs={{0,1},{1,2},{2,3},{4,5},{5,6},{6,7},{8,9},{9,10},{10,11},{12,13},{... | collective-permute-start | bytes 5898248 | tf_op jit(solution)/shard_map/ppermute | solution.py:805
  93.3 19.3 %all-to-all-start.2 = ((f32[32,32,128]{2,1,0:T(8,128)}), f32[32,32,128]{2,1,0:T(8,128)}, u32[]{:S(2)}, u32[]{:S(2)}) async-start(f32[32,32,128]{2,1,0:T(8,128)} %bitcast.19), calls=%async_computation.2 | async-start | bytes 1048576 | tf_op jit(solution)/shard_map/all_to_all | solution.py:1081
  112.6 22.1 %all-to-all-start.1 = ((f32[32,32,128]{2,1,0:T(8,128)}), f32[32,32,128]{2,1,0:T(8,128)}, u32[]{:S(2)}, u32[]{:S(2)}) async-start(f32[32,32,128]{2,1,0:T(8,128)} %bitcast.18), calls=%async_computation.1 | async-start | bytes 1048576 | tf_op jit(solution)/shard_map/all_to_all | solution.py:1081
  116.1 12.4 %collective-permute-start.10 = (f32[32,32,128]{2,1,0:T(8,128)}, f32[32,32,128]{2,1,0:T(8,128)}, u32[]{:S(2)}, u32[]{:S(2)}) collective-permute-start(f32[32,32,128]{2,1,0:T(8,128)} %all-to-all-done.2), channel_id=1, source_target_pairs={{0,1},{1,2},{2,3},{4,5},{5,6},{6,7},{8,9},{9,10},{10,11},{12,13},{... | collective-permute-start | bytes 1572872 | tf_op jit(solution)/shard_map/ppermute | solution.py:805

commit v6 on v5

--- a/solution.py
+++ b/solution.py
@@ -303,13 +303,9 @@
 
 
 def solve_kernel(
-    peers, intervals, planes, group, back, values, inverse_in, table_in,
-    sent_1, sent_2, inverse, table, out_1, out_2, sems, out_sems
+    peers, intervals, planes, group, back, values, inverse, table,
+    sent_1, sent_2, out_1, out_2, out_sems
 ):
-    start_all([
-        pltpu.make_async_copy(table_in, table, sems.at[0]),
-        pltpu.make_async_copy(inverse_in, inverse, sems.at[1]),
-    ])
     sending = []
     rows_x = peers * planes
     start = [None] * 3
@@ -1094,14 +1090,11 @@
     solved_1, solved_2 = pl.pallas_call(
         functools.partial(solve_kernel, peers, intervals, planes, group, back),
         out_shape=(struct((devices * back, lanes)),) * 2,
-        in_specs=[vmem, hbm, hbm],
+        in_specs=[vmem, vmem, vmem],
         out_specs=(hbm, hbm),
         scratch_shapes=[
-            pltpu.VMEM(rates.shape, f32),
-            pltpu.VMEM(x_table.shape, bf16),
             pltpu.VMEM((devices * back, lanes), f32),
             pltpu.VMEM((devices * back, lanes), f32),
-            pltpu.SemaphoreType.DMA((2,)),
             pltpu.SemaphoreType.DMA((2, devices)),
         ],
         compiler_params=params_but(790),

time: 142 us -> 141 us (level)
    all_to_all x2, waiting for transfers between devices: 2.96 us -> 1.44 us  [to_planes(): value = lax.all_to_all(value, both, split_axis=0, concat_axis=0, tiled=True)]
    ppermute x5, waiting for transfers between devices: 23.7 us -> 25.2 us  [later_interval(): return lax.ppermute(value, 'tm', [(i, i + 1) for i in range(count - 1)])]
where the time goes in v6:
time: 141 us; the launch traced here: 140 us
  Pallas kernels  51.4 us (36%)
  starting transfers between devices  45.1 us (32%)
  waiting for transfers between devices  41.1 us (29%)
    ppermute x5, waiting for transfers between devices, later_interval(): return lax.ppermute(value, 'tm', [(i, i + 1) for i in range(count - 1)])  25.2 us
    ppermute x5, starting transfers between devices, later_interval(): return lax.ppermute(value, 'tm', [(i, i + 1) for i in range(count - 1)])  19.3 us
    pallas_call x3, Pallas kernels, corrected(): pl.pallas_call(functools.partial(corrected_kernel, node, group, layouts,...  18.5 us
    pallas_call x1, Pallas kernels, sweep_split(): pl.pallas_call(functools.partial(interior_kernel, group, g_group), out_sh...  18.5 us
    ppermute x3, starting transfers between devices, neighbours(): lax.ppermute(low_plane, 'space', down)  11.1 us
    all_to_all x2, starting transfers between devices, to_planes(): value = lax.all_to_all(value, both, split_axis=0, concat_axis=0, tiled=True)  7.54 us
    all_to_all x1, waiting for transfers between devices, to_columns(): value = lax.all_to_all(value, both, split_axis=0, concat_axis=0, tiled=True)  6.48 us
    ppermute x3, waiting for transfers between devices, neighbours(): lax.ppermute(low_plane, 'space', down)  4.61 us
  transfers between devices with their start and end apart: 14, of which 8 were waited for; matrix products, arithmetic and copies ran while one was open for 1% of the time, Pallas kernels for 30%

profile of v6, /device:TPU:1, one launch (start us, length us, event | category | flops | bytes accessed | tf_op | source)
XLA Modules:
  0.0 140.2 jit_solution(3700455770190687326)
XLA Ops:
  0.7 2.3 %edges.1 = (f32[9,128,128]{2,1,0:T(8,128)}, f32[9,128,128]{2,1,0:T(8,128)}) custom-call(f32[9,16,128,128]{3,2,1,0:T(8,128)} %bitcast.13), custom_call_target="tpu_custom_call" | custom-call | tf_op jit(solution)/shard_map/edges/pallas_call | solution.py:914
  3.0 2.1 %collective-permute-start = (f32[9,128,128]{2,1,0:T(8,128)}, f32[9,128,128]{2,1,0:T(8,128)S(1)}, u32[]{:S(2)}, u32[]{:S(2)}) collective-permute-start(f32[9,128,128]{2,1,0:T(8,128)} %get-tuple-element.42), channel_id=1, source_target_pairs={{0,4},{4,8},{8,12},{12,16},{16,20},{20,24},{24,28},{28,0},{1,5},{5... | collective-permute-start | bytes 1769480 | tf_op jit(solution)/shard_map/ppermute | solution.py:796
  5.1 3.1 %collective-permute-start.1 = (f32[9,128,128]{2,1,0:T(8,128)}, f32[9,128,128]{2,1,0:T(8,128)S(1)}, u32[]{:S(2)}, u32[]{:S(2)}) collective-permute-start(f32[9,128,128]{2,1,0:T(8,128)} %get-tuple-element.43), channel_id=1, source_target_pairs={{4,0},{8,4},{12,8},{16,12},{20,16},{24,20},{28,24},{0,28},{5,1},{9... | collective-permute-start | bytes 1769480 | tf_op jit(solution)/shard_map/ppermute | solution.py:796
  8.2 18.5 %interior.1 = (f32[9,4,128,128]{3,2,1,0:T(8,128)S(1)}, f32[3,14,128,128]{3,2,1,0:T(8,128)S(1)}, f32[3,8,128,128]{3,2,1,0:T(8,128)S(1)}, f32[3,4,128,128]{3,2,1,0...) custom-call(f32[1]{0:T(128)} %bitcast.is_first, ...), custom_call_target="tpu_custom_call" | custom-call | flops 4000000000 | bytes 60000000 | tf_op jit(solution)/shard_map/interior/pallas_call | solution.py:924
  26.7 3.4 %collective-permute-done.low.refs_2_ = f32[9,128,128]{2,1,0:T(8,128)S(1)} collective-permute-done((f32[9,128,128]{2,1,0:T(8,128)}, f32[9,128,128]{2,1,0:T(8,128)S(1)}, u32[]{:S(2)}, u32[]{:S(2)}) %collective-permute-start) | collective-permute-done | bytes 589856 | tf_op jit(solution)/shard_map/ppermute | solution.py:796
  30.0 1.8 %collective-permute-done.1.high.refs_4_ = f32[9,128,128]{2,1,0:T(8,128)S(1)} collective-permute-done((f32[9,128,128]{2,1,0:T(8,128)}, f32[9,128,128]{2,1,0:T(8,128)S(1)}, u32[]{:S(2)}, u32[]{:S(2)}) %collective-permute-start.1) | collective-permute-done | bytes 589856 | tf_op jit(solution)/shard_map/ppermute | solution.py:796
  31.8 1.3 end_one.1
  33.5 3.8 %collective-permute-start.3 = (f32[3,128,128]{2,1,0:T(8,128)S(1)}, f32[3,128,128]{2,1,0:T(8,128)S(1)}, u32[]{:S(2)}, u32[]{:S(2)}) collective-permute-start(f32[3,128,128]{2,1,0:T(8,128)S(1)} %get-tuple-element.46.low_end.refs_1_), channel_id=1, source_target_pairs={{4,0},{8,4},{12,8},{16,12},{20,16},{24,20},{28,24},{0,28},{5,1},{9... | collective-permute-start | bytes 589832 | tf_op jit(solution)/shard_map/ppermute | solution.py:796
  37.4 5.4 %collective-permute-start.6 = (f32[768,128]{1,0:T(8,128)S(1)}, f32[768,128]{1,0:T(8,128)S(1)}, u32[]{:S(2)}, u32[]{:S(2)}) collective-permute-start(f32[768,128]{1,0:T(8,128)S(1)} %get-tuple-element.59), channel_id=1, source_target_pairs={{0,1},{1,2},{2,3},{4,5},{5,6},{6,7},{8,9},{9,10},{10,11},{12,13},{... | collective-permute-start | bytes 1179656 | tf_op jit(solution)/shard_map/ppermute | solution.py:801
  42.8 2.8 %collective-permute-done.3.high.refs_4_ = f32[3,128,128]{2,1,0:T(8,128)S(1)} collective-permute-done((f32[3,128,128]{2,1,0:T(8,128)S(1)}, f32[3,128,128]{2,1,0:T(8,128)S(1)}, u32[]{:S(2)}, u32[]{:S(2)}) %collective-permute-start.3) | collective-permute-done | bytes 196640 | tf_op jit(solution)/shard_map/ppermute | solution.py:796
  45.6 1.9 %end_two.1 = (f32[3,128,128]{2,1,0:T(8,128)S(1)}, f32[3,128,128]{2,1,0:T(8,128)S(1)}, f32[3,2,128,128]{3,2,1,0:T(8,128)S(1)}, f32[6,2,128,128]{3,2,1,0:T(8,128)S(1)}, f32[256,128]{1,0:T(8,128)S(1)}) custom-call(f32[3,14,128,128]{3,2,1,0:T(8,128)S(1)} %get-tuple-element.40.swept.refs_2_, f32[3,128,128]{2,1,0:T(8,128)S(1)} %collective-permute-done.2.low.refs_0_, ...), custom_call_target="tpu_custom_call" | custom-call | tf_op jit(solution)/shard_map/end_two/pallas_call | solution.py:969
  47.7 4.1 %collective-permute-start.5 = (f32[3,128,128]{2,1,0:T(8,128)S(1)}, f32[3,128,128]{2,1,0:T(8,128)S(1)}, u32[]{:S(2)}, u32[]{:S(2)}) collective-permute-start(f32[3,128,128]{2,1,0:T(8,128)S(1)} %get-tuple-element.51.low_end), channel_id=1, source_target_pairs={{4,0},{8,4},{12,8},{16,12},{20,16},{24,20},{28,24},{0,28},{5,1},{9... | collective-permute-start | bytes 589832 | tf_op jit(solution)/shard_map/ppermute | solution.py:796
  51.8 4.7 %collective-permute-start.7 = (f32[256,128]{1,0:T(8,128)S(1)}, f32[256,128]{1,0:T(8,128)S(1)}, u32[]{:S(2)}, u32[]{:S(2)}) collective-permute-start(f32[256,128]{1,0:T(8,128)S(1)} %get-tuple-element.60), channel_id=1, source_target_pairs={{0,1},{1,2},{2,3},{4,5},{5,6},{6,7},{8,9},{9,10},{10,11},{12,13},{... | collective-permute-start | bytes 393224 | tf_op jit(solution)/shard_map/ppermute | solution.py:801
  56.5 1.9 %collective-permute-start.8 = (f32[3,8,128,128]{3,2,1,0:T(8,128)S(1)}, f32[3,8,128,128]{3,2,1,0:T(8,128)}, u32[]{:S(2)}, u32[]{:S(2)}) collective-permute-start(f32[3,8,128,128]{3,2,1,0:T(8,128)S(1)} %get-tuple-element.53.swept.refs_1_), channel_id=1, source_target_pairs={{0,1},{1,2},{2,3},{4,5},{5,6},{6,7},{8,9},{9,10},{10,11},{12,13},{... | collective-permute-start | bytes 4718600 | tf_op jit(solution)/shard_map/ppermute | solution.py:801
  58.5 2.3 %middle.1 = (f32[6,2,128,128]{3,2,1,0:T(8,128)S(1)}, f32[1536,128]{1,0:T(8,128)S(1)}) custom-call(f32[3,8,128,128]{3,2,1,0:T(8,128)S(1)} %get-tuple-element.53.swept.refs_1_, f32[3,4,128,128]{3,2,1,0:T(8,128)S(1)} %get-tuple-element.39.side, f32[3,128,128]{2,1,0:T(8,128)S(1)} %get-tuple-element.51.low_end, f32[3,2,128,128]{3,2,1,0:T(8,128)S(1)} %get-tuple-element.52.nexts, ...), custom_call_target="tpu_custom_call" | custom-call | tf_op jit(solution)/shard_map/middle/pallas_call | solution.py:985
  60.9 2.8 %end_three.1 = (f32[3,10,128,128]{3,2,1,0:T(8,128)}, f32[1536,128]{1,0:T(8,128)}) custom-call(f32[3,4,128,128]{3,2,1,0:T(8,128)S(1)} %get-tuple-element.39.side, f32[3,128,128]{2,1,0:T(8,128)S(1)} %collective-permute-done.4.low, f32[3,128,128]{2,1,0:T(8,128)S(1)} %get-tuple-element.51.low_end, f32[3,2,128,128]{3,2,1,0:T(8,128)S(1)} %get-tuple-element.52.nexts, ...), custom_call_target="tpu_custom_call" | custom-call | tf_op jit(solution)/shard_map/end_three/pallas_call | solution.py:994
  63.7 4.6 %all-to-all-start = ((f32[32,48,128]{2,1,0:T(8,128)}), f32[32,48,128]{2,1,0:T(8,128)}, u32[]{:S(2)}, u32[]{:S(2)}) async-start(f32[32,48,128]{2,1,0:T(8,128)} %bitcast.2), calls=%async_computation | async-start | bytes 1572864 | tf_op jit(solution)/shard_map/all_to_all | solution.py:1071
  68.3 3.5 %collective-permute-start.9 = (f32[3,10,128,128]{3,2,1,0:T(8,128)}, f32[3,10,128,128]{3,2,1,0:T(8,128)}, u32[]{:S(2)}, u32[]{:S(2)}) collective-permute-start(f32[3,10,128,128]{3,2,1,0:T(8,128)} %get-tuple-element.64.refs_0_), channel_id=1, source_target_pairs={{0,1},{1,2},{2,3},{4,5},{5,6},{6,7},{8,9},{9,10},{10,11},{12,13},{... | collective-permute-start | bytes 5898248 | tf_op jit(solution)/shard_map/ppermute | solution.py:801
  71.8 0.7 dynamic-slice_bitcast_fusion
  72.5 0.7 add_divide_fusion.inverse
  73.2 8.9 %collective-permute-done.8.refs_1_ = f32[3,8,128,128]{3,2,1,0:T(8,128)} collective-permute-done((f32[3,8,128,128]{3,2,1,0:T(8,128)S(1)}, f32[3,8,128,128]{3,2,1,0:T(8,128)}, u32[]{:S(2)}, u32[]{:S(2)}) %collective-permute-start.8) | collective-permute-done | bytes 1572896 | tf_op jit(solution)/shard_map/ppermute | solution.py:801
  82.1 6.5 %all-to-all-done = f32[32,48,128]{2,1,0:T(8,128)} async-done(((f32[32,48,128]{2,1,0:T(8,128)}), f32[32,48,128]{2,1,0:T(8,128)}, u32[]{:S(2)}, u32[]{:S(2)}) %all-to-all-start) | async-done | bytes 786464 | tf_op jit(solution)/shard_map/all_to_all | solution.py:1071
  88.6 3.8 %solve.1 = (f32[1024,128]{1,0:T(8,128)}, f32[1024,128]{1,0:T(8,128)}) custom-call(f32[1536,128]{1,0:T(8,128)} %bitcast.3.values, f32[64,128]{1,0:T(8,128)} %add_divide_fusion.inverse, bf16[144,192]{1,0:T(8,128)(2,1)} %constant.35.clone.table), custom_call_target="tpu_custom_call" | custom-call | tf_op jit(solution)/shard_map/solve/pallas_call | solution.py:1090
  92.4 4.0 %all-to-all-start.2 = ((f32[32,32,128]{2,1,0:T(8,128)}), f32[32,32,128]{2,1,0:T(8,128)}, u32[]{:S(2)}, u32[]{:S(2)}) async-start(f32[32,32,128]{2,1,0:T(8,128)} %bitcast.19), calls=%async_computation.2 | async-start | bytes 1048576 | tf_op jit(solution)/shard_map/all_to_all | solution.py:1077
  96.5 13.8 %collective-permute-done.9.refs_0_ = f32[3,10,128,128]{3,2,1,0:T(8,128)} collective-permute-done((f32[3,10,128,128]{3,2,1,0:T(8,128)}, f32[3,10,128,128]{3,2,1,0:T(8,128)}, u32[]{:S(2)}, u32[]{:S(2)}) %collective-permute-start.9) | collective-permute-done | bytes 1966112 | tf_op jit(solution)/shard_map/ppermute | solution.py:801
  110.3 1.4 %all-to-all-done.2 = f32[32,32,128]{2,1,0:T(8,128)} async-done(((f32[32,32,128]{2,1,0:T(8,128)}), f32[32,32,128]{2,1,0:T(8,128)}, u32[]{:S(2)}, u32[]{:S(2)}) %all-to-all-start.2) | async-done | bytes 524320 | tf_op jit(solution)/shard_map/all_to_all | solution.py:1077
  111.8 3.5 %all-to-all-start.1 = ((f32[32,32,128]{2,1,0:T(8,128)}), f32[32,32,128]{2,1,0:T(8,128)}, u32[]{:S(2)}, u32[]{:S(2)}) async-start(f32[32,32,128]{2,1,0:T(8,128)} %bitcast.18), calls=%async_computation.1 | async-start | bytes 1048576 | tf_op jit(solution)/shard_map/all_to_all | solution.py:1077
  115.3 3.7 %collective-permute-start.10 = (f32[32,32,128]{2,1,0:T(8,128)}, f32[32,32,128]{2,1,0:T(8,128)}, u32[]{:S(2)}, u32[]{:S(2)}) collective-permute-start(f32[32,32,128]{2,1,0:T(8,128)} %all-to-all-done.2), channel_id=1, source_target_pairs={{0,1},{1,2},{2,3},{4,5},{5,6},{6,7},{8,9},{9,10},{10,11},{12,13},{... | collective-permute-start | bytes 1572872 | tf_op jit(solution)/shard_map/ppermute | solution.py:801
  119.0 6.1 %corrected_2.1 = (f32[3,3,16,128,128]{4,3,2,1,0:T(8,128)}, bf16[3,3,16,128,128]{4,3,2,1,0:T(8,128)(2,1)}) custom-call(f32[1]{0:T(128)} %bitcast.is_first, f32[1024,128]{1,0:T(8,128)} %bitcast.9.spectra, bf16[512,256]{1,0:T(8,128)(2,1)} %constant.36.clone.table, f32[3,10,128,128]{3,2,1,0:T(8,128)} %get-tuple-element.64.refs_0_, f32[3,8,128,128]{3,2,1,0:T(8,128)} %copy-done.1), custom_call_target="tpu_custom_call" | custom-call | tf_op jit(solution)/shard_map/corrected_2/pallas_call | solution.py:815
  125.1 2.5 %collective-permute-done.10 = f32[32,32,128]{2,1,0:T(8,128)} collective-permute-done((f32[32,32,128]{2,1,0:T(8,128)}, f32[32,32,128]{2,1,0:T(8,128)}, u32[]{:S(2)}, u32[]{:S(2)}) %collective-permute-start.10) | collective-permute-done | bytes 524320 | tf_op jit(solution)/shard_map/ppermute | solution.py:801
  127.6 6.2 %corrected_0.1 = (f32[3,3,16,128,128]{4,3,2,1,0:T(8,128)}, bf16[3,3,16,128,128]{4,3,2,1,0:T(8,128)(2,1)}) custom-call(f32[1]{0:T(128)} %bitcast.is_first, f32[1024,128]{1,0:T(8,128)} %bitcast.8.spectra, bf16[512,256]{1,0:T(8,128)(2,1)} %constant.36.clone.table, ...), custom_call_target="tpu_custom_call", output_to_operand_aliasing={{0}: (8, {}), {1}: (9, {})} | custom-call | tf_op jit(solution)/shard_map/corrected_0/pallas_call | solution.py:815
  133.9 6.1 %corrected_1.1 = (f32[3,3,16,128,128]{4,3,2,1,0:T(8,128)}, bf16[3,3,16,128,128]{4,3,2,1,0:T(8,128)(2,1)}) custom-call(f32[1]{0:T(128)} %bitcast.is_first, f32[1024,128]{1,0:T(8,128)} %bitcast.6.spectra, bf16[512,256]{1,0:T(8,128)(2,1)} %constant.36.clone.table, f32[3,128,128]{2,1,0:T(8,128)} %copy-done.7, ...), custom_call_target="tpu_custom_call", output_to_operand_aliasing={{0}: (8, {}), {1}: (9, {})} | custom-call | tf_op jit(solution)/shard_map/corrected_1/pallas_call | solution.py:815
  (30 shorter events, 0.5 us)
Async XLA Ops:
  0.6 7.6 %copy-start.4 = (bf16[768,128]{1,0:T(8,128)(2,1)S(1)}, bf16[768,128]{1,0:T(8,128)(2,1)}, u32[]{:S(2)}) copy-start(bf16[768,128]{1,0:T(8,128)(2,1)} %constant.33.clone.z_table) | copy-start | bytes 589828
  0.6 7.6 %copy-start.9 = (bf16[64,192]{1,0:T(8,128)(2,1)S(1)}, bf16[64,192]{1,0:T(8,128)(2,1)}, u32[]{:S(2)}) copy-start(bf16[64,192]{1,0:T(8,128)(2,1)} %constant.34.clone.y_table) | copy-start | bytes 73732
  3.0 27.1 %collective-permute-start = (f32[9,128,128]{2,1,0:T(8,128)}, f32[9,128,128]{2,1,0:T(8,128)S(1)}, u32[]{:S(2)}, u32[]{:S(2)}) collective-permute-start(f32[9,128,128]{2,1,0:T(8,128)} %get-tuple-element.42), channel_id=1, source_target_pairs={{0,4},{4,8},{8,12},{12,16},{16,20},{20,24},{24,28},{28,0},{1,5},{5... | collective-permute-start | bytes 1769480 | tf_op jit(solution)/shard_map/ppermute | solution.py:796
  5.1 26.7 %collective-permute-start.1 = (f32[9,128,128]{2,1,0:T(8,128)}, f32[9,128,128]{2,1,0:T(8,128)S(1)}, u32[]{:S(2)}, u32[]{:S(2)}) collective-permute-start(f32[9,128,128]{2,1,0:T(8,128)} %get-tuple-element.43), channel_id=1, source_target_pairs={{4,0},{8,4},{12,8},{16,12},{20,16},{24,20},{28,24},{0,28},{5,1},{9... | collective-permute-start | bytes 1769480 | tf_op jit(solution)/shard_map/ppermute | solution.py:796
  26.7 20.9 %copy-start = (f32[3,14,128,128]{3,2,1,0:T(8,128)}, f32[3,14,128,128]{3,2,1,0:T(8,128)S(1)}, u32[]{:S(2)}) copy-start(f32[3,14,128,128]{3,2,1,0:T(8,128)S(1)} %get-tuple-element.40.swept.refs_2_) | copy-start | bytes 8257540
  26.7 31.8 %copy-start.1 = (f32[3,8,128,128]{3,2,1,0:T(8,128)}, f32[3,8,128,128]{3,2,1,0:T(8,128)S(1)}, u32[]{:S(2)}) copy-start(f32[3,8,128,128]{3,2,1,0:T(8,128)S(1)} %get-tuple-element.53.swept.refs_1_) | copy-start | bytes 4718596
  30.0 17.5 %copy-start.2 = (f32[9,128,128]{2,1,0:T(8,128)}, f32[9,128,128]{2,1,0:T(8,128)S(1)}, u32[]{:S(2)}) copy-start(f32[9,128,128]{2,1,0:T(8,128)S(1)} %collective-permute-done.low.refs_2_) | copy-start | bytes 1769476
  31.8 15.8 %copy-start.3 = (f32[9,128,128]{2,1,0:T(8,128)}, f32[9,128,128]{2,1,0:T(8,128)S(1)}, u32[]{:S(2)}) copy-start(f32[9,128,128]{2,1,0:T(8,128)S(1)} %collective-permute-done.1.high.refs_4_) | copy-start | bytes 1769476
  33.1 23.4 %copy-start.5 = (f32[3,128,128]{2,1,0:T(8,128)}, f32[3,128,128]{2,1,0:T(8,128)S(1)}, u32[]{:S(2)}) copy-start(f32[3,128,128]{2,1,0:T(8,128)S(1)} %get-tuple-element.46.low_end.refs_1_) | copy-start | bytes 589828
  33.1 23.4 %copy-start.6 = (f32[3,128,128]{2,1,0:T(8,128)}, f32[3,128,128]{2,1,0:T(8,128)S(1)}, u32[]{:S(2)}) copy-start(f32[3,128,128]{2,1,0:T(8,128)S(1)} %get-tuple-element.45.high_end.refs_3_) | copy-start | bytes 589828
  33.1 9.6 %collective-permute-start.2 = (f32[3,128,128]{2,1,0:T(8,128)S(1)}, f32[3,128,128]{2,1,0:T(8,128)S(1)}, u32[]{:S(2)}, u32[]{:S(2)}) collective-permute-start(f32[3,128,128]{2,1,0:T(8,128)S(1)} %get-tuple-element.45.high_end.refs_3_), channel_id=1, source_target_pairs={{0,4},{4,8},{8,12},{12,16},{16,20},{20,24},{24,28},{28,0},{1,5},{5... | collective-permute-start | bytes 589832 | tf_op jit(solution)/shard_map/ppermute | solution.py:796
  33.5 12.1 %collective-permute-start.3 = (f32[3,128,128]{2,1,0:T(8,128)S(1)}, f32[3,128,128]{2,1,0:T(8,128)S(1)}, u32[]{:S(2)}, u32[]{:S(2)}) collective-permute-start(f32[3,128,128]{2,1,0:T(8,128)S(1)} %get-tuple-element.46.low_end.refs_1_), channel_id=1, source_target_pairs={{4,0},{8,4},{12,8},{16,12},{20,16},{24,20},{28,24},{0,28},{5,1},{9... | collective-permute-start | bytes 589832 | tf_op jit(solution)/shard_map/ppermute | solution.py:796
  37.4 23.5 %collective-permute-start.6 = (f32[768,128]{1,0:T(8,128)S(1)}, f32[768,128]{1,0:T(8,128)S(1)}, u32[]{:S(2)}, u32[]{:S(2)}) collective-permute-start(f32[768,128]{1,0:T(8,128)S(1)} %get-tuple-element.59), channel_id=1, source_target_pairs={{0,1},{1,2},{2,3},{4,5},{5,6},{6,7},{8,9},{9,10},{10,11},{12,13},{... | collective-permute-start | bytes 1179656 | tf_op jit(solution)/shard_map/ppermute | solution.py:801
  42.8 18.0 %copy-start.7 = (f32[3,128,128]{2,1,0:T(8,128)}, f32[3,128,128]{2,1,0:T(8,128)S(1)}, u32[]{:S(2)}) copy-start(f32[3,128,128]{2,1,0:T(8,128)S(1)} %collective-permute-done.2.low.refs_0_) | copy-start | bytes 589828
  45.6 12.8 %copy-start.8 = (f32[3,128,128]{2,1,0:T(8,128)}, f32[3,128,128]{2,1,0:T(8,128)S(1)}, u32[]{:S(2)}) copy-start(f32[3,128,128]{2,1,0:T(8,128)S(1)} %collective-permute-done.3.high.refs_4_) | copy-start | bytes 589828
  47.6 13.2 %collective-permute-start.4 = (f32[3,128,128]{2,1,0:T(8,128)S(1)}, f32[3,128,128]{2,1,0:T(8,128)S(1)}, u32[]{:S(2)}, u32[]{:S(2)}) collective-permute-start(f32[3,128,128]{2,1,0:T(8,128)S(1)} %get-tuple-element.50.high_end), channel_id=1, source_target_pairs={{0,4},{4,8},{8,12},{12,16},{16,20},{20,24},{24,28},{28,0},{1,5},{5... | collective-permute-start | bytes 589832 | tf_op jit(solution)/shard_map/ppermute | solution.py:796
  47.7 13.2 %collective-permute-start.5 = (f32[3,128,128]{2,1,0:T(8,128)S(1)}, f32[3,128,128]{2,1,0:T(8,128)S(1)}, u32[]{:S(2)}, u32[]{:S(2)}) collective-permute-start(f32[3,128,128]{2,1,0:T(8,128)S(1)} %get-tuple-element.51.low_end), channel_id=1, source_target_pairs={{4,0},{8,4},{12,8},{16,12},{20,16},{24,20},{28,24},{0,28},{5,1},{9... | collective-permute-start | bytes 589832 | tf_op jit(solution)/shard_map/ppermute | solution.py:796
  51.8 9.0 %collective-permute-start.7 = (f32[256,128]{1,0:T(8,128)S(1)}, f32[256,128]{1,0:T(8,128)S(1)}, u32[]{:S(2)}, u32[]{:S(2)}) collective-permute-start(f32[256,128]{1,0:T(8,128)S(1)} %get-tuple-element.60), channel_id=1, source_target_pairs={{0,1},{1,2},{2,3},{4,5},{5,6},{6,7},{8,9},{9,10},{10,11},{12,13},{... | collective-permute-start | bytes 393224 | tf_op jit(solution)/shard_map/ppermute | solution.py:801
  56.5 25.6 %collective-permute-start.8 = (f32[3,8,128,128]{3,2,1,0:T(8,128)S(1)}, f32[3,8,128,128]{3,2,1,0:T(8,128)}, u32[]{:S(2)}, u32[]{:S(2)}) collective-permute-start(f32[3,8,128,128]{3,2,1,0:T(8,128)S(1)} %get-tuple-element.53.swept.refs_1_), channel_id=1, source_target_pairs={{0,1},{1,2},{2,3},{4,5},{5,6},{6,7},{8,9},{9,10},{10,11},{12,13},{... | collective-permute-start | bytes 4718600 | tf_op jit(solution)/shard_map/ppermute | solution.py:801
  58.5 14.0 %copy-start.10 = (f32[64]{0:T(128)S(1)}, f32[64]{0:T(128)}, u32[]{:S(2)}) copy-start(f32[64]{0:T(128)} %constant.32.clone) | copy-start | bytes 772
  63.7 24.9 %all-to-all-start = ((f32[32,48,128]{2,1,0:T(8,128)}), f32[32,48,128]{2,1,0:T(8,128)}, u32[]{:S(2)}, u32[]{:S(2)}) async-start(f32[32,48,128]{2,1,0:T(8,128)} %bitcast.2), calls=%async_computation | async-start | bytes 1572864 | tf_op jit(solution)/shard_map/all_to_all | solution.py:1071
  68.3 42.1 %collective-permute-start.9 = (f32[3,10,128,128]{3,2,1,0:T(8,128)}, f32[3,10,128,128]{3,2,1,0:T(8,128)}, u32[]{:S(2)}, u32[]{:S(2)}) collective-permute-start(f32[3,10,128,128]{3,2,1,0:T(8,128)} %get-tuple-element.64.refs_0_), channel_id=1, source_target_pairs={{0,1},{1,2},{2,3},{4,5},{5,6},{6,7},{8,9},{9,10},{10,11},{12,13},{... | collective-permute-start | bytes 5898248 | tf_op jit(solution)/shard_map/ppermute | solution.py:801
  92.4 19.3 %all-to-all-start.2 = ((f32[32,32,128]{2,1,0:T(8,128)}), f32[32,32,128]{2,1,0:T(8,128)}, u32[]{:S(2)}, u32[]{:S(2)}) async-start(f32[32,32,128]{2,1,0:T(8,128)} %bitcast.19), calls=%async_computation.2 | async-start | bytes 1048576 | tf_op jit(solution)/shard_map/all_to_all | solution.py:1077
  111.8 22.1 %all-to-all-start.1 = ((f32[32,32,128]{2,1,0:T(8,128)}), f32[32,32,128]{2,1,0:T(8,128)}, u32[]{:S(2)}, u32[]{:S(2)}) async-start(f32[32,32,128]{2,1,0:T(8,128)} %bitcast.18), calls=%async_computation.1 | async-start | bytes 1048576 | tf_op jit(solution)/shard_map/all_to_all | solution.py:1077
  115.3 12.4 %collective-permute-start.10 = (f32[32,32,128]{2,1,0:T(8,128)}, f32[32,32,128]{2,1,0:T(8,128)}, u32[]{:S(2)}, u32[]{:S(2)}) collective-permute-start(f32[32,32,128]{2,1,0:T(8,128)} %all-to-all-done.2), channel_id=1, source_target_pairs={{0,1},{1,2},{2,3},{4,5},{5,6},{6,7},{8,9},{9,10},{10,11},{12,13},{... | collective-permute-start | bytes 1572872 | tf_op jit(solution)/shard_map/ppermute | solution.py:801

commit v7 on v6

--- a/solution.py
+++ b/solution.py
@@ -347,12 +347,17 @@
         copy.wait()
 
 
-def edges_kernel(source, low, high, sems):
-    length = source.shape[1]
-    start_all([
-        pltpu.make_async_copy(source.at[:, 0], low, sems.at[0]),
-        pltpu.make_async_copy(source.at[:, length - 1], high, sems.at[1]),
-    ])
+def edges_kernel(source, low, high, held, sems):
+    ends = (source.at[:, 0], low), (source.at[:, source.shape[1] - 1], high)
+    arriving = [pltpu.make_async_copy(e[0], held.at[k], sems.at[k]) for k, e in enumerate(ends)]
+    leaving = [pltpu.make_async_copy(held.at[k], e[1], sems.at[2 + k]) for k, e in enumerate(ends)]
+    for copy in arriving:
+        copy.start()
+    for k in range(2):
+        arriving[k].wait()
+        leaving[k].start()
+    for copy in leaving:
+        copy.wait()
 
 
 def sweep_one_plane(is_first, held, slot, put_s1, put_w, uv, cell):
@@ -915,8 +920,8 @@
         edges_kernel,
         out_shape=(struct((9, *plane)),) * 2,
         in_specs=[hbm],
-        out_specs=(vmem,) * 2,
-        scratch_shapes=[sems(2)],
+        out_specs=(hbm,) * 2,
+        scratch_shapes=[pltpu.VMEM((2, 9, *plane), f32), sems(4)],
         compiler_params=params_but(300),
         name="edges",
     )(fields)

time: 141 us -> 141 us (level)
  no operation moved by 1% of the time
where the time goes in v7:
time: 141 us; the launch traced here: 140 us
  Pallas kernels  51.2 us (36%)
  starting transfers between devices  45.1 us (32%)
  waiting for transfers between devices  41.1 us (29%)
    ppermute x5, waiting for transfers between devices, later_interval(): return lax.ppermute(value, 'tm', [(i, i + 1) for i in range(count - 1)])  25.2 us
    ppermute x5, starting transfers between devices, later_interval(): return lax.ppermute(value, 'tm', [(i, i + 1) for i in range(count - 1)])  19.3 us
    pallas_call x3, Pallas kernels, corrected(): pl.pallas_call(functools.partial(corrected_kernel, node, group, layouts,...  18.5 us
    pallas_call x1, Pallas kernels, sweep_split(): pl.pallas_call(functools.partial(interior_kernel, group, g_group), out_sh...  18.5 us
    ppermute x3, starting transfers between devices, neighbours(): lax.ppermute(low_plane, 'space', down)  11.1 us
    all_to_all x2, starting transfers between devices, to_planes(): value = lax.all_to_all(value, both, split_axis=0, concat_axis=0, tiled=True)  7.54 us
    all_to_all x1, waiting for transfers between devices, to_columns(): value = lax.all_to_all(value, both, split_axis=0, concat_axis=0, tiled=True)  6.48 us
    ppermute x3, waiting for transfers between devices, neighbours(): lax.ppermute(low_plane, 'space', down)  4.61 us
  transfers between devices with their start and end apart: 14, of which 8 were waited for; matrix products, arithmetic and copies ran while one was open for 1% of the time, Pallas kernels for 30%

profile of v7, /device:TPU:1, one launch (start us, length us, event | category | flops | bytes accessed | tf_op | source)
XLA Modules:
  0.0 140.0 jit_solution(15989112781402084480)
XLA Ops:
  0.7 2.1 %edges.1 = (f32[9,128,128]{2,1,0:T(8,128)}, f32[9,128,128]{2,1,0:T(8,128)}) custom-call(f32[9,16,128,128]{3,2,1,0:T(8,128)} %bitcast.13), custom_call_target="tpu_custom_call" | custom-call | tf_op jit(solution)/shard_map/edges/pallas_call | solution.py:919
  2.8 2.1 %collective-permute-start = (f32[9,128,128]{2,1,0:T(8,128)}, f32[9,128,128]{2,1,0:T(8,128)S(1)}, u32[]{:S(2)}, u32[]{:S(2)}) collective-permute-start(f32[9,128,128]{2,1,0:T(8,128)} %get-tuple-element.42), channel_id=1, source_target_pairs={{0,4},{4,8},{8,12},{12,16},{16,20},{20,24},{24,28},{28,0},{1,5},{5... | collective-permute-start | bytes 1769480 | tf_op jit(solution)/shard_map/ppermute | solution.py:801
  4.9 3.1 %collective-permute-start.1 = (f32[9,128,128]{2,1,0:T(8,128)}, f32[9,128,128]{2,1,0:T(8,128)S(1)}, u32[]{:S(2)}, u32[]{:S(2)}) collective-permute-start(f32[9,128,128]{2,1,0:T(8,128)} %get-tuple-element.43), channel_id=1, source_target_pairs={{4,0},{8,4},{12,8},{16,12},{20,16},{24,20},{28,24},{0,28},{5,1},{9... | collective-permute-start | bytes 1769480 | tf_op jit(solution)/shard_map/ppermute | solution.py:801
  8.0 18.5 %interior.1 = (f32[9,4,128,128]{3,2,1,0:T(8,128)S(1)}, f32[3,14,128,128]{3,2,1,0:T(8,128)S(1)}, f32[3,8,128,128]{3,2,1,0:T(8,128)S(1)}, f32[3,4,128,128]{3,2,1,0...) custom-call(f32[1]{0:T(128)} %bitcast.is_first, ...), custom_call_target="tpu_custom_call" | custom-call | flops 4000000000 | bytes 60000000 | tf_op jit(solution)/shard_map/interior/pallas_call | solution.py:929
  26.5 3.4 %collective-permute-done.low.refs_2_ = f32[9,128,128]{2,1,0:T(8,128)S(1)} collective-permute-done((f32[9,128,128]{2,1,0:T(8,128)}, f32[9,128,128]{2,1,0:T(8,128)S(1)}, u32[]{:S(2)}, u32[]{:S(2)}) %collective-permute-start) | collective-permute-done | bytes 589856 | tf_op jit(solution)/shard_map/ppermute | solution.py:801
  29.9 1.8 %collective-permute-done.1.high.refs_4_ = f32[9,128,128]{2,1,0:T(8,128)S(1)} collective-permute-done((f32[9,128,128]{2,1,0:T(8,128)}, f32[9,128,128]{2,1,0:T(8,128)S(1)}, u32[]{:S(2)}, u32[]{:S(2)}) %collective-permute-start.1) | collective-permute-done | bytes 589856 | tf_op jit(solution)/shard_map/ppermute | solution.py:801
  31.7 1.3 end_one.1
  33.4 3.8 %collective-permute-start.3 = (f32[3,128,128]{2,1,0:T(8,128)S(1)}, f32[3,128,128]{2,1,0:T(8,128)S(1)}, u32[]{:S(2)}, u32[]{:S(2)}) collective-permute-start(f32[3,128,128]{2,1,0:T(8,128)S(1)} %get-tuple-element.46.low_end.refs_1_), channel_id=1, source_target_pairs={{4,0},{8,4},{12,8},{16,12},{20,16},{24,20},{28,24},{0,28},{5,1},{9... | collective-permute-start | bytes 589832 | tf_op jit(solution)/shard_map/ppermute | solution.py:801
  37.2 5.4 %collective-permute-start.6 = (f32[768,128]{1,0:T(8,128)S(1)}, f32[768,128]{1,0:T(8,128)S(1)}, u32[]{:S(2)}, u32[]{:S(2)}) collective-permute-start(f32[768,128]{1,0:T(8,128)S(1)} %get-tuple-element.59), channel_id=1, source_target_pairs={{0,1},{1,2},{2,3},{4,5},{5,6},{6,7},{8,9},{9,10},{10,11},{12,13},{... | collective-permute-start | bytes 1179656 | tf_op jit(solution)/shard_map/ppermute | solution.py:806
  42.7 2.8 %collective-permute-done.3.high.refs_4_ = f32[3,128,128]{2,1,0:T(8,128)S(1)} collective-permute-done((f32[3,128,128]{2,1,0:T(8,128)S(1)}, f32[3,128,128]{2,1,0:T(8,128)S(1)}, u32[]{:S(2)}, u32[]{:S(2)}) %collective-permute-start.3) | collective-permute-done | bytes 196640 | tf_op jit(solution)/shard_map/ppermute | solution.py:801
  45.5 1.9 %end_two.1 = (f32[3,128,128]{2,1,0:T(8,128)S(1)}, f32[3,128,128]{2,1,0:T(8,128)S(1)}, f32[3,2,128,128]{3,2,1,0:T(8,128)S(1)}, f32[6,2,128,128]{3,2,1,0:T(8,128)S(1)}, f32[256,128]{1,0:T(8,128)S(1)}) custom-call(f32[3,14,128,128]{3,2,1,0:T(8,128)S(1)} %get-tuple-element.40.swept.refs_2_, f32[3,128,128]{2,1,0:T(8,128)S(1)} %collective-permute-done.2.low.refs_0_, ...), custom_call_target="tpu_custom_call" | custom-call | tf_op jit(solution)/shard_map/end_two/pallas_call | solution.py:974
  47.5 4.1 %collective-permute-start.5 = (f32[3,128,128]{2,1,0:T(8,128)S(1)}, f32[3,128,128]{2,1,0:T(8,128)S(1)}, u32[]{:S(2)}, u32[]{:S(2)}) collective-permute-start(f32[3,128,128]{2,1,0:T(8,128)S(1)} %get-tuple-element.51.low_end), channel_id=1, source_target_pairs={{4,0},{8,4},{12,8},{16,12},{20,16},{24,20},{28,24},{0,28},{5,1},{9... | collective-permute-start | bytes 589832 | tf_op jit(solution)/shard_map/ppermute | solution.py:801
  51.7 4.7 %collective-permute-start.7 = (f32[256,128]{1,0:T(8,128)S(1)}, f32[256,128]{1,0:T(8,128)S(1)}, u32[]{:S(2)}, u32[]{:S(2)}) collective-permute-start(f32[256,128]{1,0:T(8,128)S(1)} %get-tuple-element.60), channel_id=1, source_target_pairs={{0,1},{1,2},{2,3},{4,5},{5,6},{6,7},{8,9},{9,10},{10,11},{12,13},{... | collective-permute-start | bytes 393224 | tf_op jit(solution)/shard_map/ppermute | solution.py:806
  56.4 1.9 %collective-permute-start.8 = (f32[3,8,128,128]{3,2,1,0:T(8,128)S(1)}, f32[3,8,128,128]{3,2,1,0:T(8,128)}, u32[]{:S(2)}, u32[]{:S(2)}) collective-permute-start(f32[3,8,128,128]{3,2,1,0:T(8,128)S(1)} %get-tuple-element.53.swept.refs_1_), channel_id=1, source_target_pairs={{0,1},{1,2},{2,3},{4,5},{5,6},{6,7},{8,9},{9,10},{10,11},{12,13},{... | collective-permute-start | bytes 4718600 | tf_op jit(solution)/shard_map/ppermute | solution.py:806
  58.3 2.3 %middle.1 = (f32[6,2,128,128]{3,2,1,0:T(8,128)S(1)}, f32[1536,128]{1,0:T(8,128)S(1)}) custom-call(f32[3,8,128,128]{3,2,1,0:T(8,128)S(1)} %get-tuple-element.53.swept.refs_1_, f32[3,4,128,128]{3,2,1,0:T(8,128)S(1)} %get-tuple-element.39.side, f32[3,128,128]{2,1,0:T(8,128)S(1)} %get-tuple-element.51.low_end, f32[3,2,128,128]{3,2,1,0:T(8,128)S(1)} %get-tuple-element.52.nexts, ...), custom_call_target="tpu_custom_call" | custom-call | tf_op jit(solution)/shard_map/middle/pallas_call | solution.py:990
  60.7 2.8 %end_three.1 = (f32[3,10,128,128]{3,2,1,0:T(8,128)}, f32[1536,128]{1,0:T(8,128)}) custom-call(f32[3,4,128,128]{3,2,1,0:T(8,128)S(1)} %get-tuple-element.39.side, f32[3,128,128]{2,1,0:T(8,128)S(1)} %collective-permute-done.4.low, f32[3,128,128]{2,1,0:T(8,128)S(1)} %get-tuple-element.51.low_end, f32[3,2,128,128]{3,2,1,0:T(8,128)S(1)} %get-tuple-element.52.nexts, ...), custom_call_target="tpu_custom_call" | custom-call | tf_op jit(solution)/shard_map/end_three/pallas_call | solution.py:999
  63.5 4.6 %all-to-all-start = ((f32[32,48,128]{2,1,0:T(8,128)}), f32[32,48,128]{2,1,0:T(8,128)}, u32[]{:S(2)}, u32[]{:S(2)}) async-start(f32[32,48,128]{2,1,0:T(8,128)} %bitcast.2), calls=%async_computation | async-start | bytes 1572864 | tf_op jit(solution)/shard_map/all_to_all | solution.py:1076
  68.1 3.5 %collective-permute-start.9 = (f32[3,10,128,128]{3,2,1,0:T(8,128)}, f32[3,10,128,128]{3,2,1,0:T(8,128)}, u32[]{:S(2)}, u32[]{:S(2)}) collective-permute-start(f32[3,10,128,128]{3,2,1,0:T(8,128)} %get-tuple-element.64.refs_0_), channel_id=1, source_target_pairs={{0,1},{1,2},{2,3},{4,5},{5,6},{6,7},{8,9},{9,10},{10,11},{12,13},{... | collective-permute-start | bytes 5898248 | tf_op jit(solution)/shard_map/ppermute | solution.py:806
  71.7 0.7 dynamic-slice_bitcast_fusion
  72.4 0.7 add_divide_fusion.inverse
  73.1 8.9 %collective-permute-done.8.refs_1_ = f32[3,8,128,128]{3,2,1,0:T(8,128)} collective-permute-done((f32[3,8,128,128]{3,2,1,0:T(8,128)S(1)}, f32[3,8,128,128]{3,2,1,0:T(8,128)}, u32[]{:S(2)}, u32[]{:S(2)}) %collective-permute-start.8) | collective-permute-done | bytes 1572896 | tf_op jit(solution)/shard_map/ppermute | solution.py:806
  82.0 6.5 %all-to-all-done = f32[32,48,128]{2,1,0:T(8,128)} async-done(((f32[32,48,128]{2,1,0:T(8,128)}), f32[32,48,128]{2,1,0:T(8,128)}, u32[]{:S(2)}, u32[]{:S(2)}) %all-to-all-start) | async-done | bytes 786464 | tf_op jit(solution)/shard_map/all_to_all | solution.py:1076
  88.4 3.8 %solve.1 = (f32[1024,128]{1,0:T(8,128)}, f32[1024,128]{1,0:T(8,128)}) custom-call(f32[1536,128]{1,0:T(8,128)} %bitcast.3.values, f32[64,128]{1,0:T(8,128)} %add_divide_fusion.inverse, bf16[144,192]{1,0:T(8,128)(2,1)} %constant.35.clone.table), custom_call_target="tpu_custom_call" | custom-call | tf_op jit(solution)/shard_map/solve/pallas_call | solution.py:1095
  92.3 4.0 %all-to-all-start.2 = ((f32[32,32,128]{2,1,0:T(8,128)}), f32[32,32,128]{2,1,0:T(8,128)}, u32[]{:S(2)}, u32[]{:S(2)}) async-start(f32[32,32,128]{2,1,0:T(8,128)} %bitcast.19), calls=%async_computation.2 | async-start | bytes 1048576 | tf_op jit(solution)/shard_map/all_to_all | solution.py:1082
  96.3 13.8 %collective-permute-done.9.refs_0_ = f32[3,10,128,128]{3,2,1,0:T(8,128)} collective-permute-done((f32[3,10,128,128]{3,2,1,0:T(8,128)}, f32[3,10,128,128]{3,2,1,0:T(8,128)}, u32[]{:S(2)}, u32[]{:S(2)}) %collective-permute-start.9) | collective-permute-done | bytes 1966112 | tf_op jit(solution)/shard_map/ppermute | solution.py:806
  110.2 1.4 %all-to-all-done.2 = f32[32,32,128]{2,1,0:T(8,128)} async-done(((f32[32,32,128]{2,1,0:T(8,128)}), f32[32,32,128]{2,1,0:T(8,128)}, u32[]{:S(2)}, u32[]{:S(2)}) %all-to-all-start.2) | async-done | bytes 524320 | tf_op jit(solution)/shard_map/all_to_all | solution.py:1082
  111.6 3.5 %all-to-all-start.1 = ((f32[32,32,128]{2,1,0:T(8,128)}), f32[32,32,128]{2,1,0:T(8,128)}, u32[]{:S(2)}, u32[]{:S(2)}) async-start(f32[32,32,128]{2,1,0:T(8,128)} %bitcast.18), calls=%async_computation.1 | async-start | bytes 1048576 | tf_op jit(solution)/shard_map/all_to_all | solution.py:1082
  115.1 3.7 %collective-permute-start.10 = (f32[32,32,128]{2,1,0:T(8,128)}, f32[32,32,128]{2,1,0:T(8,128)}, u32[]{:S(2)}, u32[]{:S(2)}) collective-permute-start(f32[32,32,128]{2,1,0:T(8,128)} %all-to-all-done.2), channel_id=1, source_target_pairs={{0,1},{1,2},{2,3},{4,5},{5,6},{6,7},{8,9},{9,10},{10,11},{12,13},{... | collective-permute-start | bytes 1572872 | tf_op jit(solution)/shard_map/ppermute | solution.py:806
  118.8 6.1 %corrected_2.1 = (f32[3,3,16,128,128]{4,3,2,1,0:T(8,128)}, bf16[3,3,16,128,128]{4,3,2,1,0:T(8,128)(2,1)}) custom-call(f32[1]{0:T(128)} %bitcast.is_first, f32[1024,128]{1,0:T(8,128)} %bitcast.9.spectra, bf16[512,256]{1,0:T(8,128)(2,1)} %constant.36.clone.table, f32[3,10,128,128]{3,2,1,0:T(8,128)} %get-tuple-element.64.refs_0_, f32[3,8,128,128]{3,2,1,0:T(8,128)} %copy-done.1), custom_call_target="tpu_custom_call" | custom-call | tf_op jit(solution)/shard_map/corrected_2/pallas_call | solution.py:820
  125.0 2.5 %collective-permute-done.10 = f32[32,32,128]{2,1,0:T(8,128)} collective-permute-done((f32[32,32,128]{2,1,0:T(8,128)}, f32[32,32,128]{2,1,0:T(8,128)}, u32[]{:S(2)}, u32[]{:S(2)}) %collective-permute-start.10) | collective-permute-done | bytes 524320 | tf_op jit(solution)/shard_map/ppermute | solution.py:806
  127.5 6.2 %corrected_0.1 = (f32[3,3,16,128,128]{4,3,2,1,0:T(8,128)}, bf16[3,3,16,128,128]{4,3,2,1,0:T(8,128)(2,1)}) custom-call(f32[1]{0:T(128)} %bitcast.is_first, f32[1024,128]{1,0:T(8,128)} %bitcast.8.spectra, bf16[512,256]{1,0:T(8,128)(2,1)} %constant.36.clone.table, ...), custom_call_target="tpu_custom_call", output_to_operand_aliasing={{0}: (8, {}), {1}: (9, {})} | custom-call | tf_op jit(solution)/shard_map/corrected_0/pallas_call | solution.py:820
  133.7 6.1 %corrected_1.1 = (f32[3,3,16,128,128]{4,3,2,1,0:T(8,128)}, bf16[3,3,16,128,128]{4,3,2,1,0:T(8,128)(2,1)}) custom-call(f32[1]{0:T(128)} %bitcast.is_first, f32[1024,128]{1,0:T(8,128)} %bitcast.6.spectra, bf16[512,256]{1,0:T(8,128)(2,1)} %constant.36.clone.table, f32[3,128,128]{2,1,0:T(8,128)} %copy-done.7, ...), custom_call_target="tpu_custom_call", output_to_operand_aliasing={{0}: (8, {}), {1}: (9, {})} | custom-call | tf_op jit(solution)/shard_map/corrected_1/pallas_call | solution.py:820
  (30 shorter events, 0.5 us)
Async XLA Ops:
  0.6 7.4 %copy-start.4 = (bf16[768,128]{1,0:T(8,128)(2,1)S(1)}, bf16[768,128]{1,0:T(8,128)(2,1)}, u32[]{:S(2)}) copy-start(bf16[768,128]{1,0:T(8,128)(2,1)} %constant.33.clone.z_table) | copy-start | bytes 589828
  0.6 7.4 %copy-start.9 = (bf16[64,192]{1,0:T(8,128)(2,1)S(1)}, bf16[64,192]{1,0:T(8,128)(2,1)}, u32[]{:S(2)}) copy-start(bf16[64,192]{1,0:T(8,128)(2,1)} %constant.34.clone.y_table) | copy-start | bytes 73732
  2.8 27.1 %collective-permute-start = (f32[9,128,128]{2,1,0:T(8,128)}, f32[9,128,128]{2,1,0:T(8,128)S(1)}, u32[]{:S(2)}, u32[]{:S(2)}) collective-permute-start(f32[9,128,128]{2,1,0:T(8,128)} %get-tuple-element.42), channel_id=1, source_target_pairs={{0,4},{4,8},{8,12},{12,16},{16,20},{20,24},{24,28},{28,0},{1,5},{5... | collective-permute-start | bytes 1769480 | tf_op jit(solution)/shard_map/ppermute | solution.py:801
  4.9 26.7 %collective-permute-start.1 = (f32[9,128,128]{2,1,0:T(8,128)}, f32[9,128,128]{2,1,0:T(8,128)S(1)}, u32[]{:S(2)}, u32[]{:S(2)}) collective-permute-start(f32[9,128,128]{2,1,0:T(8,128)} %get-tuple-element.43), channel_id=1, source_target_pairs={{4,0},{8,4},{12,8},{16,12},{20,16},{24,20},{28,24},{0,28},{5,1},{9... | collective-permute-start | bytes 1769480 | tf_op jit(solution)/shard_map/ppermute | solution.py:801
  26.5 20.9 %copy-start = (f32[3,14,128,128]{3,2,1,0:T(8,128)}, f32[3,14,128,128]{3,2,1,0:T(8,128)S(1)}, u32[]{:S(2)}) copy-start(f32[3,14,128,128]{3,2,1,0:T(8,128)S(1)} %get-tuple-element.40.swept.refs_2_) | copy-start | bytes 8257540
  26.5 31.8 %copy-start.1 = (f32[3,8,128,128]{3,2,1,0:T(8,128)}, f32[3,8,128,128]{3,2,1,0:T(8,128)S(1)}, u32[]{:S(2)}) copy-start(f32[3,8,128,128]{3,2,1,0:T(8,128)S(1)} %get-tuple-element.53.swept.refs_1_) | copy-start | bytes 4718596
  29.9 17.5 %copy-start.2 = (f32[9,128,128]{2,1,0:T(8,128)}, f32[9,128,128]{2,1,0:T(8,128)S(1)}, u32[]{:S(2)}) copy-start(f32[9,128,128]{2,1,0:T(8,128)S(1)} %collective-permute-done.low.refs_2_) | copy-start | bytes 1769476
  31.7 15.8 %copy-start.3 = (f32[9,128,128]{2,1,0:T(8,128)}, f32[9,128,128]{2,1,0:T(8,128)S(1)}, u32[]{:S(2)}) copy-start(f32[9,128,128]{2,1,0:T(8,128)S(1)} %collective-permute-done.1.high.refs_4_) | copy-start | bytes 1769476
  33.0 23.4 %copy-start.5 = (f32[3,128,128]{2,1,0:T(8,128)}, f32[3,128,128]{2,1,0:T(8,128)S(1)}, u32[]{:S(2)}) copy-start(f32[3,128,128]{2,1,0:T(8,128)S(1)} %get-tuple-element.46.low_end.refs_1_) | copy-start | bytes 589828
  33.0 23.4 %copy-start.6 = (f32[3,128,128]{2,1,0:T(8,128)}, f32[3,128,128]{2,1,0:T(8,128)S(1)}, u32[]{:S(2)}) copy-start(f32[3,128,128]{2,1,0:T(8,128)S(1)} %get-tuple-element.45.high_end.refs_3_) | copy-start | bytes 589828
  33.0 9.6 %collective-permute-start.2 = (f32[3,128,128]{2,1,0:T(8,128)S(1)}, f32[3,128,128]{2,1,0:T(8,128)S(1)}, u32[]{:S(2)}, u32[]{:S(2)}) collective-permute-start(f32[3,128,128]{2,1,0:T(8,128)S(1)} %get-tuple-element.45.high_end.refs_3_), channel_id=1, source_target_pairs={{0,4},{4,8},{8,12},{12,16},{16,20},{20,24},{24,28},{28,0},{1,5},{5... | collective-permute-start | bytes 589832 | tf_op jit(solution)/shard_map/ppermute | solution.py:801
  33.4 12.1 %collective-permute-start.3 = (f32[3,128,128]{2,1,0:T(8,128)S(1)}, f32[3,128,128]{2,1,0:T(8,128)S(1)}, u32[]{:S(2)}, u32[]{:S(2)}) collective-permute-start(f32[3,128,128]{2,1,0:T(8,128)S(1)} %get-tuple-element.46.low_end.refs_1_), channel_id=1, source_target_pairs={{4,0},{8,4},{12,8},{16,12},{20,16},{24,20},{28,24},{0,28},{5,1},{9... | collective-permute-start | bytes 589832 | tf_op jit(solution)/shard_map/ppermute | solution.py:801
  37.2 23.5 %collective-permute-start.6 = (f32[768,128]{1,0:T(8,128)S(1)}, f32[768,128]{1,0:T(8,128)S(1)}, u32[]{:S(2)}, u32[]{:S(2)}) collective-permute-start(f32[768,128]{1,0:T(8,128)S(1)} %get-tuple-element.59), channel_id=1, source_target_pairs={{0,1},{1,2},{2,3},{4,5},{5,6},{6,7},{8,9},{9,10},{10,11},{12,13},{... | collective-permute-start | bytes 1179656 | tf_op jit(solution)/shard_map/ppermute | solution.py:806
  42.6 18.0 %copy-start.7 = (f32[3,128,128]{2,1,0:T(8,128)}, f32[3,128,128]{2,1,0:T(8,128)S(1)}, u32[]{:S(2)}) copy-start(f32[3,128,128]{2,1,0:T(8,128)S(1)} %collective-permute-done.2.low.refs_0_) | copy-start | bytes 589828
  45.5 12.8 %copy-start.8 = (f32[3,128,128]{2,1,0:T(8,128)}, f32[3,128,128]{2,1,0:T(8,128)S(1)}, u32[]{:S(2)}) copy-start(f32[3,128,128]{2,1,0:T(8,128)S(1)} %collective-permute-done.3.high.refs_4_) | copy-start | bytes 589828
  47.4 13.2 %collective-permute-start.4 = (f32[3,128,128]{2,1,0:T(8,128)S(1)}, f32[3,128,128]{2,1,0:T(8,128)S(1)}, u32[]{:S(2)}, u32[]{:S(2)}) collective-permute-start(f32[3,128,128]{2,1,0:T(8,128)S(1)} %get-tuple-element.50.high_end), channel_id=1, source_target_pairs={{0,4},{4,8},{8,12},{12,16},{16,20},{20,24},{24,28},{28,0},{1,5},{5... | collective-permute-start | bytes 589832 | tf_op jit(solution)/shard_map/ppermute | solution.py:801
  47.5 13.2 %collective-permute-start.5 = (f32[3,128,128]{2,1,0:T(8,128)S(1)}, f32[3,128,128]{2,1,0:T(8,128)S(1)}, u32[]{:S(2)}, u32[]{:S(2)}) collective-permute-start(f32[3,128,128]{2,1,0:T(8,128)S(1)} %get-tuple-element.51.low_end), channel_id=1, source_target_pairs={{4,0},{8,4},{12,8},{16,12},{20,16},{24,20},{28,24},{0,28},{5,1},{9... | collective-permute-start | bytes 589832 | tf_op jit(solution)/shard_map/ppermute | solution.py:801
  51.7 9.0 %collective-permute-start.7 = (f32[256,128]{1,0:T(8,128)S(1)}, f32[256,128]{1,0:T(8,128)S(1)}, u32[]{:S(2)}, u32[]{:S(2)}) collective-permute-start(f32[256,128]{1,0:T(8,128)S(1)} %get-tuple-element.60), channel_id=1, source_target_pairs={{0,1},{1,2},{2,3},{4,5},{5,6},{6,7},{8,9},{9,10},{10,11},{12,13},{... | collective-permute-start | bytes 393224 | tf_op jit(solution)/shard_map/ppermute | solution.py:806
  56.4 25.6 %collective-permute-start.8 = (f32[3,8,128,128]{3,2,1,0:T(8,128)S(1)}, f32[3,8,128,128]{3,2,1,0:T(8,128)}, u32[]{:S(2)}, u32[]{:S(2)}) collective-permute-start(f32[3,8,128,128]{3,2,1,0:T(8,128)S(1)} %get-tuple-element.53.swept.refs_1_), channel_id=1, source_target_pairs={{0,1},{1,2},{2,3},{4,5},{5,6},{6,7},{8,9},{9,10},{10,11},{12,13},{... | collective-permute-start | bytes 4718600 | tf_op jit(solution)/shard_map/ppermute | solution.py:806
  58.3 14.0 %copy-start.10 = (f32[64]{0:T(128)S(1)}, f32[64]{0:T(128)}, u32[]{:S(2)}) copy-start(f32[64]{0:T(128)} %constant.32.clone) | copy-start | bytes 772
  63.5 24.9 %all-to-all-start = ((f32[32,48,128]{2,1,0:T(8,128)}), f32[32,48,128]{2,1,0:T(8,128)}, u32[]{:S(2)}, u32[]{:S(2)}) async-start(f32[32,48,128]{2,1,0:T(8,128)} %bitcast.2), calls=%async_computation | async-start | bytes 1572864 | tf_op jit(solution)/shard_map/all_to_all | solution.py:1076
  68.1 42.1 %collective-permute-start.9 = (f32[3,10,128,128]{3,2,1,0:T(8,128)}, f32[3,10,128,128]{3,2,1,0:T(8,128)}, u32[]{:S(2)}, u32[]{:S(2)}) collective-permute-start(f32[3,10,128,128]{3,2,1,0:T(8,128)} %get-tuple-element.64.refs_0_), channel_id=1, source_target_pairs={{0,1},{1,2},{2,3},{4,5},{5,6},{6,7},{8,9},{9,10},{10,11},{12,13},{... | collective-permute-start | bytes 5898248 | tf_op jit(solution)/shard_map/ppermute | solution.py:806
  92.3 19.3 %all-to-all-start.2 = ((f32[32,32,128]{2,1,0:T(8,128)}), f32[32,32,128]{2,1,0:T(8,128)}, u32[]{:S(2)}, u32[]{:S(2)}) async-start(f32[32,32,128]{2,1,0:T(8,128)} %bitcast.19), calls=%async_computation.2 | async-start | bytes 1048576 | tf_op jit(solution)/shard_map/all_to_all | solution.py:1082
  111.6 22.1 %all-to-all-start.1 = ((f32[32,32,128]{2,1,0:T(8,128)}), f32[32,32,128]{2,1,0:T(8,128)}, u32[]{:S(2)}, u32[]{:S(2)}) async-start(f32[32,32,128]{2,1,0:T(8,128)} %bitcast.18), calls=%async_computation.1 | async-start | bytes 1048576 | tf_op jit(solution)/shard_map/all_to_all | solution.py:1082
  115.1 12.4 %collective-permute-start.10 = (f32[32,32,128]{2,1,0:T(8,128)}, f32[32,32,128]{2,1,0:T(8,128)}, u32[]{:S(2)}, u32[]{:S(2)}) collective-permute-start(f32[32,32,128]{2,1,0:T(8,128)} %all-to-all-done.2), channel_id=1, source_target_pairs={{0,1},{1,2},{2,3},{4,5},{5,6},{6,7},{8,9},{9,10},{10,11},{12,13},{... | collective-permute-start | bytes 1572872 | tf_op jit(solution)/shard_map/ppermute | solution.py:806
